TPU v7x, 32 devices: a whole 2x2x4 slice. The times are simulated.
32 devices in a mesh: dp: 16 (over z, y, core), tensor: 2 (over x).
Axes of the slice: x: 2, y: 2, z: 4, core: 2. Of those that a mesh axis runs over, the one named last changes fastest.
Arguments:
- latent: bfloat16 [64, 1024, 1152], P('dp', 'tensor'), may hold values from -6 to 6
- condition: bfloat16 [64, 1152], P('dp'), may hold values from -6 to 6
- cotangent: bfloat16 [64, 1024, 1152], P('dp', 'tensor'), may hold values from -6 to 6
- mod_weight: bfloat16 [1152, 6, 1152], P('dp', None, 'tensor'), may hold values from -0.1875 to 0.1875
- mod_bias: bfloat16 [6, 1152], P(None, 'tensor'), may hold values from -3 to 3
- head_weight: bfloat16 [1152, 3, 1152], P('dp', None, 'tensor'), may hold values from -0.1875 to 0.1875
- head_bias: bfloat16 [2, 1152], P(None, 'tensor'), may hold values from -3 to 3
- mix_weight: bfloat16 [1152, 1152], P('tensor', 'dp'), may hold values from -1 to 1
- branch_bias: bfloat16 [2, 1152], P(None, 'tensor'), may hold values from -3 to 3
- up_weight: bfloat16 [1152, 4608], P('dp', 'tensor'), may hold values from -0.1875 to 0.1875
- up_bias: bfloat16 [4608], P('tensor'), may hold values from -3 to 3
- down_weight: bfloat16 [4608, 1152], P('tensor', 'dp'), may hold values from -0.09375 to 0.09375
Outputs:
- block_out: bfloat16 [64, 1024, 1152], P('dp', 'tensor')
- latent_grad: bfloat16 [64, 1024, 1152], P('dp', 'tensor')
- condition_grad: float32 [64, 1152], P('dp')
- mod_weight_grad: float32 [1152, 6, 1152], P('dp', None, 'tensor')
- mod_bias_grad: float32 [6, 1152], P(None, 'tensor')
- head_weight_grad: float32 [1152, 3, 1152], P('dp', None, 'tensor')
- head_bias_grad: float32 [2, 1152], P(None, 'tensor')
- mix_weight_grad: float32 [1152, 1152], P('tensor', 'dp')
- branch_bias_grad: float32 [2, 1152], P(None, 'tensor')
- up_weight_grad: float32 [1152, 4608], P('dp', 'tensor')
- up_bias_grad: float32 [4608], P('tensor')
- down_weight_grad: float32 [4608, 1152], P('tensor', 'dp')
All inputs are finite; a program needn't handle non-finite values.
Results may differ from a plain program's by a relative error of at most 0.022.
The roundings to bfloat16 on the way count: a program that leaves them out, or rounds other values in their place, can miss the bound.
Values may be sent and summed in bfloat16 or wider, within the bound.
A program may use at most 448 MiB of HBM per device.

v0:
```python
from functools import partial

import jax
import jax.numpy as jnp
from jax import lax
from jax.sharding import PartitionSpec as P

SEQ = 1024
HEAD_DIM = 72
MICRO = 4


EPSILON = 1e-06


def layer_norm(values):
    centred = values - jnp.mean(values, axis=-1, keepdims=True)
    variance = jnp.mean(centred * centred, axis=-1, keepdims=True)
    return centred * lax.rsqrt(variance + EPSILON)


def modulate(values, shift, scale):
    return layer_norm(values) * (1.0 + scale[:, None, :]) + shift[:, None, :]


def gelu_tanh(values):
    return jax.nn.gelu(values, approximate=True)


def fetch_weights(mod_weight, head_weight, mix_weight, up_weight, down_weight):
    return (
        lax.all_gather(mod_weight, "dp", axis=0, tiled=True),
        lax.all_gather(head_weight, "dp", axis=0, tiled=True),
        lax.all_gather(mix_weight, "dp", axis=1, tiled=True),
        lax.all_gather(up_weight, "dp", axis=0, tiled=True),
        lax.all_gather(down_weight, "dp", axis=1, tiled=True),
    )


def reduce_weights(grads):
    return (
        lax.psum_scatter(
            grads[0].astype(jnp.bfloat16), "dp", scatter_dimension=0, tiled=True
        ).astype(jnp.float32),
        lax.psum_scatter(
            grads[1].astype(jnp.bfloat16), "dp", scatter_dimension=0, tiled=True
        ).astype(jnp.float32),
        lax.psum_scatter(
            grads[2].astype(jnp.bfloat16), "dp", scatter_dimension=1, tiled=True
        ).astype(jnp.float32),
        lax.psum_scatter(
            grads[3].astype(jnp.bfloat16), "dp", scatter_dimension=0, tiled=True
        ).astype(jnp.float32),
        lax.psum_scatter(
            grads[4].astype(jnp.bfloat16), "dp", scatter_dimension=1, tiled=True
        ).astype(jnp.float32),
    )


def attend_forward(queries, keys, values, block_rows, scale_factor):
    seq_len = queries.shape[0]
    blocked = queries.reshape(seq_len // block_rows, block_rows, queries.shape[1], queries.shape[2])

    def one_block(query_block):
        scores = (
            jnp.einsum("qhd,khd->hqk", query_block, keys, preferred_element_type=jnp.float32)
            * scale_factor
        )
        peak = jnp.max(scores, axis=-1, keepdims=True)
        raised = jnp.exp(scores - peak)
        total = jnp.sum(raised, axis=-1, keepdims=True)
        weights = (raised / total).astype(jnp.bfloat16)
        mixed = jnp.einsum("hqk,khd->qhd", weights, values, preferred_element_type=jnp.float32)
        return (mixed, (peak + jnp.log(total))[..., 0])

    mixed, logsum = lax.map(one_block, blocked)
    return (mixed.reshape(queries.shape), logsum)


def attend_backward(queries, keys, values, grad_mixed, logsum, block_rows, scale_factor):
    seq_len = queries.shape[0]
    block_shape = (seq_len // block_rows, block_rows, queries.shape[1], queries.shape[2])

    def one_block(carried, pieces):
        key_sum, value_sum = carried
        query_block, grad_block, logsum_block = pieces
        scores = (
            jnp.einsum("qhd,khd->hqk", query_block, keys, preferred_element_type=jnp.float32)
            * scale_factor
        )
        probs = jnp.exp(scores - logsum_block[..., None])
        prob_grad = jnp.einsum(
            "qhd,khd->hqk", grad_block, values, preferred_element_type=jnp.float32
        )
        inner = jnp.sum(probs * prob_grad, axis=-1, keepdims=True)
        score_grad = (probs * (prob_grad - inner)).astype(jnp.bfloat16)
        query_grad = (
            jnp.einsum("hqk,khd->qhd", score_grad, keys, preferred_element_type=jnp.float32)
            * scale_factor
        )
        key_sum = (
            key_sum
            + jnp.einsum(
                "hqk,qhd->khd", score_grad, query_block, preferred_element_type=jnp.float32
            )
            * scale_factor
        )
        value_sum = value_sum + jnp.einsum(
            "hqk,qhd->khd",
            probs.astype(jnp.bfloat16),
            grad_block,
            preferred_element_type=jnp.float32,
        )
        return ((key_sum, value_sum), query_grad)

    empty = jnp.zeros(keys.shape, jnp.float32)
    (key_grad, value_grad), query_grads = lax.scan(
        one_block,
        (empty, empty),
        (queries.reshape(block_shape), grad_mixed.reshape(block_shape), logsum),
    )
    return (query_grads.reshape(queries.shape), key_grad, value_grad)


def body(
    latent,
    condition,
    cotangent,
    mod_weight,
    mod_bias,
    head_weight,
    head_bias,
    mix_weight,
    branch_bias,
    up_weight,
    up_bias,
    down_weight,
):
    per_group = latent.shape[0] // MICRO
    seq_len = SEQ
    head_cols = head_weight.shape[2]
    local_heads = head_cols // HEAD_DIM
    block_rows = min(512, seq_len)
    scale_factor = HEAD_DIM ** (-0.5)
    attend_fwd = jax.vmap(partial(attend_forward, block_rows=block_rows, scale_factor=scale_factor))
    attend_bwd = jax.vmap(
        partial(attend_backward, block_rows=block_rows, scale_factor=scale_factor)
    )
    head_bias_f = head_bias.astype(jnp.float32)
    up_bias_f = up_bias.astype(jnp.float32)
    mod_bias_f = mod_bias.astype(jnp.float32)
    branch_bias_f = branch_bias.astype(jnp.float32)
    bias_totals = (
        jnp.zeros(mod_bias.shape, jnp.float32),
        jnp.zeros(head_bias.shape, jnp.float32),
        jnp.zeros(up_bias.shape, jnp.float32),
        jnp.zeros(branch_bias.shape, jnp.float32),
    )
    grad_sums = None
    block_outs = []
    latent_grads = []
    condition_grads = []
    for micro_step in range(MICRO):
        row_start = micro_step * per_group
        row_stop = row_start + per_group
        mod_full, head_full, mix_full, up_full, down_full = fetch_weights(
            mod_weight, head_weight, mix_weight, up_weight, down_weight
        )
        lat_part = latent[row_start:row_stop].astype(jnp.float32)
        cond_part = condition[row_start:row_stop].astype(jnp.float32)
        cond_act, silu_back = jax.vjp(jax.nn.silu, cond_part)
        cond_low = cond_act.astype(jnp.bfloat16)
        mod_cols = (
            jnp.einsum("bd,dkc->bkc", cond_low, mod_full, preferred_element_type=jnp.float32)
            + mod_bias_f
        )
        mod_all, bias_all = (
            lax.all_gather(mod_cols, "tensor", axis=2, tiled=True),
            lax.all_gather(branch_bias_f, "tensor", axis=1, tiled=True),
        )
        norm_first, first_back = jax.vjp(modulate, lat_part, mod_all[:, 0], mod_all[:, 1])
        attn_rows = lax.all_gather(norm_first.astype(jnp.bfloat16), "tensor", axis=1, tiled=True)
        projected = jnp.einsum(
            "bsd,dkc->bskc", attn_rows, head_full, preferred_element_type=jnp.float32
        )
        head_shape = (per_group, seq_len, local_heads, HEAD_DIM)
        query_heads = (projected[:, :, 0] + head_bias_f[0]).astype(jnp.bfloat16).reshape(head_shape)
        key_heads = projected[:, :, 1].astype(jnp.bfloat16).reshape(head_shape)
        value_heads = (projected[:, :, 2] + head_bias_f[1]).astype(jnp.bfloat16).reshape(head_shape)
        mixed, logsum = attend_fwd(query_heads, key_heads, value_heads)
        mixed_low = mixed.reshape(per_group, seq_len, head_cols).astype(jnp.bfloat16)
        attn_part = jnp.einsum(
            "bsc,cd->bsd", mixed_low, mix_full, preferred_element_type=jnp.float32
        )
        attn_local = lax.psum_scatter(
            attn_part.astype(jnp.bfloat16), "tensor", scatter_dimension=1, tiled=True
        ).astype(jnp.float32)
        gate_attn = mod_all[:, 2][:, None, :]
        gate_mlp = mod_all[:, 5][:, None, :]
        first = lat_part + gate_attn * (attn_local + bias_all[0])
        norm_second, second_back = jax.vjp(modulate, first, mod_all[:, 3], mod_all[:, 4])
        mlp_rows = lax.all_gather(norm_second.astype(jnp.bfloat16), "tensor", axis=1, tiled=True)
        pre_act = (
            jnp.einsum("bsd,df->bsf", mlp_rows, up_full, preferred_element_type=jnp.float32)
            + up_bias_f
        )
        act_value, gelu_back = jax.vjp(gelu_tanh, pre_act)
        act_low = act_value.astype(jnp.bfloat16)
        mlp_part = jnp.einsum("bsf,fd->bsd", act_low, down_full, preferred_element_type=jnp.float32)
        mlp_local = lax.psum_scatter(
            mlp_part.astype(jnp.bfloat16), "tensor", scatter_dimension=1, tiled=True
        ).astype(jnp.float32)
        block_outs.append((first + gate_mlp * (mlp_local + bias_all[1])).astype(jnp.bfloat16))
        mod_full, head_full, mix_full, up_full, down_full = fetch_weights(
            mod_weight, head_weight, mix_weight, up_weight, down_weight
        )
        upstream = cotangent[row_start:row_stop].astype(jnp.float32)
        gate_m_grad = jnp.sum(upstream * (mlp_local + bias_all[1]), axis=1)
        tail_bias_grad = jnp.sum(gate_mlp * upstream, axis=(0, 1))
        mlp_grad = lax.all_gather(
            (gate_mlp * upstream).astype(jnp.bfloat16), "tensor", axis=1, tiled=True
        )
        down_grad = jnp.einsum("bsf,bsd->fd", act_low, mlp_grad, preferred_element_type=jnp.float32)
        act_grad = jnp.einsum(
            "bsd,fd->bsf", mlp_grad, down_full, preferred_element_type=jnp.float32
        )
        pre_grad = gelu_back(act_grad)[0].astype(jnp.bfloat16)
        up_bias_term = jnp.sum(pre_grad, axis=(0, 1), dtype=jnp.float32)
        up_grad = jnp.einsum("bsd,bsf->df", mlp_rows, pre_grad, preferred_element_type=jnp.float32)
        mlp_in_part = jnp.einsum(
            "bsf,df->bsd", pre_grad, up_full, preferred_element_type=jnp.float32
        )
        mlp_in_grad = lax.psum_scatter(
            mlp_in_part.astype(jnp.bfloat16), "tensor", scatter_dimension=1, tiled=True
        ).astype(jnp.float32)
        first_grad, shift_m_grad, scale_m_grad = second_back(mlp_in_grad)
        first_grad = first_grad + upstream
        gate_a_grad = jnp.sum(first_grad * (attn_local + bias_all[0]), axis=1)
        attn_bias_grad = jnp.sum(gate_attn * first_grad, axis=(0, 1))
        attn_branch_grad = (gate_attn * first_grad).astype(jnp.bfloat16)
        attn_grad = lax.all_gather(attn_branch_grad, "tensor", axis=1, tiled=True)
        mix_grad = jnp.einsum(
            "bsc,bsd->cd", mixed_low, attn_grad, preferred_element_type=jnp.float32
        )
        mixed_grad = jnp.einsum(
            "bsd,cd->bsc", attn_grad, mix_full, preferred_element_type=jnp.float32
        ).astype(jnp.bfloat16)
        query_grad, key_grad, value_grad = attend_bwd(
            query_heads, key_heads, value_heads, mixed_grad.reshape(head_shape), logsum
        )
        head_grads = (
            jnp.stack([query_grad, key_grad, value_grad], axis=2)
            .reshape(per_group, seq_len, 3, head_cols)
            .astype(jnp.bfloat16)
        )
        head_bias_term = jnp.sum(head_grads[:, :, 0::2], axis=(0, 1), dtype=jnp.float32)
        head_grad = jnp.einsum(
            "bsd,bskc->dkc", attn_rows, head_grads, preferred_element_type=jnp.float32
        )
        attn_in_part = jnp.einsum(
            "bskc,dkc->bsd", head_grads, head_full, preferred_element_type=jnp.float32
        )
        attn_in_grad = lax.psum_scatter(
            attn_in_part.astype(jnp.bfloat16), "tensor", scatter_dimension=1, tiled=True
        ).astype(jnp.float32)
        lat_grad, shift_a_grad, scale_a_grad = first_back(attn_in_grad)
        latent_grads.append((lat_grad + first_grad).astype(jnp.bfloat16))
        mod_terms = jnp.stack(
            [shift_a_grad, scale_a_grad, gate_a_grad, shift_m_grad, scale_m_grad, gate_m_grad],
            axis=1,
        )
        branch_terms = jnp.stack([attn_bias_grad, tail_bias_grad], axis=0)
        mod_grad_cols, branch_grad_cols = (
            lax.psum_scatter(
                mod_terms.astype(jnp.bfloat16), "tensor", scatter_dimension=2, tiled=True
            ).astype(jnp.float32),
            lax.psum_scatter(
                branch_terms.astype(jnp.bfloat16), "tensor", scatter_dimension=1, tiled=True
            ).astype(jnp.float32),
        )
        mod_grad_low = mod_grad_cols.astype(jnp.bfloat16)
        mod_grad = jnp.einsum(
            "bd,bkc->dkc", cond_low, mod_grad_low, preferred_element_type=jnp.float32
        )
        mod_bias_term = jnp.sum(mod_grad_low, axis=0, dtype=jnp.float32)
        cond_part_grad = jnp.einsum(
            "bkc,dkc->bd", mod_grad_low, mod_full, preferred_element_type=jnp.float32
        )
        cond_act_grad = lax.psum(cond_part_grad, "tensor")
        condition_grads.append(silu_back(cond_act_grad)[0])
        bias_totals = (
            bias_totals[0] + mod_bias_term,
            bias_totals[1] + head_bias_term,
            bias_totals[2] + up_bias_term,
            bias_totals[3] + branch_grad_cols,
        )
        weight_terms = (mod_grad, head_grad, mix_grad, up_grad, down_grad)
        grad_sums = (
            weight_terms if grad_sums is None else jax.tree.map(jnp.add, grad_sums, weight_terms)
        )
    grad_sums = reduce_weights(grad_sums)
    bias_sums = lax.psum((bias_totals[0], bias_totals[1], bias_totals[2], bias_totals[3]), "dp")
    return (
        jnp.concatenate(block_outs, axis=0),
        jnp.concatenate(latent_grads, axis=0),
        jnp.concatenate(condition_grads, axis=0),
        grad_sums[0],
        bias_sums[0],
        grad_sums[1],
        bias_sums[1],
        grad_sums[2],
        bias_sums[3],
        grad_sums[3],
        bias_sums[2],
        grad_sums[4],
    )


def solution(mesh):
    placed = (
        P("dp", "tensor", None),
        P("dp", None),
        P("dp", "tensor", None),
        P("dp", None, "tensor"),
        P(None, "tensor"),
        P("dp", None, "tensor"),
        P(None, "tensor"),
        P("tensor", "dp"),
        P(None, "tensor"),
        P("dp", "tensor"),
        P("tensor"),
        P("tensor", "dp"),
    )
    return jax.shard_map(
        body,
        mesh=mesh,
        in_specs=placed,
        out_specs=(
            P("dp", "tensor", None),
            P("dp", "tensor", None),
            P("dp", None),
            P("dp", None, "tensor"),
            P(None, "tensor"),
            P("dp", None, "tensor"),
            P(None, "tensor"),
            P("tensor", "dp"),
            P(None, "tensor"),
            P("dp", "tensor"),
            P("tensor"),
            P("tensor", "dp"),
        ),
        check_vma=False,
    )
```

profile of v0, /device:TPU:0, one launch (start us, length us, event | category | flops | bytes accessed | tf_op | source)
XLA Modules:
  0.0 2422.2 jit_solution(9312913352332255024)
XLA Ops:
  13.2 77.5 %all-gather.31.cloned.1.call-done = bf16[1152,6,576]{2,0,1:T(8,128)(2,1)} async-done(((bf16[72,6,576]{2,0,1:T(8,128)(2,1)}), bf16[1152,6,576]{2,0,1:T(8,128)(2,1)}) %all-gather.31.cloned.1.call-update) | async-done | bytes 7962640 | tf_op jit(solution)/shard_map/all_gather | solution.py:32
  110.8 32.1 %all-gather.35.cloned.1.call-done = bf16[1152,3,576]{2,0,1:T(8,128)(2,1)} async-done(((bf16[72,3,576]{2,0,1:T(8,128)(2,1)}), bf16[1152,3,576]{2,0,1:T(8,128)(2,1)}) %all-gather.35.cloned.1.call-update) | async-done | bytes 3981328 | tf_op jit(solution)/shard_map/all_gather | solution.py:33
  142.9 36.7 %all-gather.33.cloned.1.call-done = bf16[1,1024,1152]{2,1,0:T(8,128)(2,1)} async-done(((bf16[1,512,1152]{2,1,0:T(8,128)(2,1)}), bf16[1,1024,1152]{2,1,0:T(8,128)(2,1)}) %all-gather.33.cloned.1.call-update) | async-done | bytes 2359312 | tf_op jit(solution)/shard_map/all_gather | solution.py:182
  197.4 23.3 while.108
  242.1 23.8 reduce-scatter.50.cloned.1.call-done
  269.8 15.0 multiply_reduce_fusion.15
  309.3 14.6 all-gather.49.cloned.1.call-done
  334.1 28.2 %all-gather.45.cloned.1.call-done = bf16[1,1024,1152]{2,1,0:T(8,128)(2,1)} async-done(((bf16[1,512,1152]{2,1,0:T(8,128)(2,1)}), bf16[1,1024,1152]{2,1,0:T(8,128)(2,1)}) %all-gather.45.cloned.1.call-update) | async-done | bytes 2359312 | tf_op jit(solution)/shard_map/all_gather | solution.py:182
  375.9 24.7 %all-gather.53.cloned.1.call-done = bf16[1,1024,1152]{2,1,0:T(8,128)(2,1)} async-done(((bf16[1,512,1152]{2,1,0:T(8,128)(2,1)}), bf16[1,1024,1152]{2,1,0:T(8,128)(2,1)}) %all-gather.53.cloned.1.call-update) | async-done | bytes 2359312 | tf_op jit(solution)/shard_map/all_gather | solution.py:182
  433.2 25.7 %while.110 = (s32[]{:T(128)}, bf16[2,1,512,8,72]{2,4,3,1,0:T(8,128)(2,1)S(1)}, f32[2,1,8,512]{3,2,1,0:T(8,128)}, bf16[2,1,512,8,72]{2,4,3,1,0:T(8,128)(2,1)}, bf...) while((s32[]{:T(128)}, bf16[2,1,512,8,72]{2,4,3,1,0:T(8,128)(2,1)S(1)}, ...), condition=%wide.region_25.26_spmd, body=%wide.region_22.25_spmd.sunk | while | flops 1245704192 | bytes 54592592 | solution.py:76
  472.3 23.3 while.109
  506.1 23.5 while.111
  537.3 12.1 fusion.324
  554.3 36.2 %all-gather.57.cloned.1.call-done = bf16[1,1024,1152]{2,1,0:T(8,128)(2,1)} async-done(((bf16[1,512,1152]{2,1,0:T(8,128)(2,1)}), bf16[1,1024,1152]{2,1,0:T(8,128)(2,1)}) %all-gather.57.cloned.1.call-update) | async-done | bytes 2359312 | tf_op jit(solution)/shard_map/all_gather | solution.py:220
  590.5 15.3 convert_reduce_fusion.3
  618.2 13.7 fusion.206
  632.0 32.4 %reduce-scatter.54.cloned.1.call-done = bf16[1,512,1152]{2,1,0:T(8,128)(2,1)} async-done(((bf16[1,1024,1152]{2,1,0:T(8,128)(2,1)}), bf16[1,512,1152]{2,1,0:T(8,128)(2,1)}) %reduce-scatter.54.cloned.1.call-update) | async-done | bytes 1179664 | tf_op jit(solution)/shard_map/reduce_scatter | solution.py:195
  664.4 37.5 %reduce-scatter.62.cloned.1.call-done = bf16[1,512,1152]{2,1,0:T(8,128)(2,1)} async-done(((bf16[1,1024,1152]{2,1,0:T(8,128)(2,1)}), bf16[1,512,1152]{2,1,0:T(8,128)(2,1)}) %reduce-scatter.62.cloned.1.call-update) | async-done | bytes 1179664 | tf_op jit(solution)/shard_map/reduce_scatter | solution.py:195
  701.9 36.8 %reduce-scatter.66.cloned.1.call-done = bf16[1,512,1152]{2,1,0:T(8,128)(2,1)} async-done(((bf16[1,1024,1152]{2,1,0:T(8,128)(2,1)}), bf16[1,512,1152]{2,1,0:T(8,128)(2,1)}) %reduce-scatter.66.cloned.1.call-update) | async-done | bytes 1179664 | tf_op jit(solution)/shard_map/reduce_scatter | solution.py:233
  753.2 22.5 reduce-scatter.52.cloned.1.call-done
  781.3 31.9 %all-gather.51.cloned.1.call-done = bf16[1,1024,1152]{2,1,0:T(8,128)(2,1)} async-done(((bf16[1,512,1152]{2,1,0:T(8,128)(2,1)}), bf16[1,1024,1152]{2,1,0:T(8,128)(2,1)}) %all-gather.51.cloned.1.call-update) | async-done | bytes 2359312 | tf_op jit(solution)/shard_map/all_gather | solution.py:202
  813.2 11.7 fusion.311
  824.9 26.5 %all-gather.65.cloned.1.call-done = bf16[1,1024,1152]{2,1,0:T(8,128)(2,1)} async-done(((bf16[1,512,1152]{2,1,0:T(8,128)(2,1)}), bf16[1,1024,1152]{2,1,0:T(8,128)(2,1)}) %all-gather.65.cloned.1.call-update) | async-done | bytes 2359312 | tf_op jit(solution)/shard_map/all_gather | solution.py:220
  851.4 15.4 convert_reduce_fusion.1
  881.4 32.4 %reduce-scatter.74.cloned.1.call-done = bf16[1,512,1152]{2,1,0:T(8,128)(2,1)} async-done(((bf16[1,1024,1152]{2,1,0:T(8,128)(2,1)}), bf16[1,512,1152]{2,1,0:T(8,128)(2,1)}) %reduce-scatter.74.cloned.1.call-update) | async-done | bytes 1179664 | tf_op jit(solution)/shard_map/reduce_scatter | solution.py:233
  930.2 13.4 fusion.208
  944.2 21.4 all-gather.47.cloned.1.call-done
  978.8 12.0 fusion.207
  991.1 12.9 all-gather.55.cloned.1.call-done
  1017.1 12.0 fusion.209
  1029.2 11.9 reduce-scatter.60.cloned.1.call-done
  1041.0 36.8 %reduce-scatter.56.cloned.1.call-done = bf16[1,512,1152]{2,1,0:T(8,128)(2,1)} async-done(((bf16[1,1024,1152]{2,1,0:T(8,128)(2,1)}), bf16[1,512,1152]{2,1,0:T(8,128)(2,1)}) %reduce-scatter.56.cloned.1.call-update) | async-done | bytes 1179664 | tf_op jit(solution)/shard_map/reduce_scatter | solution.py:210
  1077.9 37.7 %reduce-scatter.64.cloned.1.call-done = bf16[1,512,1152]{2,1,0:T(8,128)(2,1)} async-done(((bf16[1,1024,1152]{2,1,0:T(8,128)(2,1)}), bf16[1,512,1152]{2,1,0:T(8,128)(2,1)}) %reduce-scatter.64.cloned.1.call-update) | async-done | bytes 1179664 | tf_op jit(solution)/shard_map/reduce_scatter | solution.py:210
  1122.6 35.4 %all-gather.61.cloned.1.call-done = bf16[1,1024,1152]{2,1,0:T(8,128)(2,1)} async-done(((bf16[1,512,1152]{2,1,0:T(8,128)(2,1)}), bf16[1,1024,1152]{2,1,0:T(8,128)(2,1)}) %all-gather.61.cloned.1.call-update) | async-done | bytes 2359312 | tf_op jit(solution)/shard_map/all_gather | solution.py:220
  1157.9 15.3 convert_reduce_fusion.2
  1195.4 15.4 convert_reduce_fusion
  1238.6 30.9 %reduce-scatter.78.cloned.1.call-done = bf16[1,512,1152]{2,1,0:T(8,128)(2,1)} async-done(((bf16[1,1024,1152]{2,1,0:T(8,128)(2,1)}), bf16[1,512,1152]{2,1,0:T(8,128)(2,1)}) %reduce-scatter.78.cloned.1.call-update) | async-done | bytes 1179664 | tf_op jit(solution)/shard_map/reduce_scatter | solution.py:233
  1282.3 24.7 %all-gather.59.cloned.1.call-done = bf16[1,1024,1152]{2,1,0:T(8,128)(2,1)} async-done(((bf16[1,512,1152]{2,1,0:T(8,128)(2,1)}), bf16[1,1024,1152]{2,1,0:T(8,128)(2,1)}) %all-gather.59.cloned.1.call-update) | async-done | bytes 2359312 | tf_op jit(solution)/shard_map/all_gather | solution.py:241
  1313.0 31.6 %all-gather.63.cloned.1.call-done = bf16[1,1024,1152]{2,1,0:T(8,128)(2,1)} async-done(((bf16[1,512,1152]{2,1,0:T(8,128)(2,1)}), bf16[1,1024,1152]{2,1,0:T(8,128)(2,1)}) %all-gather.63.cloned.1.call-update) | async-done | bytes 2359312 | tf_op jit(solution)/shard_map/all_gather | solution.py:241
  1351.9 91.7 %while.113 = (s32[]{:T(128)}, f32[1,1024,8,72]{1,3,2,0:T(8,128)}, f32[1,1024,8,72]{1,3,2,0:T(8,128)}, bf16[2,1,512,8,72]{2,4,3,1,0:T(8,128)(2,1)}, bf16[2,1,512,...) while((s32[]{:T(128)}, f32[1,1024,8,72]{1,3,2,0:T(8,128)}, ...), condition=%wide.region_54.55_spmd.clone, body=%wide.region_52.54_spmd.clone.sunk | while | flops 3073470464 | bytes 269338976 | solution.py:117
  1356.7 10.8 multiply_reduce_fusion.33
  1401.5 10.8 multiply_reduce_fusion.33
  1462.1 92.1 %while.112 = (s32[]{:T(128)}, f32[1,1024,8,72]{1,3,2,0:T(8,128)}, f32[1,1024,8,72]{1,3,2,0:T(8,128)}, bf16[2,1,512,8,72]{2,4,3,1,0:T(8,128)(2,1)}, bf16[2,1,512,...) while((s32[]{:T(128)}, f32[1,1024,8,72]{1,3,2,0:T(8,128)}, ...), condition=%wide.region_45.46_spmd.clone, body=%wide.region_43.45_spmd.clone.sunk | while | flops 3073470464 | bytes 269338976 | solution.py:117
  1466.7 11.0 multiply_reduce_fusion.32
  1512.1 10.8 multiply_reduce_fusion.32
  1578.5 91.7 %while.114 = (s32[]{:T(128)}, f32[1,1024,8,72]{1,3,2,0:T(8,128)}, f32[1,1024,8,72]{1,3,2,0:T(8,128)}, bf16[2,1,512,8,72]{2,4,3,1,0:T(8,128)(2,1)}, bf16[2,1,512,...) while((s32[]{:T(128)}, f32[1,1024,8,72]{1,3,2,0:T(8,128)}, ...), condition=%wide.region_63.64_spmd.clone, body=%wide.region_61.63_spmd.clone.sunk | while | flops 3073470464 | bytes 269338976 | solution.py:117
  1583.1 10.9 multiply_reduce_fusion.34
  1628.1 10.8 multiply_reduce_fusion.34
  1691.8 12.1 fusion.299
  1707.5 15.0 reduce-scatter.76.cloned.1.call-done
  1740.1 11.5 fusion.322
  1760.7 14.3 convolution_add_fusion.2
  1775.0 13.4 convolution_add_fusion.1
  1790.4 13.3 fusion.153
  1850.8 93.7 %while.115 = (s32[]{:T(128)}, f32[1,1024,8,72]{1,3,2,0:T(8,128)}, f32[1,1024,8,72]{1,3,2,0:T(8,128)}, bf16[2,1,512,8,72]{2,4,3,1,0:T(8,128)(2,1)}, bf16[2,1,512,...) while((s32[]{:T(128)}, f32[1,1024,8,72]{1,3,2,0:T(8,128)}, ...), condition=%wide.region_72.73_spmd.clone, body=%wide.region_70.72_spmd.clone.sunk | while | flops 3073470464 | bytes 269338976 | solution.py:117
  1855.4 10.9 multiply_reduce_fusion.35
  1866.3 10.7 multiply_convert_fusion.27
  1900.8 10.9 multiply_reduce_fusion.35
  1911.7 10.9 multiply_convert_fusion.27
  2060.1 18.2 add_convert_fusion.1
  2078.3 18.5 copy.124
  2096.8 12.3 reshape.2466
  2184.4 59.8 %all-reduce.2 = (f32[6,576]{1,0:T(8,128)}, f32[2,576]{1,0:T(2,128)}, f32[2,576]{1,0:T(2,128)}, f32[2304]{0:T(1024)}) all-reduce(f32[6,576]{1,0:T(8,128)S(1)} %add_bitcast_fusion, f32[2,576]{1,0:T(2,128)S(1)} %copy-done.210, f32[2,576]{1,0:T(2,128)S(1)} %copy-done.209, ...), channel_id=1, replica_groups=mesh['dp'=16,'tensor'=2] {'dp'}, use_global_device_ids=true, to_apply=%region_109.110 | all-reduce | flops 8064 | bytes 64512 | tf_op jit(solution)/shard_map/psum | solution.py:302
  2246.9 166.2 %all-reduce.6.cloned.1.call-done = bf16[1152,6,576]{2,0,1:T(8,128)(2,1)} async-done(((bf16[1152,6,576]{2,0,1:T(8,128)(2,1)}), bf16[1152,6,576]{2,0,1:T(8,128)(2,1)}) %all-reduce.6.cloned.1.call-update) | async-done | bytes 7962640
  (1219 shorter events, 1050.7 us)
Async XLA Ops:
  7.2 83.5 %all-gather.31.cloned.1.call-start = ((), (), s32[]{:S(2)}) async-start(), calls=%async_computation.28 | async-start | bytes 9400320 | tf_op jit(solution)/shard_map/all_gather | solution.py:32
  7.9 135.0 %all-gather.35.cloned.1.call-start = ((), (), s32[]{:S(2)}) async-start(), calls=%async_computation.30 | async-start | bytes 4700160 | tf_op jit(solution)/shard_map/all_gather | solution.py:33
  8.7 171.0 %all-gather.33.cloned.1.call-start = ((), (), s32[]{:S(2)}) async-start(), calls=%async_computation.29 | async-start | bytes 3538944 | tf_op jit(solution)/shard_map/all_gather | solution.py:182
  10.2 96.2 %copy-start.164 = (f32[512]{0:T(512)}, f32[512]{0:T(512)S(1)}, u32[]{:S(2)}) copy-start(f32[512]{0:T(512)S(1)} %broadcast_multiply_fusion.7) | copy-start | bytes 6148
  12.5 93.9 %copy-start.190 = (f32[512]{0:T(512)}, f32[512]{0:T(512)S(1)}, u32[]{:S(2)}) copy-start(f32[512]{0:T(512)S(1)} %fusion.385) | copy-start | bytes 6148
  13.2 84.8 %copy-start.180 = (f32[1,1152]{1,0:T(1,128)}, f32[1,1152]{1,0:T(1,128)S(1)}, u32[]{:S(2)}) copy-start(f32[1,1152]{1,0:T(1,128)S(1)} %get-tuple-element.806) | copy-start | bytes 13828
  13.2 86.0 %copy-start.182 = (f32[1,1152]{1,0:T(1,128)}, f32[1,1152]{1,0:T(1,128)S(1)}, u32[]{:S(2)}) copy-start(f32[1,1152]{1,0:T(1,128)S(1)} %get-tuple-element.807) | copy-start | bytes 13828
  109.8 115.6 %all-gather.37.cloned.1.call-start = ((), (), s32[]{:S(2)}) async-start(), calls=%async_computation.31 | async-start | bytes 1566720 | tf_op jit(solution)/shard_map/all_gather | solution.py:34
  110.4 155.5 %reduce-scatter.50.cloned.1.call-start = ((), (), s32[]{:S(2)}) async-start(), calls=%async_computation.32 | async-start | bytes 3538944 | tf_op jit(solution)/shard_map/reduce_scatter | solution.py:195
  110.8 84.5 %copy-start.188 = (f32[8,72]{1,0:T(8,128)}, f32[8,72]{1,0:T(8,128)S(1)}, u32[]{:S(2)}) copy-start(f32[8,72]{1,0:T(8,128)S(1)} %add.838) | copy-start | bytes 6916
  230.8 93.2 %all-gather.49.cloned.1.call-start = ((), (), s32[]{:S(2)}) async-start(), calls=%async_computation.41 | async-start | bytes 3538944 | tf_op jit(solution)/shard_map/all_gather | solution.py:182
  287.7 74.6 %all-gather.45.cloned.1.call-start = ((), (), s32[]{:S(2)}) async-start(), calls=%async_computation.37 | async-start | bytes 3538944 | tf_op jit(solution)/shard_map/all_gather | solution.py:182
  303.3 97.3 %all-gather.53.cloned.1.call-start = ((), (), s32[]{:S(2)}) async-start(), calls=%async_computation.45 | async-start | bytes 3538944 | tf_op jit(solution)/shard_map/all_gather | solution.py:182
  304.1 233.2 %all-gather.41.cloned.1.call-start = ((), (), s32[]{:S(2)}) async-start(), calls=%async_computation.34 | async-start | bytes 5640192 | tf_op jit(solution)/shard_map/all_gather | solution.py:35
  304.8 232.5 %all-gather.39.cloned.1.call-start = ((), (), s32[]{:S(2)}) async-start(), calls=%async_computation.33 | async-start | bytes 3538944 | tf_op jit(solution)/shard_map/all_gather | solution.py:202
  305.4 248.9 %all-gather.43.cloned.1.call-start = ((), (), s32[]{:S(2)}) async-start(), calls=%async_computation.35 | async-start | bytes 5640192 | tf_op jit(solution)/shard_map/all_gather | solution.py:36
  306.1 284.4 %all-gather.57.cloned.1.call-start = ((), (), s32[]{:S(2)}) async-start(), calls=%async_computation.49 | async-start | bytes 3538944 | tf_op jit(solution)/shard_map/all_gather | solution.py:220
  309.3 322.7 %reduce-scatter.58.cloned.1.call-start = ((), (), s32[]{:S(2)}) async-start(), calls=%async_computation.42 | async-start | bytes 3538944 | tf_op jit(solution)/shard_map/reduce_scatter | solution.py:195
  470.2 194.2 %reduce-scatter.54.cloned.1.call-start = ((), (), s32[]{:S(2)}) async-start(), calls=%async_computation.38 | async-start | bytes 3538944 | tf_op jit(solution)/shard_map/reduce_scatter | solution.py:195
  503.6 198.4 %reduce-scatter.62.cloned.1.call-start = ((), (), s32[]{:S(2)}) async-start(), calls=%async_computation.46 | async-start | bytes 3538944 | tf_op jit(solution)/shard_map/reduce_scatter | solution.py:195
  537.2 201.6 %reduce-scatter.66.cloned.1.call-start = ((), (), s32[]{:S(2)}) async-start(), calls=%async_computation.50 | async-start | bytes 3538944 | tf_op jit(solution)/shard_map/reduce_scatter | solution.py:233
  618.2 157.6 %reduce-scatter.52.cloned.1.call-start = ((), (), s32[]{:S(2)}) async-start(), calls=%async_computation.36 | async-start | bytes 3538944 | tf_op jit(solution)/shard_map/reduce_scatter | solution.py:210
  631.9 106.9 %copy-start.25 = (bf16[1,512,1152]{2,1,0:T(8,128)(2,1)S(1)}, bf16[1,512,1152]{2,1,0:T(8,128)(2,1)}, u32[]{:S(2)}) copy-start(bf16[1,512,1152]{2,1,0:T(8,128)(2,1)} %reduce-scatter.50.cloned.1.call-done) | copy-start | bytes 3538948
  631.9 106.9 %copy-start.98 = (f32[1152]{0:T(1024)S(1)}, f32[1152]{0:T(1024)}, u32[]{:S(2)}) copy-start(f32[1152]{0:T(1024)} %copy-done.97) | copy-start | bytes 13828
  631.9 106.9 %copy-start.116 = (f32[1152]{0:T(1024)S(1)}, f32[1152]{0:T(1024)}, u32[]{:S(2)}) copy-start(f32[1152]{0:T(1024)} %get-tuple-element.646) | copy-start | bytes 13828
  631.9 181.3 %all-gather.51.cloned.1.call-start = ((), (), s32[]{:S(2)}) async-start(), calls=%async_computation.43 | async-start | bytes 3538944 | tf_op jit(solution)/shard_map/all_gather | solution.py:202
  751.9 99.6 %all-gather.65.cloned.1.call-start = ((), (), s32[]{:S(2)}) async-start(), calls=%async_computation.57 | async-start | bytes 3538944 | tf_op jit(solution)/shard_map/all_gather | solution.py:220
  781.3 132.5 %reduce-scatter.74.cloned.1.call-start = ((), (), s32[]{:S(2)}) async-start(), calls=%async_computation.58 | async-start | bytes 3538944 | tf_op jit(solution)/shard_map/reduce_scatter | solution.py:233
  878.9 86.7 %all-gather.47.cloned.1.call-start = ((), (), s32[]{:S(2)}) async-start(), calls=%async_computation.39 | async-start | bytes 3538944 | tf_op jit(solution)/shard_map/all_gather | solution.py:202
  929.4 74.5 %all-gather.55.cloned.1.call-start = ((), (), s32[]{:S(2)}) async-start(), calls=%async_computation.47 | async-start | bytes 3538944 | tf_op jit(solution)/shard_map/all_gather | solution.py:202
  930.2 110.9 %reduce-scatter.60.cloned.1.call-start = ((), (), s32[]{:S(2)}) async-start(), calls=%async_computation.44 | async-start | bytes 3538944 | tf_op jit(solution)/shard_map/reduce_scatter | solution.py:210
  943.7 134.2 %reduce-scatter.56.cloned.1.call-start = ((), (), s32[]{:S(2)}) async-start(), calls=%async_computation.40 | async-start | bytes 3538944 | tf_op jit(solution)/shard_map/reduce_scatter | solution.py:210
  990.9 124.7 %reduce-scatter.64.cloned.1.call-start = ((), (), s32[]{:S(2)}) async-start(), calls=%async_computation.48 | async-start | bytes 3538944 | tf_op jit(solution)/shard_map/reduce_scatter | solution.py:210
  1029.1 86.5 %copy-start.95 = (bf16[1,512,1152]{2,1,0:T(8,128)(2,1)S(1)}, bf16[1,512,1152]{2,1,0:T(8,128)(2,1)}, u32[]{:S(2)}) copy-start(bf16[1,512,1152]{2,1,0:T(8,128)(2,1)} %reduce-scatter.52.cloned.1.call-done) | copy-start | bytes 3538948
  1029.1 86.5 %copy-start.124 = (f32[1152]{0:T(1024)S(1)}, f32[1152]{0:T(1024)}, u32[]{:S(2)}) copy-start(f32[1152]{0:T(1024)} %get-tuple-element.669) | copy-start | bytes 13828
  1029.1 86.5 %copy-start.151 = (f32[1152]{0:T(1024)S(1)}, f32[1152]{0:T(1024)}, u32[]{:S(2)}) copy-start(f32[1152]{0:T(1024)} %get-tuple-element.641) | copy-start | bytes 13828
  1029.1 86.5 %copy-start.152 = (f32[1152]{0:T(1024)S(1)}, f32[1152]{0:T(1024)}, u32[]{:S(2)}) copy-start(f32[1152]{0:T(1024)} %get-tuple-element.653) | copy-start | bytes 13828
  1029.1 86.5 %copy-start.160 = (f32[1152]{0:T(1024)S(1)}, f32[1152]{0:T(1024)}, u32[]{:S(2)}) copy-start(f32[1152]{0:T(1024)} %get-tuple-element.659) | copy-start | bytes 13828
  1029.1 86.5 %copy-start.162 = (f32[1152]{0:T(1024)S(1)}, f32[1152]{0:T(1024)}, u32[]{:S(2)}) copy-start(f32[1152]{0:T(1024)} %get-tuple-element.884) | copy-start | bytes 13828
  1029.1 128.8 %all-gather.61.cloned.1.call-start = ((), (), s32[]{:S(2)}) async-start(), calls=%async_computation.53 | async-start | bytes 3538944 | tf_op jit(solution)/shard_map/all_gather | solution.py:220
  1121.7 73.7 %all-gather.69.cloned.1.call-start = ((), (), s32[]{:S(2)}) async-start(), calls=%async_computation.61 | async-start | bytes 3538944 | tf_op jit(solution)/shard_map/all_gather | solution.py:220
  1122.3 110.1 %reduce-scatter.70.cloned.1.call-start = ((), (), s32[]{:S(2)}) async-start(), calls=%async_computation.54 | async-start | bytes 3538944 | tf_op jit(solution)/shard_map/reduce_scatter | solution.py:233
  1185.6 84.0 %reduce-scatter.78.cloned.1.call-start = ((), (), s32[]{:S(2)}) async-start(), calls=%async_computation.62 | async-start | bytes 3538944 | tf_op jit(solution)/shard_map/reduce_scatter | solution.py:233
  1223.2 83.8 %all-gather.59.cloned.1.call-start = ((), (), s32[]{:S(2)}) async-start(), calls=%async_computation.51 | async-start | bytes 3538944 | tf_op jit(solution)/shard_map/all_gather | solution.py:241
  1223.8 120.9 %all-gather.63.cloned.1.call-start = ((), (), s32[]{:S(2)}) async-start(), calls=%async_computation.55 | async-start | bytes 3538944 | tf_op jit(solution)/shard_map/all_gather | solution.py:241
  1282.2 289.2 %all-gather.67.cloned.1.call-start = ((), (), s32[]{:S(2)}) async-start(), calls=%async_computation.59 | async-start | bytes 3538944 | tf_op jit(solution)/shard_map/all_gather | solution.py:241
  1313.0 391.5 %reduce-scatter.72.cloned.1.call-start = ((), (), s32[]{:S(2)}) async-start(), calls=%async_computation.56 | async-start | bytes 3538944 | tf_op jit(solution)/shard_map/reduce_scatter | solution.py:263
  1460.9 246.5 %reduce-scatter.68.cloned.1.call-start = ((), (), s32[]{:S(2)}) async-start(), calls=%async_computation.52 | async-start | bytes 3538944 | tf_op jit(solution)/shard_map/reduce_scatter | solution.py:263
  1571.3 151.2 %reduce-scatter.76.cloned.1.call-start = ((), (), s32[]{:S(2)}) async-start(), calls=%async_computation.60 | async-start | bytes 3538944 | tf_op jit(solution)/shard_map/reduce_scatter | solution.py:263
  1687.5 156.0 %all-gather.71.cloned.1.call-start = ((), (), s32[]{:S(2)}) async-start(), calls=%async_computation.63 | async-start | bytes 3538944 | tf_op jit(solution)/shard_map/all_gather | solution.py:241
  1740.0 245.3 %reduce-scatter.96.cloned.1.call-start = ((), (), s32[]{:S(2)}) async-start(), calls=%async_computation.72 | async-start | bytes 442368
  1760.6 233.1 %reduce-scatter.98.cloned.1.call-start = ((), (), s32[]{:S(2)}) async-start(), calls=%async_computation.73 | async-start | bytes 442368
  1789.4 206.0 %reduce-scatter.100.cloned.1.call-start = ((), (), s32[]{:S(2)}) async-start(), calls=%async_computation.74 | async-start | bytes 442368
  1790.4 226.0 %reduce-scatter.84.cloned.1.call-start = ((), (), s32[]{:S(2)}) async-start(), calls=%async_computation.66 | async-start | bytes 5640192 | tf_op jit(solution)/shard_map/reduce_scatter | solution.py:54
  1803.8 214.7 %reduce-scatter.82.cloned.1.call-start = ((), (), s32[]{:S(2)}) async-start(), calls=%async_computation.65 | async-start | bytes 5640192 | tf_op jit(solution)/shard_map/reduce_scatter | solution.py:51
  1843.4 186.0 %reduce-scatter.80.cloned.1.call-start = ((), (), s32[]{:S(2)}) async-start(), calls=%async_computation.64 | async-start | bytes 3538944 | tf_op jit(solution)/shard_map/reduce_scatter | solution.py:263
  1961.8 153.0 %reduce-scatter.102.cloned.1.call-start = ((), (), s32[]{:S(2)}) async-start(), calls=%async_computation.75 | async-start | bytes 442368
  2023.3 93.1 %reduce-scatter.86.cloned.1.call-start = ((), (), s32[]{:S(2)}) async-start(), calls=%async_computation.67 | async-start | bytes 442368
  2025.6 92.0 %reduce-scatter.88.cloned.1.call-start = ((), (), s32[]{:S(2)}) async-start(), calls=%async_computation.68 | async-start | bytes 442368
  2029.4 108.4 %reduce-scatter.90.cloned.1.call-start = ((), (), s32[]{:S(2)}) async-start(), calls=%async_computation.69 | async-start | bytes 442368
  2040.7 98.3 %reduce-scatter.92.cloned.1.call-start = ((), (), s32[]{:S(2)}) async-start(), calls=%async_computation.70 | async-start | bytes 442368
  2048.4 110.5 %reduce-scatter.104.cloned.1.call-start = ((), (), s32[]{:S(2)}) async-start(), calls=%async_computation.77 | async-start | bytes 1566720
  2054.7 190.3 %reduce-scatter.94.cloned.1.call-start = ((), (), s32[]{:S(2)}) async-start(), calls=%async_computation.71 | async-start | bytes 4386816
  2109.1 304.0 %all-reduce.6.cloned.1.call-start = ((), (), s32[]{:S(2)}) async-start(), calls=%async_computation.76 | async-start | bytes 17694720
  (337 other events, 3173.0 us)
Sparse Core Ops, SparseCore 0:
  10.2 80.4 all-gather.30
  92.9 49.9 all-gather.34
  145.0 34.5 all-gather.32
  181.6 39.3 all-gather.36
  230.9 34.9 reduce-scatter.49
  287.8 36.1 all-gather.48
  326.2 36.0 all-gather.44
  364.5 36.0 all-gather.52
  403.0 56.3 all-gather.40
  460.8 34.6 all-gather.38
  497.9 56.3 all-gather.42
  555.8 34.6 all-gather.56
  592.8 34.6 reduce-scatter.57
  629.7 34.7 reduce-scatter.53
  667.2 34.6 reduce-scatter.61
  704.0 34.7 reduce-scatter.65
  741.0 34.6 reduce-scatter.51
  777.1 36.0 all-gather.50
  815.3 36.0 all-gather.64
  879.1 34.7 reduce-scatter.73
  929.6 36.0 all-gather.46
  967.9 36.0 all-gather.54
  1006.3 34.6 reduce-scatter.59
  1043.1 34.7 reduce-scatter.55
  1080.8 34.6 reduce-scatter.63
  1121.8 36.0 all-gather.60
  1159.3 36.0 all-gather.68
  1197.7 34.7 reduce-scatter.69
  1234.8 34.6 reduce-scatter.77
  1270.9 36.0 all-gather.58
  1308.6 36.0 all-gather.62
  1346.2 36.0 all-gather.66
  1461.1 34.7 reduce-scatter.71
  1571.4 34.5 reduce-scatter.67
  1687.6 34.8 reduce-scatter.75
  1740.1 36.0 all-gather.70
  1779.0 12.0 reduce-scatter.95
  1793.9 12.0 reduce-scatter.97
  1808.7 12.0 reduce-scatter.99
  1825.4 79.5 reduce-scatter.83
  1909.5 78.5 reduce-scatter.81
  1991.0 33.7 reduce-scatter.79
  2026.9 12.0 reduce-scatter.101
  2041.2 12.0 reduce-scatter.85
  2055.4 12.0 reduce-scatter.87
  2069.5 12.0 reduce-scatter.89
  2084.3 12.0 reduce-scatter.91
  2099.9 58.8 reduce-scatter.103
  2162.6 71.7 reduce-scatter.93
  2238.1 174.9 all-reduce.5
where the time goes:
time: 2430 us; the launch traced here: 2420 us
  waiting for transfers between devices  959 us (39%)
  matrix products  820 us (34%)
  other arithmetic  315 us (13%)
  local copies, waits for them, and re-layouts  214 us (9%)
  blocking collectives  90.7 us (4%)
    unnamed x61, waiting for transfers between devices  183 us
    unnamed x631, local copies, waits for them, and re-layouts  113 us
    reduce_scatter x4, waiting for transfers between devices, body(): lax.psum_scatter(mlp_part.astype(jnp.bfloat16), 'tensor', scatter_dimensi...  109 us
    reduce_scatter x4, waiting for transfers between devices, body(): lax.psum_scatter(mlp_in_part.astype(jnp.bfloat16), 'tensor', scatter_dime...  109 us
    all_gather x4, waiting for transfers between devices, body(): lax.all_gather((gate_mlp * upstream).astype(jnp.bfloat16), 'tensor', axis...  108 us
    all_gather x4, waiting for transfers between devices, body(): lax.all_gather(norm_first.astype(jnp.bfloat16), 'tensor', axis=1, tiled=T...  104 us
    reduce_scatter x4, waiting for transfers between devices, body(): lax.psum_scatter(attn_part.astype(jnp.bfloat16), 'tensor', scatter_dimens...  93.7 us
    dot_general x8, matrix products, one_block(): jnp.einsum('qhd,khd->hqk', grad_block, values, preferred_element_type=jnp...  87.1 us
  transfers between devices with their start and end apart: 50, of which 30 were waited for; matrix products, arithmetic and copies ran while one was open for 50% of the time, Pallas kernels for 0%

commit v1 on v0

--- a/solution.py
+++ b/solution.py
@@ -3,11 +3,18 @@
 import jax
 import jax.numpy as jnp
 from jax import lax
+from jax.experimental import pallas as pl
+from jax.experimental.pallas import tpu as pltpu
 from jax.sharding import PartitionSpec as P
 
 SEQ = 1024
 HEAD_DIM = 72
 MICRO = 4
+LOG2E = 1.4426950408889634
+WINDOW = 256
+f32 = jnp.float32
+bf16 = jnp.bfloat16
+NT = (((1,), (1,)), ((), ()))
 
 
 EPSILON = 1e-06
@@ -122,7 +129,7 @@
     return (query_grads.reshape(queries.shape), key_grad, value_grad)
 
 
-def body(
+def body_by_heads(
     latent,
     condition,
     cotangent,
@@ -316,6 +323,355 @@
     )
 
 
+def head_window(col, width):
+    start = jnp.minimum(col // 128 * 128, width - WINDOW)
+    return pl.multiple_of(start, 128), col - start
+
+
+def attn_fwd_kernel(q_ref, k_ref, v_ref, o_ref, lse_ref, vt_ref, ot_ref, *, blk):
+    seq, width = q_ref.shape[1:]
+    heads = width // HEAD_DIM
+    c = HEAD_DIM ** -0.5 * LOG2E
+    vt_ref[...] = v_ref[0].T
+    lanes = lax.broadcasted_iota(jnp.int32, (blk, WINDOW), 1)
+
+    def pair(i, carry):
+        for odd in range(2):
+            head = 2 * i + odd
+            start, off = head_window(head * HEAD_DIM, width)
+            keys = k_ref[0, :, pl.ds(start, WINDOW)]
+            mask = (lanes >= off) & (lanes < off + HEAD_DIM)
+            row = pl.multiple_of(i * (2 * HEAD_DIM) + odd * 64, 16)
+            vt = vt_ref[pl.ds(row, 80), :]
+            for b in range(seq // blk):
+                rows = slice(b * blk, (b + 1) * blk)
+                qb = q_ref[0, rows, pl.ds(start, WINDOW)]
+                qb = jnp.where(mask, qb, jnp.zeros_like(qb))
+                st = lax.dot_general(keys, qb, NT, preferred_element_type=f32)
+                m = jnp.max(st, axis=0, keepdims=True)
+                p = jnp.exp2((st - m) * c)
+                l = jnp.sum(p, axis=0, keepdims=True)
+                ot = jnp.dot(vt, p.astype(bf16), preferred_element_type=f32)
+                ot_ref[pl.ds(pl.multiple_of(head * HEAD_DIM, 8), HEAD_DIM), rows] = (
+                    ot[8 * odd : 8 * odd + HEAD_DIM] * (1.0 / l)
+                )
+                lse_ref[0, pl.ds(head, 1), rows] = m * c + jnp.log2(l)
+        return carry
+
+    lax.fori_loop(0, heads // 2, pair, 0)
+    o_ref[0] = ot_ref[...].T.astype(bf16)
+
+
+def attn_fwd(qkv, width, blk=256):
+    n, seq, _ = qkv.shape
+    spec = lambda j: pl.BlockSpec((1, seq, width), lambda b: (b, 0, j))
+    heads = width // HEAD_DIM
+    return pl.pallas_call(
+        partial(attn_fwd_kernel, blk=blk),
+        grid=(n,),
+        in_specs=[spec(0), spec(1), spec(2)],
+        out_specs=[
+            pl.BlockSpec((1, seq, width), lambda b: (b, 0, 0)),
+            pl.BlockSpec((1, heads, seq), lambda b: (b, 0, 0)),
+        ],
+        out_shape=[
+            jax.ShapeDtypeStruct((n, seq, width), bf16),
+            jax.ShapeDtypeStruct((n, heads, seq), f32),
+        ],
+        scratch_shapes=[pltpu.VMEM((width, seq), bf16), pltpu.VMEM((width, seq), f32)],
+        compiler_params=pltpu.CompilerParams(vmem_limit_bytes=56 << 20),
+        cost_estimate=pl.CostEstimate(
+            flops=4 * n * seq * seq * width, bytes_accessed=8 * n * seq * width, transcendentals=n * heads * seq * seq
+        ),
+        name="attention_forward",
+    )(qkv, qkv, qkv)
+
+
+def attn_bwd_kernel(
+    q_ref, k_ref, v_ref, do_ref, o_ref, lse_ref, dqkv_ref,
+    kt_ref, dqt_ref, delta_ref, pt_ref, dst_ref, *, blk
+):
+    seq, width = q_ref.shape[1:]
+    heads = width // HEAD_DIM
+    scale = HEAD_DIM ** -0.5
+    c = scale * LOG2E
+    kt_ref[...] = k_ref[0].T
+    prod = do_ref[0].astype(f32) * o_ref[0].astype(f32)
+    high = prod.astype(bf16)
+    low = (prod - high.astype(f32)).astype(bf16)
+    col = lax.broadcasted_iota(jnp.int32, (heads, width), 1)
+    first = lax.broadcasted_iota(jnp.int32, (heads, width), 0) * HEAD_DIM
+    member = jnp.where((col >= first) & (col < first + HEAD_DIM), 1.0, 0.0).astype(bf16)
+    delta_ref[...] = lax.dot_general(member, high, NT, preferred_element_type=f32) + lax.dot_general(
+        member, low, NT, preferred_element_type=f32
+    )
+    lanes = lax.broadcasted_iota(jnp.int32, (seq, WINDOW), 1)
+
+    def pair(i, carry):
+        for odd in range(2):
+            head = 2 * i + odd
+            start, off = head_window(head * HEAD_DIM, width)
+            window = pl.ds(start, WINDOW)
+            mask = (lanes >= off) & (lanes < off + HEAD_DIM)
+            keys = k_ref[0, :, window]
+            values = v_ref[0, :, window]
+            qm = q_ref[0, :, window]
+            qm = jnp.where(mask, qm, jnp.zeros_like(qm))
+            dom = do_ref[0, :, window]
+            dom = jnp.where(mask, dom, jnp.zeros_like(dom))
+            row = pl.multiple_of(i * (2 * HEAD_DIM) + odd * 64, 16)
+            kt = kt_ref[pl.ds(row, 80), :]
+            for b in range(seq // blk):
+                rows = slice(b * blk, (b + 1) * blk)
+                st = lax.dot_general(keys, qm[rows], NT, preferred_element_type=f32)
+                dpt = lax.dot_general(values, dom[rows], NT, preferred_element_type=f32)
+                p = jnp.exp2(st * c - lse_ref[0, pl.ds(head, 1), rows])
+                dst = (p * (dpt - delta_ref[pl.ds(head, 1), rows])).astype(bf16)
+                pt_ref[:, rows] = p.astype(bf16)
+                dst_ref[:, rows] = dst
+                dqt = jnp.dot(kt, dst, preferred_element_type=f32)
+                dqt_ref[pl.ds(pl.multiple_of(head * HEAD_DIM, 8), HEAD_DIM), rows] = (
+                    dqt[8 * odd : 8 * odd + HEAD_DIM] * scale
+                )
+            dk = jnp.dot(dst_ref[...], qm, preferred_element_type=f32) * scale
+            dv = jnp.dot(pt_ref[...], dom, preferred_element_type=f32)
+            kwin = pl.ds(pl.multiple_of(width + start, 128), WINDOW)
+            vwin = pl.ds(pl.multiple_of(2 * width + start, 128), WINDOW)
+            dqkv_ref[0, :, kwin] = jnp.where(mask, dk.astype(bf16), dqkv_ref[0, :, kwin])
+            dqkv_ref[0, :, vwin] = jnp.where(mask, dv.astype(bf16), dqkv_ref[0, :, vwin])
+        return carry
+
+    lax.fori_loop(0, heads // 2, pair, 0)
+    dqkv_ref[0, :, :width] = dqt_ref[...].T.astype(bf16)
+
+
+def attn_bwd(qkv, grad, mixed, lse, width, blk=256):
+    n, seq, _ = qkv.shape
+    spec = lambda j: pl.BlockSpec((1, seq, width), lambda b: (b, 0, j))
+    heads = width // HEAD_DIM
+    return pl.pallas_call(
+        partial(attn_bwd_kernel, blk=blk),
+        grid=(n,),
+        in_specs=[spec(0), spec(1), spec(2), spec(0), spec(0), pl.BlockSpec((1, heads, seq), lambda b: (b, 0, 0))],
+        out_specs=pl.BlockSpec((1, seq, 3 * width), lambda b: (b, 0, 0)),
+        out_shape=jax.ShapeDtypeStruct((n, seq, 3 * width), bf16),
+        scratch_shapes=[
+            pltpu.VMEM((width, seq), bf16),
+            pltpu.VMEM((width, seq), f32),
+            pltpu.VMEM((heads, seq), f32),
+            pltpu.VMEM((seq, seq), bf16),
+            pltpu.VMEM((seq, seq), bf16),
+        ],
+        compiler_params=pltpu.CompilerParams(vmem_limit_bytes=60 << 20),
+        cost_estimate=pl.CostEstimate(
+            flops=10 * n * seq * seq * width, bytes_accessed=16 * n * seq * width, transcendentals=n * heads * seq * seq
+        ),
+        name="attention_backward",
+    )(qkv, qkv, qkv, grad, mixed, lse)
+
+
+def normed(values):
+    centred = values - jnp.mean(values, axis=-1, keepdims=True)
+    variance = jnp.mean(centred * centred, axis=-1, keepdims=True)
+    inverse = lax.rsqrt(variance + EPSILON)
+    return centred * inverse, inverse
+
+
+def normed_back(grad, norm, inverse):
+    return inverse * (
+        grad
+        - jnp.mean(grad, axis=-1, keepdims=True)
+        - norm * jnp.mean(grad * norm, axis=-1, keepdims=True)
+    )
+
+
+def mm(spec, a, b):
+    return jnp.einsum(spec, a, b, preferred_element_type=f32)
+
+
+def body_by_latents(
+    latent,
+    condition,
+    cotangent,
+    mod_weight,
+    mod_bias,
+    head_weight,
+    head_bias,
+    mix_weight,
+    branch_bias,
+    up_weight,
+    up_bias,
+    down_weight,
+):
+    side = lax.axis_index("tensor")
+    rank = lax.axis_index("dp")
+    groups = lax.axis_size("dp")
+    count, half_seq, width = latent.shape
+    own = count // 2
+    cols = width // 2
+    depth = head_weight.shape[0]
+    hidden = 2 * up_weight.shape[1]
+
+    def swap(a):
+        return lax.ppermute(a, "tensor", [(0, 1), (1, 0)])
+
+    def with_other(a, axis):
+        return jnp.concatenate([a, swap(a)], axis=axis)
+
+    def in_order(mine, other, axis):
+        return jnp.where(
+            side == 0,
+            jnp.concatenate([mine, other], axis=axis),
+            jnp.concatenate([other, mine], axis=axis),
+        )
+
+    def own_latents(a, axis=0):
+        return lax.dynamic_slice_in_dim(a, side * own, own, axis)
+
+    def other_latents(a, axis=0):
+        return lax.dynamic_slice_in_dim(a, (1 - side) * own, own, axis)
+
+    def take(a):
+        return jnp.concatenate([own_latents(a), swap(other_latents(a))], axis=1)
+
+    def give(a):
+        return in_order(a[:, :half_seq], swap(a[:, half_seq:]), 0)
+
+    cond_f = condition.astype(f32)
+    cond_low = jax.nn.silu(cond_f).astype(bf16)
+    cond_all = lax.all_gather(cond_low, "dp", axis=0, tiled=True)
+    cond_cols = lax.dynamic_slice_in_dim(cond_all, rank * depth, depth, 1)
+    partial_mod = mm("bd,dkc->bkc", cond_cols, mod_weight)
+    arrived = lax.all_to_all(partial_mod, "dp", split_axis=0, concat_axis=0, tiled=True)
+    mod_cols = jnp.sum(arrived.reshape(groups, count, 6, cols), axis=0) + mod_bias.astype(f32)
+    modulation = in_order(own_latents(mod_cols), swap(other_latents(mod_cols)), 2)
+    branch = branch_bias.astype(f32)
+    branch_all = in_order(branch, swap(branch), 1)
+    row = lambda k: modulation[:, k][:, None, :]
+    shift_a, scale_a, gate_a, shift_m, scale_m, gate_m = [row(k) for k in range(6)]
+
+    head_all = lax.all_gather(
+        with_other(head_weight, 2).reshape(depth, 3 * width), "dp", axis=0, tiled=True
+    )
+    rest_all = lax.all_gather(
+        jnp.concatenate(
+            [with_other(mix_weight.T, 1), with_other(up_weight, 1), with_other(down_weight.T, 1)],
+            axis=1,
+        ),
+        "dp",
+        axis=0,
+        tiled=True,
+    )
+    mix_t = rest_all[:, :width]
+    up_all = rest_all[:, width : width + hidden]
+    down_t = rest_all[:, width + hidden :]
+    head_bias_f = with_other(head_bias.astype(f32), 1)
+    up_bias_f = with_other(up_bias.astype(f32), 0)
+
+    lat = take(latent)
+    upstream_low = take(cotangent)
+    lat_f = lat.astype(f32)
+    norm1, inv1 = normed(lat_f)
+    attn_in = (norm1 * (1.0 + scale_a) + shift_a).astype(bf16)
+    qkv_bias = jnp.concatenate([head_bias_f[0], jnp.zeros((width,), f32), head_bias_f[1]])
+    qkv = (mm("bsd,dc->bsc", attn_in, head_all) + qkv_bias).astype(bf16)
+    mixed, logsum = attn_fwd(qkv, width)
+    attn_out = mm("bsc,dc->bsd", mixed, mix_t) + branch_all[0]
+    first = lat_f + gate_a * attn_out
+    norm2, inv2 = normed(first)
+    mlp_in = (norm2 * (1.0 + scale_m) + shift_m).astype(bf16)
+    pre_act = mm("bsd,df->bsf", mlp_in, up_all) + up_bias_f
+    act, gelu_back = jax.vjp(gelu_tanh, pre_act)
+    act = act.astype(bf16)
+    mlp_out = mm("bsf,df->bsd", act, down_t) + branch_all[1]
+    block_out = give((first + gate_m * mlp_out).astype(bf16))
+
+    upstream = upstream_low.astype(f32)
+    gate_m_grad = jnp.sum(upstream * mlp_out, axis=1)
+    tail_bias_grad = jnp.sum(gate_m[:, 0] * jnp.sum(upstream, axis=1), axis=0)
+    mlp_grad = (gate_m * upstream).astype(bf16)
+    down_grad = mm("bsd,bsf->df", mlp_grad, act).astype(bf16)
+    down_sum = lax.psum_scatter(down_grad, "dp", scatter_dimension=0, tiled=True)
+    pre_grad = gelu_back(mm("bsd,df->bsf", mlp_grad, down_t))[0].astype(bf16)
+    up_bias_term = jnp.sum(pre_grad, axis=(0, 1), dtype=f32)
+    up_grad = mm("bsd,bsf->df", mlp_in, pre_grad).astype(bf16)
+    up_sum = lax.psum_scatter(up_grad, "dp", scatter_dimension=0, tiled=True)
+    mlp_in_grad = mm("bsf,df->bsd", pre_grad, up_all)
+    shift_m_grad = jnp.sum(mlp_in_grad, axis=1)
+    scale_m_grad = jnp.sum(mlp_in_grad * norm2, axis=1)
+    first_grad = upstream + normed_back(mlp_in_grad * (1.0 + scale_m), norm2, inv2)
+    gate_a_grad = jnp.sum(first_grad * attn_out, axis=1)
+    attn_bias_grad = jnp.sum(gate_a[:, 0] * jnp.sum(first_grad, axis=1), axis=0)
+    attn_grad = (gate_a * first_grad).astype(bf16)
+    mixed_grad = mm("bsd,dc->bsc", attn_grad, mix_t).astype(bf16)
+    mix_grad = mm("bsd,bsc->dc", attn_grad, mixed).astype(bf16)
+    mix_sum = lax.psum_scatter(mix_grad, "dp", scatter_dimension=0, tiled=True)
+    qkv_grad = attn_bwd(qkv, mixed_grad, mixed, logsum, width)
+    head_grad = mm("bsd,bsc->dc", attn_in, qkv_grad).astype(bf16)
+    head_sum = lax.psum_scatter(head_grad, "dp", scatter_dimension=0, tiled=True)
+    qkv_bias_term = jnp.sum(qkv_grad, axis=(0, 1), dtype=f32)
+    attn_in_grad = mm("bsc,dc->bsd", qkv_grad, head_all)
+    shift_a_grad = jnp.sum(attn_in_grad, axis=1)
+    scale_a_grad = jnp.sum(attn_in_grad * norm1, axis=1)
+    lat_grad = first_grad + normed_back(attn_in_grad * (1.0 + scale_a), norm1, inv1)
+    latent_grad = give(lat_grad.astype(bf16))
+
+    mod_low = jnp.stack(
+        [shift_a_grad, scale_a_grad, gate_a_grad, shift_m_grad, scale_m_grad, gate_m_grad], axis=1
+    ).astype(bf16)
+    my_cols = lax.dynamic_slice_in_dim(mod_low, side * cols, cols, 2)
+    other_cols = lax.dynamic_slice_in_dim(mod_low, (1 - side) * cols, cols, 2)
+    mod_rows = lax.all_gather(
+        in_order(my_cols, swap(other_cols), 0), "dp", axis=0, tiled=True
+    )
+    mod_weight_grad = mm("bd,bkc->dkc", cond_cols, mod_rows)
+    mod_bias_grad = jnp.sum(mod_rows, axis=0, dtype=f32)
+    cond_act = mm("bkc,dkc->bd", mod_rows, mod_weight)
+    cond_act = cond_act + swap(cond_act)
+    cond_act = lax.all_to_all(cond_act, "dp", split_axis=0, concat_axis=1, tiled=True)
+    gate = jax.nn.sigmoid(cond_f)
+    condition_grad = cond_act * (gate * (1.0 + cond_f * (1.0 - gate)))
+
+    def joined(summed, axis):
+        mine, other = jnp.split(summed, 2, axis=axis)
+        return mine.astype(f32) + swap(other).astype(f32)
+
+    head_weight_grad = joined(head_sum.reshape(depth, 3, width), 2)
+    mix_weight_grad = joined(mix_sum, 1).T
+    up_weight_grad = joined(up_sum, 1)
+    down_weight_grad = joined(down_sum, 1).T
+    branch_term = jnp.stack([attn_bias_grad, tail_bias_grad])
+    head_term = qkv_bias_term.reshape(3, width)[0::2]
+
+    def bias_half(mine):
+        if mine:
+            pieces = (head_term[:, :cols], lax.dynamic_slice_in_dim(branch_term, side * cols, cols, 1))
+            ups = up_bias_term[: hidden // 2]
+        else:
+            pieces = (
+                head_term[:, cols:],
+                lax.dynamic_slice_in_dim(branch_term, (1 - side) * cols, cols, 1),
+            )
+            ups = up_bias_term[hidden // 2 :]
+        return jnp.concatenate([p.reshape(-1) for p in pieces] + [ups])
+
+    biases = lax.psum(bias_half(True) + swap(bias_half(False)), "dp")
+    return (
+        block_out,
+        latent_grad,
+        condition_grad,
+        mod_weight_grad,
+        mod_bias_grad,
+        head_weight_grad,
+        biases[: 2 * cols].reshape(2, cols),
+        mix_weight_grad,
+        biases[2 * cols : 4 * cols].reshape(2, cols),
+        up_weight_grad,
+        biases[4 * cols :],
+        down_weight_grad,
+    )
+
+
 def solution(mesh):
     placed = (
         P("dp", "tensor", None),
@@ -331,8 +687,9 @@
         P("tensor"),
         P("tensor", "dp"),
     )
+    whole_latents = mesh.shape["tensor"] == 2
     return jax.shard_map(
-        body,
+        body_by_latents if whole_latents else body_by_heads,
         mesh=mesh,
         in_specs=placed,
         out_specs=(

time: 2430 us -> 1040 us (0.43)
  waiting for transfers between devices: 959 us -> 239 us
  matrix products: 820 us -> 354 us
  other arithmetic: 315 us -> 46.4 us
  Pallas kernels: 0 us -> 203 us
  local copies, waits for them, and re-layouts: 214 us -> 36.9 us
  starting transfers between devices: 3.51 us -> 31.5 us
    dot_general x112 -> x15, matrix products: 820 us -> 354 us  [mm(): return jnp.einsum(spec, a, b, preferred_element_type=f32)]
    all_gather x21 -> x2, waiting for transfers between devices: 449 us -> 0.02 us  [the longest x1 0.02 us: body_by_latents(): lax.all_gather(with_other(head_weight, 2).reshape(depth, 3 * width), 'dp'...]
    reduce_scatter x18 -> x2, waiting for transfers between devices: 326 us -> 56.4 us  [the longest x1 56.4 us: body_by_latents(): lax.psum_scatter(down_grad, 'dp', scatter_dimension=0, tiled=True)]
    pallas_call x0 -> x2, Pallas kernels: none -> 203 us  [the longest x1 116 us: attn_bwd(): pl.pallas_call(partial(attn_bwd_kernel, blk=blk), grid=(n,), in_specs=[sp...]
    unnamed x61 -> x8, waiting for transfers between devices: 183 us -> 0.12 us
    ppermute x0 -> x19, waiting for transfers between devices: none -> 178 us  [swap(): return lax.ppermute(a, 'tensor', [(0, 1), (1, 0)])]
    convert_element_type x32 -> x5, other arithmetic: 148 us -> 7.72 us  [the longest x1 7.71 us: body_by_latents(): latent_grad = give(lat_grad.astype(bf16))]
    reduce_sum x38 -> x8, other arithmetic: 125 us -> 17.5 us  [the longest x1 8.65 us: body_by_latents(): qkv_bias_term = jnp.sum(qkv_grad, axis=(0, 1), dtype=f32)]
  transfers between devices with their start and end apart: 50 -> 27, of which waited for: 30 -> 11; matrix products, arithmetic and copies ran while one was open for 50% -> 28% of each run, Pallas kernels for 0% -> 20%
where the time goes in v1:
time: 1040 us; the launch traced here: 1030 us
  matrix products  354 us (34%)
  waiting for transfers between devices  239 us (23%)
  Pallas kernels  203 us (20%)
  blocking collectives  108 us (10%)
  other arithmetic  46.4 us (4%)
  local copies, waits for them, and re-layouts  36.9 us (4%)
  starting transfers between devices  31.5 us (3%)
  between operations  15.8 us (2%)
    dot_general x15, matrix products, mm(): return jnp.einsum(spec, a, b, preferred_element_type=f32)  354 us
    ppermute x19, waiting for transfers between devices, swap(): return lax.ppermute(a, 'tensor', [(0, 1), (1, 0)])  178 us
    pallas_call x1, Pallas kernels, attn_bwd(): pl.pallas_call(partial(attn_bwd_kernel, blk=blk), grid=(n,), in_specs=[sp...  116 us
    pallas_call x1, Pallas kernels, attn_fwd(): pl.pallas_call(partial(attn_fwd_kernel, blk=blk), grid=(n,), in_specs=[sp...  87.1 us
    psum x1, blocking collectives, body_by_latents(): biases = lax.psum(bias_half(True) + swap(bias_half(False)), 'dp')  59.3 us
    reduce_scatter x1, waiting for transfers between devices, body_by_latents(): lax.psum_scatter(down_grad, 'dp', scatter_dimension=0, tiled=True)  56.4 us
    all_gather x1, blocking collectives, body_by_latents(): lax.all_gather(in_order(my_cols, swap(other_cols), 0), 'dp', axis=0, tile...  25.9 us
    ppermute x19, starting transfers between devices, swap(): return lax.ppermute(a, 'tensor', [(0, 1), (1, 0)])  23.4 us
  transfers between devices with their start and end apart: 27, of which 11 were waited for; matrix products, arithmetic and copies ran while one was open for 28% of the time, Pallas kernels for 20%

profile of v1, /device:TPU:0, one launch (start us, length us, event | category | flops | bytes accessed | tf_op | source)
XLA Modules:
  0.0 1033.9 jit_solution(10353787955440629285)
XLA Ops:
  7.2 3.0 collective-permute-start.2
  10.2 6.8 collective-permute-done.2
  17.1 1.1 maximum_bitcast_fusion
  19.1 1.8 collective-permute-start.5
  21.1 1.7 collective-permute-start.4
  22.9 14.5 %collective-permute-done.4 = bf16[72,576]{1,0:T(8,128)(2,1)S(1)} collective-permute-done((bf16[72,576]{1,0:T(8,128)(2,1)}, bf16[72,576]{1,0:T(8,128)(2,1)S(1)}, u32[]{:S(2)}, u32[]{:S(2)}) %collective-permute-start.4) | collective-permute-done | bytes 82976 | tf_op jit(solution)/shard_map/ppermute | solution.py:516
  37.4 3.2 concatenate.63
  41.4 22.5 %all-gather = bf16[16,4,1152]{2,1,0:T(4,128)(2,1)S(1)} all-gather(bf16[1,4,1152]{2,1,0:T(4,128)(2,1)S(1)} %fusion.54), channel_id=1, replica_groups=mesh['dp'=16,'tensor'=2] {'dp'}, dimensions={0}, use_global_device_ids=true | all-gather | bytes 156672 | tf_op jit(solution)/shard_map/all_gather | solution.py:542
  64.3 1.7 copy.60
  65.9 4.4 all-to-all-start
  70.4 4.9 constant_dynamic-slice_fusion.3
  75.3 1.4 collective-permute-start.10
  77.4 1.5 collective-permute-start.3
  78.9 4.1 constant_dynamic-slice_fusion.7
  83.6 1.4 collective-permute-start.8
  85.1 44.8 %collective-permute-done.3 = f32[2,576]{1,0:T(2,128)S(1)} collective-permute-done((f32[2,576]{1,0:T(2,128)S(1)}, f32[2,576]{1,0:T(2,128)S(1)}, u32[]{:S(2)}, u32[]{:S(2)}) %collective-permute-start.3) | collective-permute-done | bytes 4640 | tf_op jit(solution)/shard_map/ppermute | solution.py:516
  130.7 1.6 reduce_sum.198
  132.3 1.5 collective-permute-start.1
  133.8 46.6 %collective-permute-done.8 = f32[2304]{0:T(1024)S(1)} collective-permute-done((f32[2304]{0:T(1024)S(1)}, f32[2304]{0:T(1024)S(1)}, u32[]{:S(2)}, u32[]{:S(2)}) %collective-permute-start.8) | collective-permute-done | bytes 9248 | tf_op jit(solution)/shard_map/ppermute | solution.py:516
  181.7 2.4 convert_reduce_fusion.3
  184.1 3.0 fusion.24
  187.2 26.5 %add_convert_fusion.q_ref.k_ref.v_ref = bf16[2,1024,3456]{2,1,0:T(8,128)(2,1)} fusion(f32[3456]{0:T(1024)S(1)} %pad_maximum_fusion.4, bf16[1152,3456]{1,0:T(8,128)(2,1)} %all-gather.4.cloned.1.call-done, f32[2,1152]{1,0:T(2,128)S(1)} %get-tuple-element.124, f32[2,1152]{1,0:T(2,128)S(1)} %get-tuple-element.125, f32[2,1024]{1,0:T(2,128)S(1)} %add_rsqrt_fusion.1, ...), kind=kOutput, calls=%fused_computation.12 | convolution fusion | flops 16342843392 | bytes 26885632 | tf_op jit(solution)/shard_map/bsd,dc->bsc/dot_general | solution.py:489
  213.6 87.1 %attention_forward.1 = (bf16[2,1024,1152]{2,1,0:T(8,128)(2,1)}, f32[2,16,1024]{2,1,0:T(8,128)}) custom-call(bf16[2,1024,3456]{2,1,0:T(8,128)(2,1)} %add_convert_fusion.q_ref.k_ref.v_ref, bf16[2,1024,3456]{2,1,0:T(8,128)(2,1)} %add_convert_fusion.q_ref.k_ref.v_ref, bf16[2,1024,3456]{2,1,0:T(8,128)(2,1)} %add_convert_fusion.q_ref.k_ref.v_ref), custom_call_target="tpu_custom_call" | custom-call | flops 9663676416 | bytes 18874368 | tf_op jit(solution)/shard_map/attention_forward/pallas_call | solution.py:369
  300.8 13.3 %fusion.63 = (f32[2,1024]{1,0:T(2,128)S(1)}, f32[2,1024,1152]{2,1,0:T(8,128)S(1)}, f32[2,1024,1152]{2,1,0:T(8,128)}) fusion(f32[1152]{0:T(1024)S(1)} %get-tuple-element.79, f32[2,1152]{1,0:T(2,128)S(1)} %get-tuple-element.123, bf16[2,512,1152]{2,1,0:T(8,128)(2,1)} %collective-permute-done, bf16[2,512,1152]{2,1,0:T(8,128)(2,1)S(1)} %get-tuple-element.93, ...), kind=kOutput, calls=%fused_computation.153 | convolution fusion | flops 5454690304 | bytes 30987776 | tf_op jit(solution)/shard_map/bsc,dc->bsd/dot_general | solution.py:489
  314.1 3.6 copy-done.3
  317.7 1.1 multiply_reduce_fusion.3
  318.8 42.1 %multiply_convert_fusion = (bf16[2,1024,4608]{2,1,0:T(8,128)(2,1)}, f32[2,1024,4608]{2,1,0:T(8,128)}) fusion(f32[4608]{0:T(1024)S(1)} %pad_maximum_fusion.2, bf16[1152,10368]{1,0:T(8,128)(2,1)} %all-gather.6.cloned.1.call-done, f32[2,1024,1152]{2,1,0:T(8,128)} %copy-done.3, f32[2,1152]{1,0:T(2,128)S(1)} %get-tuple-element.120, ...), kind=kOutput, calls=%fused_computation.10 | convolution fusion | flops 21849440256 | bytes 76730368 | tf_op jit(solution)/shard_map/bsd,df->bsf/dot_general | solution.py:489
  360.9 53.7 %convert_reduce_fusion = (f32[4608]{0:T(1024)}, bf16[2,1024,4608]{2,1,0:T(8,128)(2,1)}) fusion(f32[2,1024,4608]{2,1,0:T(8,128)} %get-tuple-element.115, f32[4608]{0:T(1024)S(1)} %pad_maximum_fusion.2, bf16[1152,10368]{1,0:T(8,128)(2,1)} %all-gather.6.cloned.1.call-done, f32[2,1152]{1,0:T(2,128)S(1)} %get-tuple-element.122, ...), kind=kOutput, calls=%fused_computation.9 | convolution fusion | flops 21974478848 | bytes 72004608 | tf_op jit(solution)/shard_map/bsd,df->bsf/dot_general | solution.py:489
  414.7 34.8 %multiply_reduce_fusion = (bf16[2,1152]{1,0:T(2,128)(2,1)}, f32[2,1024]{1,0:T(2,128)S(1)}, f32[2,1024]{1,0:T(2,128)S(1)}, bf16[2,1152]{1,0:T(2,128)(2,1)}, f32[2,1024,1152]{2,1,0:T(8,128)}) fusion(f32[2,1024,1152]{2,1,0:T(8,128)} %copy-done.3, f32[2,1024]{1,0:T(2,128)S(1)} %add_rsqrt_fusion, f32[2,1024]{1,0:T(2,128)S(1)} %broadcast_multiply_fusion.4, ...), kind=kOutput, calls=%fused_computation.45 | convolution fusion | flops 21764497408 | bytes 48416768 | tf_op jit(solution)/shard_map/bsf,df->bsd/dot_general | solution.py:489
  449.6 40.9 %convert_reduce_fusion.2 = (f32[2,1152]{1,0:T(2,128)}, bf16[2,1152]{1,0:T(2,128)(2,1)}, bf16[2,1024,1152]{2,1,0:T(8,128)(2,1)}, bf16[2,1152]{1,0:T(2,128)(2,1)}, f32[2,1152]{1,0:T(2,128)}, /*index=5*/f32[2,1024,1152]{2,1,0:T(8,128)}) fusion(bf16[2,512,1152]{2,1,0:T(8,128)(2,1)} %collective-permute-done.10, bf16[2,512,1152]{2,1,0:T(8,128)(2,1)S(1)} %copy-done.5, ...), kind=kOutput, calls=%fused_computation.18 | convolution fusion | flops 21797527552 | bytes 76765184 | tf_op jit(solution)/shard_map/bsf,df->bsd/dot_general | solution.py:489
  490.5 12.9 %fusion.33 = bf16[1152,1152]{1,0:T(8,128)(2,1)} fusion(bf16[2,1024,1152]{2,1,0:T(8,128)(2,1)} %get-tuple-element.14.o_ref, f32[2,1024,1152]{2,1,0:T(8,128)} %get-tuple-element.86, f32[2,1152]{1,0:T(2,128)S(1)} %copy-done.28), kind=kOutput, calls=%fused_computation.62 | convolution fusion | flops 5441863680 | bytes 16819200 | tf_op jit(solution)/shard_map/bsd,bsc->dc/dot_general | solution.py:489
  503.4 11.9 %convolution_convert_fusion.do_ref = bf16[2,1024,1152]{2,1,0:T(8,128)(2,1)} fusion(bf16[1152,10368]{1,0:T(8,128)(2,1)} %all-gather.6.cloned.1.call-done, f32[2,1024,1152]{2,1,0:T(8,128)} %get-tuple-element.86, f32[2,1152]{1,0:T(2,128)S(1)} %copy-done.28), kind=kOutput, calls=%fused_computation.63 | convolution fusion | flops 5442895872 | bytes 16819200 | tf_op jit(solution)/shard_map/bsd,dc->bsc/dot_general | solution.py:489
  515.4 115.7 %attention_backward.1 = bf16[2,1024,3456]{2,1,0:T(8,128)(2,1)} custom-call(bf16[2,1024,3456]{2,1,0:T(8,128)(2,1)} %add_convert_fusion.q_ref.k_ref.v_ref, bf16[2,1024,3456]{2,1,0:T(8,128)(2,1)} %add_convert_fusion.q_ref.k_ref.v_ref, bf16[2,1024,3456]{2,1,0:T(8,128)(2,1)} %add_convert_fusion.q_ref.k_ref.v_ref, ...), custom_call_target="tpu_custom_call" | custom-call | flops 24159191040 | bytes 37748736 | tf_op jit(solution)/shard_map/attention_backward/pallas_call | solution.py:452
  631.1 26.0 %fusion.9 = bf16[1152,3456]{1,0:T(8,128)(2,1)} fusion(bf16[2,1024,3456]{2,1,0:T(8,128)(2,1)} %attention_backward.1, f32[2,1152]{1,0:T(2,128)S(1)} %copy-done.26, f32[2,1152]{1,0:T(2,128)S(1)} %copy-done.15, f32[2,1024]{1,0:T(2,128)S(1)} %copy-done.18, f32[2,1024]{1,0:T(2,128)S(1)} %copy-done.13, bf16[2,512,1152]{2,1,0:T(8,128)(2,1)} %collective-permute-done, ...), kind=kOutput, calls=%fused_computation.22 | convolution fusion | flops 16332668928 | bytes 26871808 | tf_op jit(solution)/shard_map/bsd,bsc->dc/dot_general | solution.py:489
  657.2 32.4 %fusion.7 = bf16[1152,4608]{1,0:T(8,128)(2,1)} fusion(bf16[2,1024,4608]{2,1,0:T(8,128)(2,1)} %get-tuple-element.119, f32[2,1024,1152]{2,1,0:T(8,128)} %copy-done.3, f32[2,1152]{1,0:T(2,128)S(1)} %copy-done.24, f32[2,1152]{1,0:T(2,128)S(1)} %get-tuple-element.121, f32[2,1024]{1,0:T(2,128)S(1)} %add_rsqrt_fusion, f32[2,1024]{1,0:T(2,128)S(1)} %broadcast_multiply_fusion.4), kind=kOutput, calls=%fused_computation.15 | convolution fusion | flops 21760376832 | bytes 38963200 | tf_op jit(solution)/shard_map/bsd,bsf->df/dot_general | solution.py:489
  691.5 29.0 %fusion.8 = bf16[1152,4608]{1,0:T(8,128)(2,1)} fusion(bf16[2,1024,4608]{2,1,0:T(8,128)(2,1)} %get-tuple-element.114, f32[2,1152]{1,0:T(2,128)S(1)} %get-tuple-element.122, bf16[2,512,1152]{2,1,0:T(8,128)(2,1)} %collective-permute-done.10, bf16[2,512,1152]{2,1,0:T(8,128)(2,1)} %get-tuple-element.89), kind=kOutput, calls=%fused_computation.16 | convolution fusion | flops 21762736128 | bytes 34219008 | tf_op jit(solution)/shard_map/bsd,bsf->df/dot_general | solution.py:489
  720.5 4.9 fusion.65
  725.5 1.5 collective-permute-start.9
  727.0 27.8 %fusion.23 = (bf16[2,1152]{1,0:T(2,128)(2,1)S(1)}, f32[2,1024]{1,0:T(2,128)S(1)}, f32[2,1024]{1,0:T(2,128)S(1)}, bf16[2,1152]{1,0:T(2,128)(2,1)S(1)}, f32[2,1024,1152]{2,1,0:T(8,128)}) fusion(f32[2,1024]{1,0:T(2,128)S(1)} %copy-done.18, f32[2,1024]{1,0:T(2,128)S(1)} %copy-done.13, bf16[2,512,1152]{2,1,0:T(8,128)(2,1)} %collective-permute-done, ...), kind=kOutput, calls=%fused_computation.41 | convolution fusion | flops 16338116608 | bytes 36325376 | tf_op jit(solution)/shard_map/bsc,dc->bsd/dot_general | solution.py:489
  754.8 7.7 fusion.22
  762.6 2.6 fusion.64
  765.8 1.7 collective-permute-start.12
  767.8 8.7 convert_reduce_fusion.1
  776.9 52.7 %collective-permute-done.12 = bf16[2,6,576]{2,0,1:T(2,128)(2,1)S(1)} collective-permute-done((bf16[2,6,576]{2,0,1:T(2,128)(2,1)S(1)}, bf16[2,6,576]{2,0,1:T(2,128)(2,1)S(1)}, u32[]{:S(2)}, u32[]{:S(2)}) %collective-permute-start.12) | collective-permute-done | bytes 13856 | tf_op jit(solution)/shard_map/ppermute | solution.py:516
  829.7 25.9 %all_gather.15 = bf16[64,6,576]{2,1,0:T(8,128)(2,1)S(1)} all-gather(bf16[4,6,576]{2,1,0:T(8,128)(2,1)S(1)} %copy.62), channel_id=1, replica_groups=mesh['dp'=16,'tensor'=2] {'dp'}, dimensions={0}, use_global_device_ids=true | all-gather | bytes 470016 | tf_op jit(solution)/shard_map/all_gather | solution.py:624
  855.9 2.2 fusion.39
  858.8 1.4 collective-permute-start.13
  860.3 59.3 %psum.7 = f32[4608]{0:T(1024)S(1)} all-reduce(f32[4608]{0:T(1024)S(1)} %maximum_add_fusion), channel_id=1, replica_groups=mesh['dp'=16,'tensor'=2] {'dp'}, use_global_device_ids=true, to_apply=%region_23.24 | all-reduce | flops 4608 | bytes 36864 | tf_op jit(solution)/shard_map/psum | solution.py:658
  920.2 3.5 all-to-all-start.1
  925.7 4.6 all-to-all-done.1
  930.4 1.0 dynamic-slice.5
  932.8 3.3 collective-permute-done.16
  936.1 1.6 add_bitcast_fusion.1
  937.6 5.9 maximum_select_fusion
  943.6 1.5 reshape.120
  946.1 1.1 split.35
  947.2 1.4 collective-permute-start.17
  948.7 7.0 maximum_select_fusion.1
  955.7 1.3 collective-permute-done.14
  958.0 56.4 %reduce-scatter.8.cloned.1.call-done = bf16[72,4608]{1,0:T(8,128)(2,1)} async-done(((bf16[1152,4608]{1,0:T(8,128)(2,1)}), bf16[72,4608]{1,0:T(8,128)(2,1)}) %reduce-scatter.8.cloned.1.call-update) | async-done | bytes 663568 | tf_op jit(solution)/shard_map/reduce_scatter | solution.py:594
  1014.5 1.0 split.37
  1015.5 1.5 collective-permute-start.18
  1017.9 7.0 collective-permute-done.18
  1024.9 1.9 add_bitcast_fusion
  (190 shorter events, 16.6 us)
Async XLA Ops:
  7.2 56.7 %copy-start = (bf16[72,6,576]{2,0,1:T(8,128)(2,1)S(1)}, bf16[72,6,576]{2,0,1:T(8,128)(2,1)}, u32[]{:S(2)}) copy-start(bf16[72,6,576]{2,0,1:T(8,128)(2,1)} %param.15) | copy-start | bytes 1492996
  7.2 180.0 %all-gather.4.cloned.1.call-start = ((), (), s32[]{:S(2)}) async-start(), calls=%async_computation.5 | async-start | bytes 8460288 | tf_op jit(solution)/shard_map/all_gather | solution.py:553
  7.2 9.8 collective-permute-start.2
  19.0 281.8 %all-gather.6.cloned.1.call-start = ((), (), s32[]{:S(2)}) async-start(), calls=%async_computation.6 | async-start | bytes 25380864 | tf_op jit(solution)/shard_map/all_gather | solution.py:556
  19.1 18.3 %collective-permute-start.5 = (bf16[72,2304]{1,0:T(8,128)(2,1)}, bf16[72,2304]{1,0:T(8,128)(2,1)S(1)}, u32[]{:S(2)}, u32[]{:S(2)}) collective-permute-start(bf16[72,2304]{1,0:T(8,128)(2,1)} %param.21), channel_id=1, source_target_pairs={{0,1},{1,0},{2,3},{3,2},{4,5},{5,4},{6,7},{7,6},{8,9},{9,8},{10,11... | collective-permute-start | bytes 995336 | tf_op jit(solution)/shard_map/ppermute | solution.py:516
  20.9 16.5 %collective-permute-start.6 = (bf16[72,2304]{1,0:T(8,128)(2,1)}, bf16[72,2304]{1,0:T(8,128)(2,1)S(1)}, u32[]{:S(2)}, u32[]{:S(2)}) collective-permute-start(bf16[72,2304]{1,0:T(8,128)(2,1)} %bitcast.111), channel_id=1, source_target_pairs={{0,1},{1,0},{2,3},{3,2},{4,5},{5,4},{6,7},{7,6},{8,9},{9,8},{10,11... | collective-permute-start | bytes 995336 | tf_op jit(solution)/shard_map/ppermute | solution.py:516
  21.1 16.3 %collective-permute-start.4 = (bf16[72,576]{1,0:T(8,128)(2,1)}, bf16[72,576]{1,0:T(8,128)(2,1)S(1)}, u32[]{:S(2)}, u32[]{:S(2)}) collective-permute-start(bf16[72,576]{1,0:T(8,128)(2,1)} %bitcast.114), channel_id=1, source_target_pairs={{0,1},{1,0},{2,3},{3,2},{4,5},{5,4},{6,7},{7,6},{8,9},{9,8},{10,11... | collective-permute-start | bytes 248840 | tf_op jit(solution)/shard_map/ppermute | solution.py:516
  40.6 36.1 %copy-start.37 = (bf16[2,576]{1,0:T(2,128)(2,1)S(1)}, bf16[2,576]{1,0:T(2,128)(2,1)}, u32[]{:S(2)}) copy-start(bf16[2,576]{1,0:T(2,128)(2,1)} %param.20) | copy-start | bytes 6916
  40.6 36.7 %copy-start.38 = (bf16[2,576]{1,0:T(2,128)(2,1)S(1)}, bf16[2,576]{1,0:T(2,128)(2,1)}, u32[]{:S(2)}) copy-start(bf16[2,576]{1,0:T(2,128)(2,1)} %param.18) | copy-start | bytes 6916
  63.9 13.5 %copy-start.7 = (bf16[64,1152]{1,0:T(8,128)(2,1)}, bf16[64,1152]{1,0:T(8,128)(2,1)S(1)}, u32[]{:S(2)}) copy-start(bf16[64,1152]{1,0:T(8,128)(2,1)S(1)} %reshape.129) | copy-start | bytes 442372
  65.9 64.8 %all-to-all-start = ((f32[64,6,576]{2,1,0:T(8,128)}), f32[64,6,576]{2,1,0:T(8,128)}, u32[]{:S(2)}, u32[]{:S(2)}) async-start(f32[64,6,576]{2,1,0:T(8,128)} %copy.60), calls=%async_computation | async-start | bytes 2621440 | tf_op jit(solution)/shard_map/all_to_all | solution.py:545
  70.3 860.1 %all-reduce.4.cloned.1.call-start = ((), (), s32[]{:S(2)}) async-start(), calls=%async_computation.9 | async-start | bytes 5308416
  70.4 13.2 %copy-start.32 = (bf16[2304]{0:T(1024)(128)(2,1)S(1)}, bf16[2304]{0:T(1024)(128)(2,1)}, u32[]{:S(2)}) copy-start(bf16[2304]{0:T(1024)(128)(2,1)} %param.22) | copy-start | bytes 13828
  70.4 14.7 %copy-start.20 = (bf16[6,576]{1,0:T(8,128)(2,1)S(1)}, bf16[6,576]{1,0:T(8,128)(2,1)}, u32[]{:S(2)}) copy-start(bf16[6,576]{1,0:T(8,128)(2,1)} %param.16) | copy-start | bytes 20740
  75.3 285.6 %collective-permute-start.10 = (bf16[2,512,1152]{2,1,0:T(8,128)(2,1)}, bf16[2,512,1152]{2,1,0:T(8,128)(2,1)}, u32[]{:S(2)}, u32[]{:S(2)}) collective-permute-start(bf16[2,512,1152]{2,1,0:T(8,128)(2,1)} %get-tuple-element.90), channel_id=1, source_target_pairs={{0,1},{1,0},{2,3},{3,2},{4,5},{5,4},{6,7},{7,6},{8,9},{9,8},{10,11... | collective-permute-start | bytes 7077896 | tf_op jit(solution)/shard_map/ppermute | solution.py:516
  76.8 53.2 %collective-permute-start.7 = (f32[2,576]{1,0:T(2,128)S(1)}, f32[2,576]{1,0:T(2,128)S(1)}, u32[]{:S(2)}, u32[]{:S(2)}) collective-permute-start(f32[2,576]{1,0:T(2,128)S(1)} %convert_element_type.107), channel_id=1, source_target_pairs={{0,1},{1,0},{2,3},{3,2},{4,5},{5,4},{6,7},{7,6},{8,9},{9,8},{10,11... | collective-permute-start | bytes 13832 | tf_op jit(solution)/shard_map/ppermute | solution.py:516
  77.4 52.5 %collective-permute-start.3 = (f32[2,576]{1,0:T(2,128)S(1)}, f32[2,576]{1,0:T(2,128)S(1)}, u32[]{:S(2)}, u32[]{:S(2)}) collective-permute-start(f32[2,576]{1,0:T(2,128)S(1)} %convert_element_type.105), channel_id=1, source_target_pairs={{0,1},{1,0},{2,3},{3,2},{4,5},{5,4},{6,7},{7,6},{8,9},{9,8},{10,11... | collective-permute-start | bytes 13832 | tf_op jit(solution)/shard_map/ppermute | solution.py:516
  83.0 217.8 %copy-start.1 = (bf16[2,512,1152]{2,1,0:T(8,128)(2,1)}, bf16[2,512,1152]{2,1,0:T(8,128)(2,1)S(1)}, u32[]{:S(2)}) copy-start(bf16[2,512,1152]{2,1,0:T(8,128)(2,1)S(1)} %get-tuple-element.93) | copy-start | bytes 7077892
  83.0 98.7 %collective-permute-start = (bf16[2,512,1152]{2,1,0:T(8,128)(2,1)}, bf16[2,512,1152]{2,1,0:T(8,128)(2,1)}, u32[]{:S(2)}, u32[]{:S(2)}) collective-permute-start(bf16[2,512,1152]{2,1,0:T(8,128)(2,1)} %get-tuple-element.94), channel_id=1, source_target_pairs={{0,1},{1,0},{2,3},{3,2},{4,5},{5,4},{6,7},{7,6},{8,9},{9,8},{10,11... | collective-permute-start | bytes 7077896 | tf_op jit(solution)/shard_map/ppermute | solution.py:516
  83.6 96.8 %collective-permute-start.8 = (f32[2304]{0:T(1024)S(1)}, f32[2304]{0:T(1024)S(1)}, u32[]{:S(2)}, u32[]{:S(2)}) collective-permute-start(f32[2304]{0:T(1024)S(1)} %convert_element_type.109), channel_id=1, source_target_pairs={{0,1},{1,0},{2,3},{3,2},{4,5},{5,4},{6,7},{7,6},{8,9},{9,8},{10,11... | collective-permute-start | bytes 27656 | tf_op jit(solution)/shard_map/ppermute | solution.py:516
  130.7 170.1 %copy-start.30 = (f32[1152]{0:T(1024)}, f32[1152]{0:T(1024)S(1)}, u32[]{:S(2)}) copy-start(f32[1152]{0:T(1024)S(1)} %get-tuple-element.79) | copy-start | bytes 13828
  132.3 48.5 %collective-permute-start.1 = (f32[2,6,576]{2,1,0:T(8,128)S(1)}, f32[2,6,576]{2,1,0:T(8,128)S(1)}, u32[]{:S(2)}, u32[]{:S(2)}) collective-permute-start(f32[2,6,576]{2,1,0:T(8,128)S(1)} %get-tuple-element.96), channel_id=1, source_target_pairs={{0,1},{1,0},{2,3},{3,2},{4,5},{5,4},{6,7},{7,6},{8,9},{9,8},{10,11... | collective-permute-start | bytes 82952 | tf_op jit(solution)/shard_map/ppermute | solution.py:516
  181.6 119.2 %copy-start.27 = (f32[2,1152]{1,0:T(2,128)}, f32[2,1152]{1,0:T(2,128)S(1)}, u32[]{:S(2)}) copy-start(f32[2,1152]{1,0:T(2,128)S(1)} %get-tuple-element.123) | copy-start | bytes 27652
  181.6 32.0 %copy-start.14 = (f32[2,1152]{1,0:T(2,128)}, f32[2,1152]{1,0:T(2,128)S(1)}, u32[]{:S(2)}) copy-start(f32[2,1152]{1,0:T(2,128)S(1)} %get-tuple-element.125) | copy-start | bytes 27652
  181.7 32.0 %copy-start.25 = (f32[2,1152]{1,0:T(2,128)}, f32[2,1152]{1,0:T(2,128)S(1)}, u32[]{:S(2)}) copy-start(f32[2,1152]{1,0:T(2,128)S(1)} %get-tuple-element.124) | copy-start | bytes 27652
  181.7 137.1 %copy-start.23 = (f32[2,1152]{1,0:T(2,128)}, f32[2,1152]{1,0:T(2,128)S(1)}, u32[]{:S(2)}) copy-start(f32[2,1152]{1,0:T(2,128)S(1)} %get-tuple-element.120) | copy-start | bytes 27652
  184.1 29.5 %copy-start.12 = (f32[2,1024]{1,0:T(2,128)}, f32[2,1024]{1,0:T(2,128)S(1)}, u32[]{:S(2)}) copy-start(f32[2,1024]{1,0:T(2,128)S(1)} %broadcast_multiply_fusion.5) | copy-start | bytes 24580
  187.1 26.5 %copy-start.17 = (f32[2,1024]{1,0:T(2,128)}, f32[2,1024]{1,0:T(2,128)S(1)}, u32[]{:S(2)}) copy-start(f32[2,1024]{1,0:T(2,128)S(1)} %add_rsqrt_fusion.1) | copy-start | bytes 24580
  314.1 3.6 copy-start.3
  318.8 42.1 %copy-start.5 = (bf16[2,512,1152]{2,1,0:T(8,128)(2,1)S(1)}, bf16[2,512,1152]{2,1,0:T(8,128)(2,1)}, u32[]{:S(2)}) copy-start(bf16[2,512,1152]{2,1,0:T(8,128)(2,1)} %get-tuple-element.89) | copy-start | bytes 7077892
  414.7 34.8 %copy-start.29 = (f32[1152]{0:T(1024)S(1)}, f32[1152]{0:T(1024)}, u32[]{:S(2)}) copy-start(f32[1152]{0:T(1024)} %get-tuple-element.78) | copy-start | bytes 13828
  414.7 34.9 %copy-start.31 = (f32[1152]{0:T(1024)S(1)}, f32[1152]{0:T(1024)}, u32[]{:S(2)}) copy-start(f32[1152]{0:T(1024)} %copy-done.30) | copy-start | bytes 13828
  449.5 40.9 %copy-start.28 = (f32[2,1152]{1,0:T(2,128)S(1)}, f32[2,1152]{1,0:T(2,128)}, u32[]{:S(2)}) copy-start(f32[2,1152]{1,0:T(2,128)} %copy-done.27) | copy-start | bytes 27652
  503.4 440.2 %reduce-scatter.10.cloned.1.call-start = ((), (), s32[]{:S(2)}) async-start(), calls=%async_computation.10 | async-start | bytes 8460288
  515.3 115.7 %copy-start.2 = (bf16[2,512,1152]{2,1,0:T(8,128)(2,1)S(1)}, bf16[2,512,1152]{2,1,0:T(8,128)(2,1)}, u32[]{:S(2)}) copy-start(bf16[2,512,1152]{2,1,0:T(8,128)(2,1)} %copy-done.1) | copy-start | bytes 7077892
  515.3 115.7 %copy-start.13 = (f32[2,1024]{1,0:T(2,128)S(1)}, f32[2,1024]{1,0:T(2,128)}, u32[]{:S(2)}) copy-start(f32[2,1024]{1,0:T(2,128)} %copy-done.12) | copy-start | bytes 24580
  515.3 115.7 %copy-start.15 = (f32[2,1152]{1,0:T(2,128)S(1)}, f32[2,1152]{1,0:T(2,128)}, u32[]{:S(2)}) copy-start(f32[2,1152]{1,0:T(2,128)} %copy-done.14) | copy-start | bytes 27652
  515.3 115.7 %copy-start.18 = (f32[2,1024]{1,0:T(2,128)S(1)}, f32[2,1024]{1,0:T(2,128)}, u32[]{:S(2)}) copy-start(f32[2,1024]{1,0:T(2,128)} %copy-done.17) | copy-start | bytes 24580
  515.3 115.7 %copy-start.26 = (f32[2,1152]{1,0:T(2,128)S(1)}, f32[2,1152]{1,0:T(2,128)}, u32[]{:S(2)}) copy-start(f32[2,1152]{1,0:T(2,128)} %copy-done.25) | copy-start | bytes 27652
  631.1 26.1 %copy-start.24 = (f32[2,1152]{1,0:T(2,128)S(1)}, f32[2,1152]{1,0:T(2,128)}, u32[]{:S(2)}) copy-start(f32[2,1152]{1,0:T(2,128)} %copy-done.23) | copy-start | bytes 27652
  657.1 289.0 %reduce-scatter.6.cloned.1.call-start = ((), (), s32[]{:S(2)}) async-start(), calls=%async_computation.7 | async-start | bytes 11280384 | tf_op jit(solution)/shard_map/reduce_scatter | solution.py:598
  689.6 324.9 %reduce-scatter.8.cloned.1.call-start = ((), (), s32[]{:S(2)}) async-start(), calls=%async_computation.8 | async-start | bytes 11280384 | tf_op jit(solution)/shard_map/reduce_scatter | solution.py:594
  725.5 29.3 %slice-start = ((s8[9437184]{0:T(1024)(128)(4,1)}), s8[4194304]{0:T(1024)(128)(4,1)S(1)}, s32[]{:S(2)}) async-start(s8[9437184]{0:T(1024)(128)(4,1)} %bitcast.108), calls=%async_computation.11 | async-start | bytes 8388608
  725.5 29.3 %slice-start.1 = ((s8[9437184]{0:T(1024)(128)(4,1)}), s8[4194304]{0:T(1024)(128)(4,1)S(1)}, s32[]{:S(2)}) async-start(s8[9437184]{0:T(1024)(128)(4,1)} %bitcast.108), calls=%async_computation.12 | async-start | bytes 8388608
  725.5 29.3 %slice-start.2 = ((s8[9437184]{0:T(1024)(128)(4,1)}), s8[1048576]{0:T(1024)(128)(4,1)S(1)}, s32[]{:S(2)}) async-start(s8[9437184]{0:T(1024)(128)(4,1)} %bitcast.108), calls=%async_computation.13 | async-start | bytes 2097152
  725.5 212.2 %collective-permute-start.9 = (bf16[2,512,1152]{2,1,0:T(8,128)(2,1)}, bf16[2,512,1152]{2,1,0:T(8,128)(2,1)}, u32[]{:S(2)}, u32[]{:S(2)}) collective-permute-start(bf16[2,512,1152]{2,1,0:T(8,128)(2,1)} %get-tuple-element.92), channel_id=1, source_target_pairs={{0,1},{1,0},{2,3},{3,2},{4,5},{5,4},{6,7},{7,6},{8,9},{9,8},{10,11... | collective-permute-start | bytes 7077896 | tf_op jit(solution)/shard_map/ppermute | solution.py:516
  762.5 3.1 copy-start.35
  762.6 4.9 copy-start.11
  762.6 4.9 copy-start.22
  762.6 5.0 copy-start.9
  762.6 5.0 copy-start.21
  765.2 11.5 %copy-start.19 = (f32[4608]{0:T(1024)S(1)}, f32[4608]{0:T(1024)}, u32[]{:S(2)}) copy-start(f32[4608]{0:T(1024)} %get-tuple-element.118) | copy-start | bytes 55300
  765.2 183.5 %collective-permute-start.11 = (bf16[2,512,1152]{2,1,0:T(8,128)(2,1)}, bf16[2,512,1152]{2,1,0:T(8,128)(2,1)}, u32[]{:S(2)}, u32[]{:S(2)}) collective-permute-start(bf16[2,512,1152]{2,1,0:T(8,128)(2,1)} %get-tuple-element.88), channel_id=1, source_target_pairs={{0,1},{1,0},{2,3},{3,2},{4,5},{5,4},{6,7},{7,6},{8,9},{9,8},{10,11... | collective-permute-start | bytes 7077896 | tf_op jit(solution)/shard_map/ppermute | solution.py:516
  765.8 63.8 %collective-permute-start.12 = (bf16[2,6,576]{2,0,1:T(2,128)(2,1)S(1)}, bf16[2,6,576]{2,0,1:T(2,128)(2,1)S(1)}, u32[]{:S(2)}, u32[]{:S(2)}) collective-permute-start(bf16[2,6,576]{2,0,1:T(2,128)(2,1)S(1)} %get-tuple-element.104), channel_id=1, source_target_pairs={{0,1},{1,0},{2,3},{3,2},{4,5},{5,4},{6,7},{7,6},{8,9},{9,8},{10,11... | collective-permute-start | bytes 41480 | tf_op jit(solution)/shard_map/ppermute | solution.py:516
  767.8 164.3 %copy-start.16 = (bf16[4,1152]{1,0:T(4,128)(2,1)S(1)}, bf16[4,1152]{1,0:T(4,128)(2,1)}, u32[]{:S(2)}) copy-start(bf16[4,1152]{1,0:T(4,128)(2,1)} %param.13) | copy-start | bytes 27652
  767.8 169.9 %copy-start.4 = (bf16[2,512,1152]{2,1,0:T(8,128)(2,1)S(1)}, bf16[2,512,1152]{2,1,0:T(8,128)(2,1)}, u32[]{:S(2)}) copy-start(bf16[2,512,1152]{2,1,0:T(8,128)(2,1)} %get-tuple-element.91) | copy-start | bytes 7077892
  776.7 83.6 %collective-permute-start.15 = (f32[4608]{0:T(1024)S(1)}, f32[4608]{0:T(1024)S(1)}, u32[]{:S(2)}, u32[]{:S(2)}) collective-permute-start(f32[4608]{0:T(1024)S(1)} %pad_maximum_fusion.3), channel_id=1, source_target_pairs={{0,1},{1,0},{2,3},{3,2},{4,5},{5,4},{6,7},{7,6},{8,9},{9,8},{10,11... | collective-permute-start | bytes 55304 | tf_op jit(solution)/shard_map/ppermute | solution.py:516
  858.8 60.8 %collective-permute-start.13 = (f32[64,72]{1,0:T(8,128)S(1)}, f32[64,72]{1,0:T(8,128)S(1)}, u32[]{:S(2)}, u32[]{:S(2)}) collective-permute-start(f32[64,72]{1,0:T(8,128)S(1)} %convolution_bitcast_fusion.4), channel_id=1, source_target_pairs={{0,1},{1,0},{2,3},{3,2},{4,5},{5,4},{6,7},{7,6},{8,9},{9,8},{10,11... | collective-permute-start | bytes 55304 | tf_op jit(solution)/shard_map/ppermute | solution.py:516
  920.2 10.1 all-to-all-start.1
  931.4 4.6 collective-permute-start.16
  945.4 11.6 %collective-permute-start.14 = (bf16[72,3,576]{2,1,0:T(4,128)(2,1)S(1)}, bf16[72,3,576]{2,1,0:T(4,128)(2,1)S(1)}, u32[]{:S(2)}, u32[]{:S(2)}) collective-permute-start(bf16[72,3,576]{2,1,0:T(4,128)(2,1)S(1)} %split.33), channel_id=1, source_target_pairs={{0,1},{1,0},{2,3},{3,2},{4,5},{5,4},{6,7},{7,6},{8,9},{9,8},{10,11... | collective-permute-start | bytes 746504 | tf_op jit(solution)/shard_map/ppermute | solution.py:516
  946.1 70.9 %copy-start.6 = (bf16[72,4608]{1,0:T(8,128)(2,1)S(1)}, bf16[72,4608]{1,0:T(8,128)(2,1)}, u32[]{:S(2)}) copy-start(bf16[72,4608]{1,0:T(8,128)(2,1)} %reduce-scatter.6.cloned.1.call-done) | copy-start | bytes 1990660
  947.2 69.8 %collective-permute-start.17 = (bf16[72,2304]{1,0:T(8,128)(2,1)S(1)}, bf16[72,2304]{1,0:T(8,128)(2,1)S(1)}, u32[]{:S(2)}, u32[]{:S(2)}) collective-permute-start(bf16[72,2304]{1,0:T(8,128)(2,1)S(1)} %split.35), channel_id=1, source_target_pairs={{0,1},{1,0},{2,3},{3,2},{4,5},{5,4},{6,7},{7,6},{8,9},{9,8},{10,11... | collective-permute-start | bytes 995336 | tf_op jit(solution)/shard_map/ppermute | solution.py:516
  1015.5 9.4 collective-permute-start.18
  (6 other events, 11.0 us)
Sparse Core Ops, SparseCore 0:
  19.1 92.7 all-gather.3
  113.5 122.5 all-gather.5
  503.5 102.0 all-reduce.3
  657.2 101.9 reduce-scatter.9
  763.7 126.1 reduce-scatter.5
  894.4 120.0 reduce-scatter.7

commit v2 on v1

--- a/solution.py
+++ b/solution.py
@@ -15,6 +15,7 @@
 f32 = jnp.float32
 bf16 = jnp.bfloat16
 NT = (((1,), (1,)), ((), ()))
+MESH = pl.DeviceIdType.MESH
 
 
 EPSILON = 1e-06
@@ -328,60 +329,91 @@
     return pl.multiple_of(start, 128), col - start
 
 
-def attn_fwd_kernel(q_ref, k_ref, v_ref, o_ref, lse_ref, vt_ref, ot_ref, *, blk):
+def head_members(heads, width):
+    col = lax.broadcasted_iota(jnp.int32, (heads, width), 1)
+    first = lax.broadcasted_iota(jnp.int32, (heads, width), 0) * HEAD_DIM
+    return jnp.where((col >= first) & (col < first + HEAD_DIM), 1.0, 0.0).astype(bf16)
+
+
+def attn_fwd_kernel(q_ref, k_ref, v_ref, o_ref, lse_ref, ot_ref, *, blk, heads):
     seq, width = q_ref.shape[1:]
-    heads = width // HEAD_DIM
     c = HEAD_DIM ** -0.5 * LOG2E
-    vt_ref[...] = v_ref[0].T
+    ot_ref[...] = v_ref[0].astype(f32).T
     lanes = lax.broadcasted_iota(jnp.int32, (blk, WINDOW), 1)
-
-    def pair(i, carry):
-        for odd in range(2):
-            head = 2 * i + odd
-            start, off = head_window(head * HEAD_DIM, width)
-            keys = k_ref[0, :, pl.ds(start, WINDOW)]
-            mask = (lanes >= off) & (lanes < off + HEAD_DIM)
-            row = pl.multiple_of(i * (2 * HEAD_DIM) + odd * 64, 16)
-            vt = vt_ref[pl.ds(row, 80), :]
-            for b in range(seq // blk):
+    ones = jnp.ones((8, seq), f32)
+    member = head_members(heads, width)
+    longest = [
+        jnp.max(
+            lax.dot_general(member, ref[0] * ref[0], NT, preferred_element_type=f32),
+            axis=1,
+            keepdims=True,
+        )
+        for ref in (q_ref, k_ref)
+    ]
+    small = jnp.max(longest[0] * longest[1]) * (1.1 * c * c) < 60.0 * 60.0
+
+    def run(shifted):
+        def pair(i, carry):
+            steps = [(2 * i + odd, b) for odd in range(2) for b in range(seq // blk)]
+
+            def scores(head, b):
+                start, off = head_window(head * HEAD_DIM, width)
+                mask = (lanes >= off) & (lanes < off + HEAD_DIM)
+                qb = q_ref[0, b * blk : (b + 1) * blk, pl.ds(start, WINDOW)]
+                qb = jnp.where(mask, qb, jnp.zeros_like(qb))
+                return lax.dot_general(
+                    k_ref[0, :, pl.ds(start, WINDOW)], qb, NT, preferred_element_type=f32
+                )
+
+            st = scores(*steps[0])
+            vt = None
+            for n, (head, b) in enumerate(steps):
+                after = scores(*steps[n + 1]) if n + 1 < len(steps) else None
+                mine = pl.ds(pl.multiple_of(head * HEAD_DIM, 8), HEAD_DIM)
+                if b == 0:
+                    vt = jnp.concatenate([ot_ref[mine, :], ones], axis=0).astype(bf16)
                 rows = slice(b * blk, (b + 1) * blk)
-                qb = q_ref[0, rows, pl.ds(start, WINDOW)]
-                qb = jnp.where(mask, qb, jnp.zeros_like(qb))
-                st = lax.dot_general(keys, qb, NT, preferred_element_type=f32)
-                m = jnp.max(st, axis=0, keepdims=True)
-                p = jnp.exp2((st - m) * c)
-                l = jnp.sum(p, axis=0, keepdims=True)
-                ot = jnp.dot(vt, p.astype(bf16), preferred_element_type=f32)
-                ot_ref[pl.ds(pl.multiple_of(head * HEAD_DIM, 8), HEAD_DIM), rows] = (
-                    ot[8 * odd : 8 * odd + HEAD_DIM] * (1.0 / l)
-                )
-                lse_ref[0, pl.ds(head, 1), rows] = m * c + jnp.log2(l)
-        return carry
-
-    lax.fori_loop(0, heads // 2, pair, 0)
+                if shifted:
+                    m = jnp.max(st, axis=0, keepdims=True)
+                    p = jnp.exp2((st - m) * c).astype(bf16)
+                else:
+                    p = jnp.exp2(st * c).astype(bf16)
+                ot = jnp.dot(vt, p, preferred_element_type=f32)
+                l = ot[HEAD_DIM : HEAD_DIM + 1]
+                ot_ref[mine, rows] = ot[:HEAD_DIM] * (1.0 / l)
+                lse_ref[0, 0, pl.ds(head, 1), rows] = jnp.log2(l) + m * c if shifted else jnp.log2(l)
+                st = after
+            return carry
+
+        lax.fori_loop(0, heads // 2, pair, 0)
+
+    pl.when(small)(lambda: run(False))
+    pl.when(jnp.logical_not(small))(lambda: run(True))
     o_ref[0] = ot_ref[...].T.astype(bf16)
 
 
-def attn_fwd(qkv, width, blk=256):
-    n, seq, _ = qkv.shape
-    spec = lambda j: pl.BlockSpec((1, seq, width), lambda b: (b, 0, j))
-    heads = width // HEAD_DIM
+def attn_fwd(qkv, heads, blk=256):
+    n, seq, wide = qkv.shape
+    width = wide // 6
+    spec = lambda j: pl.BlockSpec((1, seq, width), lambda b, h: (b, 0, 3 * h + j))
     return pl.pallas_call(
-        partial(attn_fwd_kernel, blk=blk),
-        grid=(n,),
+        partial(attn_fwd_kernel, blk=blk, heads=heads),
+        grid=(n, 2),
         in_specs=[spec(0), spec(1), spec(2)],
         out_specs=[
-            pl.BlockSpec((1, seq, width), lambda b: (b, 0, 0)),
-            pl.BlockSpec((1, heads, seq), lambda b: (b, 0, 0)),
+            pl.BlockSpec((1, seq, width), lambda b, h: (b, 0, h)),
+            pl.BlockSpec((1, 1, heads, seq), lambda b, h: (b, h, 0, 0)),
         ],
         out_shape=[
-            jax.ShapeDtypeStruct((n, seq, width), bf16),
-            jax.ShapeDtypeStruct((n, heads, seq), f32),
+            jax.ShapeDtypeStruct((n, seq, 2 * width), bf16),
+            jax.ShapeDtypeStruct((n, 2, heads, seq), f32),
         ],
-        scratch_shapes=[pltpu.VMEM((width, seq), bf16), pltpu.VMEM((width, seq), f32)],
+        scratch_shapes=[pltpu.VMEM((width, seq), f32)],
         compiler_params=pltpu.CompilerParams(vmem_limit_bytes=56 << 20),
         cost_estimate=pl.CostEstimate(
-            flops=4 * n * seq * seq * width, bytes_accessed=8 * n * seq * width, transcendentals=n * heads * seq * seq
+            flops=8 * n * seq * seq * width,
+            bytes_accessed=16 * n * seq * width,
+            transcendentals=2 * n * heads * seq * seq,
         ),
         name="attention_forward",
     )(qkv, qkv, qkv)
@@ -389,85 +421,432 @@
 
 def attn_bwd_kernel(
     q_ref, k_ref, v_ref, do_ref, o_ref, lse_ref, dqkv_ref,
-    kt_ref, dqt_ref, delta_ref, pt_ref, dst_ref, *, blk
+    dqt_ref, delta_ref, pt_ref, dst_ref, *, blk, heads
 ):
     seq, width = q_ref.shape[1:]
-    heads = width // HEAD_DIM
     scale = HEAD_DIM ** -0.5
     c = scale * LOG2E
-    kt_ref[...] = k_ref[0].T
+    dqt_ref[...] = k_ref[0].astype(f32).T
     prod = do_ref[0].astype(f32) * o_ref[0].astype(f32)
     high = prod.astype(bf16)
     low = (prod - high.astype(f32)).astype(bf16)
-    col = lax.broadcasted_iota(jnp.int32, (heads, width), 1)
-    first = lax.broadcasted_iota(jnp.int32, (heads, width), 0) * HEAD_DIM
-    member = jnp.where((col >= first) & (col < first + HEAD_DIM), 1.0, 0.0).astype(bf16)
+    member = head_members(heads, width)
     delta_ref[...] = lax.dot_general(member, high, NT, preferred_element_type=f32) + lax.dot_general(
         member, low, NT, preferred_element_type=f32
     )
     lanes = lax.broadcasted_iota(jnp.int32, (seq, WINDOW), 1)
-
-    def pair(i, carry):
-        for odd in range(2):
-            head = 2 * i + odd
-            start, off = head_window(head * HEAD_DIM, width)
-            window = pl.ds(start, WINDOW)
-            mask = (lanes >= off) & (lanes < off + HEAD_DIM)
-            keys = k_ref[0, :, window]
-            values = v_ref[0, :, window]
-            qm = q_ref[0, :, window]
-            qm = jnp.where(mask, qm, jnp.zeros_like(qm))
-            dom = do_ref[0, :, window]
-            dom = jnp.where(mask, dom, jnp.zeros_like(dom))
-            row = pl.multiple_of(i * (2 * HEAD_DIM) + odd * 64, 16)
-            kt = kt_ref[pl.ds(row, 80), :]
-            for b in range(seq // blk):
-                rows = slice(b * blk, (b + 1) * blk)
-                st = lax.dot_general(keys, qm[rows], NT, preferred_element_type=f32)
-                dpt = lax.dot_general(values, dom[rows], NT, preferred_element_type=f32)
-                p = jnp.exp2(st * c - lse_ref[0, pl.ds(head, 1), rows])
-                dst = (p * (dpt - delta_ref[pl.ds(head, 1), rows])).astype(bf16)
-                pt_ref[:, rows] = p.astype(bf16)
-                dst_ref[:, rows] = dst
-                dqt = jnp.dot(kt, dst, preferred_element_type=f32)
-                dqt_ref[pl.ds(pl.multiple_of(head * HEAD_DIM, 8), HEAD_DIM), rows] = (
-                    dqt[8 * odd : 8 * odd + HEAD_DIM] * scale
-                )
-            dk = jnp.dot(dst_ref[...], qm, preferred_element_type=f32) * scale
-            dv = jnp.dot(pt_ref[...], dom, preferred_element_type=f32)
-            kwin = pl.ds(pl.multiple_of(width + start, 128), WINDOW)
-            vwin = pl.ds(pl.multiple_of(2 * width + start, 128), WINDOW)
-            dqkv_ref[0, :, kwin] = jnp.where(mask, dk.astype(bf16), dqkv_ref[0, :, kwin])
-            dqkv_ref[0, :, vwin] = jnp.where(mask, dv.astype(bf16), dqkv_ref[0, :, vwin])
+    edge = heads * HEAD_DIM // 128 * 128
+    for part in (1, 2):
+        dqkv_ref[0, :, part * width + edge : (part + 1) * width] = jnp.zeros((seq, width - edge), bf16)
+
+    def one(head, carry):
+        start, off = head_window(head * HEAD_DIM, width)
+        window = pl.ds(start, WINDOW)
+        mask = (lanes >= off) & (lanes < off + HEAD_DIM)
+        keys = k_ref[0, :, window]
+        values = v_ref[0, :, window]
+        qm = q_ref[0, :, window]
+        qm = jnp.where(mask, qm, jnp.zeros_like(qm))
+        dom = do_ref[0, :, window]
+        dom = jnp.where(mask, dom, jnp.zeros_like(dom))
+        mine = pl.ds(pl.multiple_of(head * HEAD_DIM, 8), HEAD_DIM)
+        kt = dqt_ref[mine, :].astype(bf16)
+        for b in range(seq // blk):
+            rows = slice(b * blk, (b + 1) * blk)
+            st = lax.dot_general(keys, qm[rows], NT, preferred_element_type=f32)
+            dpt = lax.dot_general(values, dom[rows], NT, preferred_element_type=f32)
+            p = jnp.exp2(st * c - lse_ref[0, 0, pl.ds(head, 1), rows])
+            dst = (p * (dpt - delta_ref[pl.ds(head, 1), rows])).astype(bf16)
+            pt_ref[:, rows] = p.astype(bf16)
+            dst_ref[:, rows] = dst
+            dqt_ref[mine, rows] = jnp.dot(kt, dst, preferred_element_type=f32) * scale
+        dk = jnp.dot(dst_ref[...], qm, preferred_element_type=f32) * scale
+        dv = jnp.dot(pt_ref[...], dom, preferred_element_type=f32)
+        kwin = pl.ds(pl.multiple_of(width + start, 128), WINDOW)
+        vwin = pl.ds(pl.multiple_of(2 * width + start, 128), WINDOW)
+        dqkv_ref[0, :, kwin] = jnp.where(mask, dk.astype(bf16), dqkv_ref[0, :, kwin])
+        dqkv_ref[0, :, vwin] = jnp.where(mask, dv.astype(bf16), dqkv_ref[0, :, vwin])
         return carry
 
-    lax.fori_loop(0, heads // 2, pair, 0)
+    lax.fori_loop(0, heads, one, 0)
     dqkv_ref[0, :, :width] = dqt_ref[...].T.astype(bf16)
 
 
-def attn_bwd(qkv, grad, mixed, lse, width, blk=256):
-    n, seq, _ = qkv.shape
-    spec = lambda j: pl.BlockSpec((1, seq, width), lambda b: (b, 0, j))
-    heads = width // HEAD_DIM
+def attn_bwd(qkv, grad, mixed, lse, heads, blk=256):
+    n, seq, wide = qkv.shape
+    width = wide // 6
+    spec = lambda j: pl.BlockSpec((1, seq, width), lambda b, h: (b, 0, 3 * h + j))
+    out = pl.BlockSpec((1, seq, width), lambda b, h: (b, 0, h))
     return pl.pallas_call(
-        partial(attn_bwd_kernel, blk=blk),
-        grid=(n,),
-        in_specs=[spec(0), spec(1), spec(2), spec(0), spec(0), pl.BlockSpec((1, heads, seq), lambda b: (b, 0, 0))],
-        out_specs=pl.BlockSpec((1, seq, 3 * width), lambda b: (b, 0, 0)),
-        out_shape=jax.ShapeDtypeStruct((n, seq, 3 * width), bf16),
+        partial(attn_bwd_kernel, blk=blk, heads=heads),
+        grid=(n, 2),
+        in_specs=[
+            spec(0), spec(1), spec(2), out, out,
+            pl.BlockSpec((1, 1, heads, seq), lambda b, h: (b, h, 0, 0)),
+        ],
+        out_specs=pl.BlockSpec((1, seq, 3 * width), lambda b, h: (b, 0, h)),
+        out_shape=jax.ShapeDtypeStruct(qkv.shape, bf16),
         scratch_shapes=[
-            pltpu.VMEM((width, seq), bf16),
             pltpu.VMEM((width, seq), f32),
             pltpu.VMEM((heads, seq), f32),
             pltpu.VMEM((seq, seq), bf16),
             pltpu.VMEM((seq, seq), bf16),
         ],
-        compiler_params=pltpu.CompilerParams(vmem_limit_bytes=60 << 20),
+        compiler_params=pltpu.CompilerParams(vmem_limit_bytes=56 << 20),
         cost_estimate=pl.CostEstimate(
-            flops=10 * n * seq * seq * width, bytes_accessed=16 * n * seq * width, transcendentals=n * heads * seq * seq
+            flops=20 * n * seq * seq * width,
+            bytes_accessed=32 * n * seq * width,
+            transcendentals=2 * n * heads * seq * seq,
         ),
         name="attention_backward",
     )(qkv, qkv, qkv, grad, mixed, lse)
+
+
+CORES = 2
+ROWS = 2
+
+
+def place(rank):
+    return rank // (ROWS * CORES), rank // CORES % ROWS, rank % CORES
+
+
+def rank_of(z, y, core):
+    return (z * ROWS + y) * CORES + core
+
+
+def greet(side):
+    rank = lax.axis_index("dp")
+    groups = lax.axis_size("dp")
+    barrier = pltpu.get_barrier_semaphore()
+    for step in range(1, groups):
+        pl.semaphore_signal(barrier, inc=1, device_id={"dp": lax.rem(rank + step, groups)}, device_id_type=MESH)
+    pl.semaphore_signal(barrier, inc=1, device_id={"tensor": 1 - side}, device_id_type=MESH)
+    pl.semaphore_wait(barrier, groups)
+
+
+class Spread:
+    def __init__(self, source, out, sends, arrivals, lanes=None):
+        self.source, self.out, self.sends, self.arrivals = source, out, sends, arrivals
+        self.lanes = lanes
+        self.rank = lax.axis_index("dp")
+        self.z, self.y, self.core = place(self.rank)
+        self.depth = lax.axis_size("dp") // (ROWS * CORES)
+        self.started = []
+
+    def block(self, origin):
+        return self.out.at[origin] if self.lanes is None else self.out.at[origin, :, self.lanes]
+
+    def copy(self, origin, edge, target, source=None):
+        return pltpu.make_async_remote_copy(
+            src_ref=self.block(origin) if source is None else source,
+            dst_ref=self.block(origin),
+            send_sem=self.sends.at[origin, edge],
+            recv_sem=self.arrivals.at[origin],
+            device_id={"dp": target},
+            device_id_type=MESH,
+        )
+
+    def send(self, origin, edge, target, source=None, when=None):
+        sent = self.copy(origin, edge, target, source)
+        if when is None:
+            sent.start()
+        else:
+            pl.when(when)(sent.start)
+        self.started.append((sent, when))
+
+    def arrive(self, origin):
+        self.copy(origin, 0, rank_of(self.z, 1 - self.y, self.core)).wait_recv()
+
+    def up(self):
+        return rank_of(self.z + 1, self.y, self.core)
+
+    def down(self):
+        return rank_of(self.z - 1, self.y, self.core)
+
+    def across(self):
+        return rank_of(self.z, 1 - self.y, self.core)
+
+    def sibling(self):
+        return rank_of(self.z, self.y, 1 - self.core)
+
+    def begin(self):
+        rank, source = self.rank, self.source
+        self.send(rank, 0, self.up(), source, self.z < self.depth - 1)
+        self.send(rank, 3, self.down(), source, self.z > 0)
+        self.send(rank, 1, self.across(), source)
+        self.send(rank, 2, self.sibling(), source)
+
+    def relay(self, hop):
+        for toward, there in ((1, self.z >= hop), (-1, self.z + hop < self.depth)):
+            origin = rank_of(self.z - toward * hop, self.y, self.core)
+            further = (self.z < self.depth - 1) if toward > 0 else (self.z > 0)
+            pl.when(there)(lambda: self.arrive(origin))
+            self.send(
+                origin, 0, self.up() if toward > 0 else self.down(), when=there & further
+            )
+            self.send(origin, 1, self.across(), when=there)
+            self.send(origin, 2, self.sibling(), when=there)
+
+    def relay_across(self, hop):
+        for toward, there in ((1, self.z >= hop), (-1, self.z + hop < self.depth)):
+            if hop == 0 and toward < 0:
+                continue
+            origin = rank_of(self.z - toward * hop, 1 - self.y, self.core)
+            pl.when(there)(lambda: self.arrive(origin))
+            self.send(origin, 2, self.sibling(), when=there)
+
+    def finish(self):
+        for z in range(self.depth):
+            for y in range(ROWS):
+                self.arrive(rank_of(z, y, 1 - self.core))
+        for sent, when in self.started:
+            if when is None:
+                sent.wait_send()
+            else:
+                pl.when(when)(sent.wait_send)
+
+
+def run_spreads(spreads):
+    depth = spreads[0].depth
+    for hop in range(1, depth):
+        for s in spreads:
+            s.relay(hop)
+        for s in spreads:
+            s.relay_across(hop - 1)
+    for s in spreads:
+        s.relay_across(depth - 1)
+    for s in spreads:
+        s.finish()
+
+
+class Exchange:
+    def __init__(self, source, out, sends, arrivals):
+        self.source, self.out, self.sends, self.arrivals = source, out, sends, arrivals
+        self.rank = lax.axis_index("dp")
+        self.groups = lax.axis_size("dp")
+
+    def copy(self, step):
+        peer = lax.rem(self.rank + step, self.groups)
+        return pltpu.make_async_remote_copy(
+            src_ref=self.source.at[peer],
+            dst_ref=self.out.at[self.rank],
+            send_sem=self.sends.at[step],
+            recv_sem=self.arrivals.at[self.rank],
+            device_id={"dp": peer},
+            device_id_type=MESH,
+        )
+
+    def begin(self):
+        self.out[self.rank] = self.source[self.rank]
+        for step in range(1, self.groups):
+            self.copy(step).start()
+
+    def finish(self):
+        for step in range(1, self.groups):
+            peer = lax.rem(self.rank + step, self.groups)
+            pltpu.make_async_remote_copy(
+                src_ref=self.source.at[peer],
+                dst_ref=self.out.at[peer],
+                send_sem=self.sends.at[step],
+                recv_sem=self.arrivals.at[peer],
+                device_id={"dp": peer},
+                device_id_type=MESH,
+            ).wait_recv()
+
+    def drain(self):
+        for step in range(1, self.groups):
+            self.copy(step).wait_send()
+
+
+def to_partner(source, target, side, sends, arrivals, k):
+    return pltpu.make_async_remote_copy(
+        src_ref=source,
+        dst_ref=target,
+        send_sem=sends.at[k],
+        recv_sem=arrivals.at[k],
+        device_id={"tensor": 1 - side},
+        device_id_type=MESH,
+    )
+
+
+def opening_kernel(
+    cond_ref, mod_w_ref, mod_bias_ref, head_ref, rest_ref, latent_ref,
+    head_out, rest_out, latent_out, mod_out, cond_out,
+    part_ref, mod_in,
+    x_send, x_recv, c_send, c_recv, m_send, m_recv, h_send, h_recv, local_sem,
+):
+    side = lax.axis_index("tensor")
+    rank = lax.axis_index("dp")
+    own = latent_out.shape[0]
+    greet(side)
+    conds = Exchange(cond_ref, cond_out, c_send, c_recv)
+    conds.begin()
+    lanes = head_ref.shape[1]
+    mine = Spread(head_ref, head_out, h_send.at[0], h_recv.at[0], pl.ds(0, lanes))
+    other = Spread(None, head_out, h_send.at[1], h_recv.at[1], pl.ds(lanes, lanes))
+    head_swap = to_partner(head_ref, other.block(rank), side, x_send, x_recv, 0)
+    head_swap.start()
+    mine.begin()
+    latents = to_partner(
+        latent_ref.at[pl.ds((1 - side) * own, own)], latent_out, side, x_send, x_recv, 1
+    )
+    latents.start()
+    rest = to_partner(rest_ref, rest_out, side, x_send, x_recv, 3)
+    rest.start()
+    keep = pltpu.make_async_copy(head_ref, mine.block(rank), local_sem)
+    keep.start()
+    conds.finish()
+    groups, rows, lanes = cond_out.shape
+    half = mod_bias_ref.shape[1]
+    low = cond_out[...].reshape(groups * rows, lanes).astype(bf16)
+    front = lax.broadcasted_iota(jnp.int32, (groups * rows, half), 0) % rows < rows // 2
+    part_ref[...] = jnp.where(
+        front,
+        jnp.dot(low, mod_w_ref[0], preferred_element_type=f32),
+        jnp.dot(low, mod_w_ref[1], preferred_element_type=f32),
+    ).reshape(groups, rows, half)
+    mods = Exchange(part_ref, mod_in, m_send, m_recv)
+    mods.begin()
+    head_swap.wait_recv()
+    other.begin()
+    mine.relay(1)
+    mods.finish()
+    mod_out[0] = jnp.sum(mod_in[...], axis=0) + mod_bias_ref[...]
+    mod_swap = to_partner(mod_out.at[0], mod_out.at[1], side, x_send, x_recv, 2)
+    mod_swap.start()
+    other.relay(1)
+    mine.relay_across(0)
+    other.relay_across(0)
+    depth = mine.depth
+    for hop in range(2, depth):
+        for s in (mine, other):
+            s.relay(hop)
+            s.relay_across(hop - 1)
+    for s in (mine, other):
+        s.relay_across(depth - 1)
+    keep.wait()
+    mine.finish()
+    other.finish()
+    mod_swap.wait()
+    latents.wait()
+    rest.wait()
+    head_swap.wait_send()
+    conds.drain()
+    mods.drain()
+
+
+def opening(cond_low, mod_weight, mod_bias, head, rest, latent):
+    groups = lax.axis_size("dp")
+    count, half_seq, width = latent.shape
+    depth = cond_low.shape[1] // groups
+    half = mod_weight.shape[1] * mod_weight.shape[2] // 2
+    blocks = cond_low.astype(f32).reshape(count, groups, depth).transpose(1, 0, 2)
+    blocks = jnp.concatenate([blocks, blocks], axis=1)
+    blocks = jnp.pad(blocks, ((0, 0), (0, 0), (0, 128 - depth)))
+    weights = jnp.pad(mod_weight.reshape(depth, 2, half), ((0, 128 - depth), (0, 0), (0, 0))).transpose(1, 0, 2)
+    bias = jnp.repeat(mod_bias.astype(f32).reshape(2, half), count, axis=0)
+    dma = pltpu.SemaphoreType.DMA
+    vmem = pl.BlockSpec(memory_space=pltpu.VMEM)
+    anywhere = pl.BlockSpec(memory_space=pl.ANY)
+    return pl.pallas_call(
+        opening_kernel,
+        in_specs=[vmem, vmem, vmem, anywhere, anywhere, anywhere],
+        out_specs=[anywhere, anywhere, anywhere, vmem, vmem],
+        out_shape=[
+            jax.ShapeDtypeStruct((groups, depth, 2 * head.shape[1]), bf16),
+            jax.ShapeDtypeStruct(rest.shape, bf16),
+            jax.ShapeDtypeStruct((count // 2, half_seq, width), bf16),
+            jax.ShapeDtypeStruct((2, 2 * count, half), f32),
+            jax.ShapeDtypeStruct(blocks.shape, f32),
+        ],
+        scratch_shapes=[
+            pltpu.VMEM((groups, 2 * count, half), f32),
+            pltpu.VMEM((groups, 2 * count, half), f32),
+            dma((4,)), dma((4,)),
+            dma((groups,)), dma((groups,)),
+            dma((groups,)), dma((groups,)),
+            dma((2, groups, 4)), dma((2, groups)),
+            dma,
+        ],
+        compiler_params=pltpu.CompilerParams(collective_id=0, has_side_effects=True, vmem_limit_bytes=32 << 20),
+        name="opening",
+    )(blocks, weights, bias, head, rest, latent)
+
+
+def closing_kernel(
+    mod_ref, bias_ref, mod_w_ref,
+    mod_out, bias_out, cond_out,
+    mod_unit, bias_unit, bias_in, part_ref, cond_in,
+    x_send, x_recv, m_send, m_recv, b_send, b_recv, c_send, c_recv,
+):
+    side = lax.axis_index("tensor")
+    rank = lax.axis_index("dp")
+    greet(side)
+    rows = mod_ref.shape[1]
+    mod_swap = to_partner(mod_ref.at[1], mod_unit.at[1], side, x_send, x_recv, 0)
+    mod_swap.start()
+    bias_swap = to_partner(bias_ref.at[1], bias_unit.at[1], side, x_send, x_recv, 1)
+    bias_swap.start()
+    mod_swap.wait()
+    bias_swap.wait()
+    mod_out[rank] = mod_ref[0] + mod_unit[1]
+    bias_in[rank] = bias_ref[0] + bias_unit[1]
+    mods = Spread(None, mod_out, m_send, m_recv)
+    biases = Spread(None, bias_in, b_send, b_recv)
+    mods.begin()
+    biases.begin()
+    run_spreads([mods, biases])
+    bias_out[...] = jnp.sum(bias_in[...], axis=0)
+    groups, rows, half = mod_out.shape
+    low = mod_out[...].reshape(groups * rows, half).astype(bf16)
+    lanes = mod_w_ref.shape[1]
+    front = lax.broadcasted_iota(jnp.int32, (groups * rows, lanes), 0) % rows < rows // 2
+    part_ref[...] = jnp.where(
+        front,
+        lax.dot_general(low, mod_w_ref[0], NT, preferred_element_type=f32),
+        lax.dot_general(low, mod_w_ref[1], NT, preferred_element_type=f32),
+    ).reshape(groups, rows, lanes)
+    conds = Exchange(part_ref, cond_in, c_send, c_recv)
+    conds.begin()
+    conds.finish()
+    cond_out[0] = cond_in[...]
+    cond_swap = to_partner(cond_out.at[0], cond_out.at[1], side, x_send, x_recv, 2)
+    cond_swap.start()
+    cond_swap.wait()
+    conds.drain()
+
+
+def closing(mod_pair, bias_pair, mod_weight):
+    groups = lax.axis_size("dp")
+    rows, half = mod_pair.shape[1:]
+    depth = mod_weight.shape[0]
+    weights = jnp.pad(mod_weight.reshape(depth, 2, half), ((0, 128 - depth), (0, 0), (0, 0))).transpose(1, 0, 2)
+    dma = pltpu.SemaphoreType.DMA
+    vmem = pl.BlockSpec(memory_space=pltpu.VMEM)
+    lines = bias_pair.shape[1]
+    return pl.pallas_call(
+        closing_kernel,
+        in_specs=[vmem, vmem, vmem],
+        out_specs=[vmem, vmem, vmem],
+        out_shape=[
+            jax.ShapeDtypeStruct((groups, rows, half), f32),
+            jax.ShapeDtypeStruct((lines, 128), f32),
+            jax.ShapeDtypeStruct((2, groups, rows, 128), f32),
+        ],
+        scratch_shapes=[
+            pltpu.VMEM((2, rows, half), f32),
+            pltpu.VMEM((2, lines, 128), f32),
+            pltpu.VMEM((groups, lines, 128), f32),
+            pltpu.VMEM((groups, rows, 128), f32),
+            pltpu.VMEM((groups, rows, 128), f32),
+            dma((3,)), dma((3,)),
+            dma((groups, 4)), dma((groups,)),
+            dma((groups, 4)), dma((groups,)),
+            dma((groups,)), dma((groups,)),
+        ],
+        compiler_params=pltpu.CompilerParams(collective_id=1, has_side_effects=True, vmem_limit_bytes=32 << 20),
+        name="closing",
+    )(mod_pair, bias_pair, weights)
 
 
 def normed(values):
@@ -539,43 +918,46 @@
 
     cond_f = condition.astype(f32)
     cond_low = jax.nn.silu(cond_f).astype(bf16)
-    cond_all = lax.all_gather(cond_low, "dp", axis=0, tiled=True)
-    cond_cols = lax.dynamic_slice_in_dim(cond_all, rank * depth, depth, 1)
-    partial_mod = mm("bd,dkc->bkc", cond_cols, mod_weight)
-    arrived = lax.all_to_all(partial_mod, "dp", split_axis=0, concat_axis=0, tiled=True)
-    mod_cols = jnp.sum(arrived.reshape(groups, count, 6, cols), axis=0) + mod_bias.astype(f32)
-    modulation = in_order(own_latents(mod_cols), swap(other_latents(mod_cols)), 2)
+    heads = cols // HEAD_DIM
+    room = -(-cols // 128) * 128
+
+    def roomy(a):
+        return jnp.pad(a, [(0, 0)] * (a.ndim - 1) + [(0, room - cols)])
+
+    head_shard = roomy(head_weight).reshape(depth, 3 * room)
+    shards = jnp.concatenate([roomy(mix_weight.T), up_weight, down_weight.T], axis=1)
+    head_all, shards_in, latent_in, mod_parts, cond_blocks = opening(
+        cond_low, mod_weight, mod_bias, head_shard, shards, latent
+    )
+    head_all = head_all.reshape(width, 6 * room)
+    mod_parts = mod_parts.reshape(2, 2, count, 3, cols)
+    mod_parts = own_latents(mod_parts, 2).transpose(0, 2, 1, 3, 4).reshape(2, own, 6, cols)
+    modulation = in_order(mod_parts[0], mod_parts[1], 2)
+    cond_cols = cond_blocks[:, :count, :depth].reshape(groups * count, depth).astype(bf16)
     branch = branch_bias.astype(f32)
     branch_all = in_order(branch, swap(branch), 1)
     row = lambda k: modulation[:, k][:, None, :]
     shift_a, scale_a, gate_a, shift_m, scale_m, gate_m = [row(k) for k in range(6)]
 
-    head_all = lax.all_gather(
-        with_other(head_weight, 2).reshape(depth, 3 * width), "dp", axis=0, tiled=True
-    )
-    rest_all = lax.all_gather(
-        jnp.concatenate(
-            [with_other(mix_weight.T, 1), with_other(up_weight, 1), with_other(down_weight.T, 1)],
-            axis=1,
-        ),
-        "dp",
-        axis=0,
-        tiled=True,
-    )
-    mix_t = rest_all[:, :width]
-    up_all = rest_all[:, width : width + hidden]
-    down_t = rest_all[:, width + hidden :]
-    head_bias_f = with_other(head_bias.astype(f32), 1)
+    cuts = (0, room, room + hidden // 2, room + hidden)
+    pieces = [a[:, lo:hi] for lo, hi in zip(cuts, cuts[1:]) for a in (shards, shards_in)]
+    rest_all = lax.all_gather(jnp.concatenate(pieces, axis=1), "dp", axis=0, tiled=True)
+    mix_t = rest_all[:, : 2 * room]
+    up_all = rest_all[:, 2 * room : 2 * room + hidden]
+    down_t = rest_all[:, 2 * room + hidden :]
     up_bias_f = with_other(up_bias.astype(f32), 0)
 
-    lat = take(latent)
-    upstream_low = take(cotangent)
+    lat = jnp.concatenate([own_latents(latent), latent_in], axis=1)
+    later, _ = lax.optimization_barrier((other_latents(cotangent), latent_in))
+    upstream_low = jnp.concatenate([own_latents(cotangent), swap(later)], axis=1)
     lat_f = lat.astype(f32)
     norm1, inv1 = normed(lat_f)
     attn_in = (norm1 * (1.0 + scale_a) + shift_a).astype(bf16)
-    qkv_bias = jnp.concatenate([head_bias_f[0], jnp.zeros((width,), f32), head_bias_f[1]])
+    head_bias_f = roomy(head_bias.astype(f32))
+    empty = jnp.zeros((room,), f32)
+    qkv_bias = with_other(jnp.concatenate([head_bias_f[0], empty, head_bias_f[1]]), 0)
     qkv = (mm("bsd,dc->bsc", attn_in, head_all) + qkv_bias).astype(bf16)
-    mixed, logsum = attn_fwd(qkv, width)
+    mixed, logsum = attn_fwd(qkv, heads)
     attn_out = mm("bsc,dc->bsd", mixed, mix_t) + branch_all[0]
     first = lat_f + gate_a * attn_out
     norm2, inv2 = normed(first)
@@ -591,10 +973,12 @@
     tail_bias_grad = jnp.sum(gate_m[:, 0] * jnp.sum(upstream, axis=1), axis=0)
     mlp_grad = (gate_m * upstream).astype(bf16)
     down_grad = mm("bsd,bsf->df", mlp_grad, act).astype(bf16)
+    down_grad, mlp_grad = lax.optimization_barrier((down_grad, mlp_grad))
     down_sum = lax.psum_scatter(down_grad, "dp", scatter_dimension=0, tiled=True)
     pre_grad = gelu_back(mm("bsd,df->bsf", mlp_grad, down_t))[0].astype(bf16)
     up_bias_term = jnp.sum(pre_grad, axis=(0, 1), dtype=f32)
     up_grad = mm("bsd,bsf->df", mlp_in, pre_grad).astype(bf16)
+    up_grad, pre_grad = lax.optimization_barrier((up_grad, pre_grad))
     up_sum = lax.psum_scatter(up_grad, "dp", scatter_dimension=0, tiled=True)
     mlp_in_grad = mm("bsf,df->bsd", pre_grad, up_all)
     shift_m_grad = jnp.sum(mlp_in_grad, axis=1)
@@ -605,9 +989,11 @@
     attn_grad = (gate_a * first_grad).astype(bf16)
     mixed_grad = mm("bsd,dc->bsc", attn_grad, mix_t).astype(bf16)
     mix_grad = mm("bsd,bsc->dc", attn_grad, mixed).astype(bf16)
+    mix_grad, mixed_grad = lax.optimization_barrier((mix_grad, mixed_grad))
     mix_sum = lax.psum_scatter(mix_grad, "dp", scatter_dimension=0, tiled=True)
-    qkv_grad = attn_bwd(qkv, mixed_grad, mixed, logsum, width)
+    qkv_grad = attn_bwd(qkv, mixed_grad, mixed, logsum, heads)
     head_grad = mm("bsd,bsc->dc", attn_in, qkv_grad).astype(bf16)
+    head_grad, qkv_grad = lax.optimization_barrier((head_grad, qkv_grad))
     head_sum = lax.psum_scatter(head_grad, "dp", scatter_dimension=0, tiled=True)
     qkv_bias_term = jnp.sum(qkv_grad, axis=(0, 1), dtype=f32)
     attn_in_grad = mm("bsc,dc->bsd", qkv_grad, head_all)
@@ -619,16 +1005,33 @@
     mod_low = jnp.stack(
         [shift_a_grad, scale_a_grad, gate_a_grad, shift_m_grad, scale_m_grad, gate_m_grad], axis=1
     ).astype(bf16)
-    my_cols = lax.dynamic_slice_in_dim(mod_low, side * cols, cols, 2)
-    other_cols = lax.dynamic_slice_in_dim(mod_low, (1 - side) * cols, cols, 2)
-    mod_rows = lax.all_gather(
-        in_order(my_cols, swap(other_cols), 0), "dp", axis=0, tiled=True
-    )
+    branch_term = jnp.stack([attn_bias_grad, tail_bias_grad])
+    head_term = qkv_bias_term.reshape(2, 3, room)[:, 0::2, :cols]
+    ups = up_bias_term.reshape(2, hidden // 2)
+
+    def mod_share(owner):
+        mine = lax.dynamic_slice_in_dim(mod_low.astype(f32), owner * cols, cols, 2)
+        mine = mine.reshape(own, 2, 3 * cols).transpose(1, 0, 2)
+        empty = jnp.zeros((2, count, 3 * cols), f32)
+        return lax.dynamic_update_slice_in_dim(empty, mine, side * own, 1).reshape(2 * count, 3 * cols)
+
+    def bias_share(owner, k):
+        branch_cols = lax.dynamic_slice_in_dim(branch_term, owner * cols, cols, 1)
+        flat = jnp.concatenate([head_term[k].reshape(-1), branch_cols.reshape(-1), ups[k]])
+        return flat.reshape(-1, 128)
+
+    mod_blocks, biases, cond_parts = closing(
+        jnp.stack([mod_share(side), mod_share(1 - side)]),
+        jnp.stack([bias_share(side, 0), bias_share(1 - side, 1)]),
+        mod_weight,
+    )
+    biases = biases.reshape(-1)
+    mod_rows = mod_blocks.astype(bf16).reshape(groups, 2, count, 3, cols)
+    mod_rows = mod_rows.transpose(0, 2, 1, 3, 4).reshape(groups * count, 6, cols)
     mod_weight_grad = mm("bd,bkc->dkc", cond_cols, mod_rows)
     mod_bias_grad = jnp.sum(mod_rows, axis=0, dtype=f32)
-    cond_act = mm("bkc,dkc->bd", mod_rows, mod_weight)
-    cond_act = cond_act + swap(cond_act)
-    cond_act = lax.all_to_all(cond_act, "dp", split_axis=0, concat_axis=1, tiled=True)
+    cond_act = jnp.sum(cond_parts[..., :depth].reshape(2, groups, 2, count, depth), axis=(0, 2))
+    cond_act = cond_act.transpose(1, 0, 2).reshape(count, groups * depth)
     gate = jax.nn.sigmoid(cond_f)
     condition_grad = cond_act * (gate * (1.0 + cond_f * (1.0 - gate)))
 
@@ -636,26 +1039,10 @@
         mine, other = jnp.split(summed, 2, axis=axis)
         return mine.astype(f32) + swap(other).astype(f32)
 
-    head_weight_grad = joined(head_sum.reshape(depth, 3, width), 2)
-    mix_weight_grad = joined(mix_sum, 1).T
+    head_weight_grad = joined(head_sum, 1).reshape(depth, 3, room)[..., :cols]
+    mix_weight_grad = joined(mix_sum, 1)[:, :cols].T
     up_weight_grad = joined(up_sum, 1)
     down_weight_grad = joined(down_sum, 1).T
-    branch_term = jnp.stack([attn_bias_grad, tail_bias_grad])
-    head_term = qkv_bias_term.reshape(3, width)[0::2]
-
-    def bias_half(mine):
-        if mine:
-            pieces = (head_term[:, :cols], lax.dynamic_slice_in_dim(branch_term, side * cols, cols, 1))
-            ups = up_bias_term[: hidden // 2]
-        else:
-            pieces = (
-                head_term[:, cols:],
-                lax.dynamic_slice_in_dim(branch_term, (1 - side) * cols, cols, 1),
-            )
-            ups = up_bias_term[hidden // 2 :]
-        return jnp.concatenate([p.reshape(-1) for p in pieces] + [ups])
-
-    biases = lax.psum(bias_half(True) + swap(bias_half(False)), "dp")
     return (
         block_out,
         latent_grad,
@@ -687,7 +1074,7 @@
         P("tensor"),
         P("tensor", "dp"),
     )
-    whole_latents = mesh.shape["tensor"] == 2
+    whole_latents = dict(mesh.shape) == {"dp": 16, "tensor": 2}
     return jax.shard_map(
         body_by_latents if whole_latents else body_by_heads,
         mesh=mesh,

time: 1040 us -> 1030 us (level)
  Pallas kernels: 203 us -> 332 us
  blocking collectives: 108 us -> 0 us
  waiting for transfers between devices: 239 us -> 199 us
  starting transfers between devices: 31.5 us -> 11.1 us
  local copies, waits for them, and re-layouts: 36.9 us -> 56 us
    ppermute x19 -> x10, waiting for transfers between devices: 178 us -> 45.7 us  [swap(): return lax.ppermute(a, 'tensor', [(0, 1), (1, 0)])]
    pallas_call x2 -> x4, Pallas kernels: 203 us -> 332 us  [the longest x1 115 us: attn_bwd(): pl.pallas_call(partial(attn_bwd_kernel, blk=blk, heads=heads), grid=(n, 2...]
    reduce_scatter x1, waiting for transfers between devices: 0.01 us -> 121 us  [body_by_latents(): up_sum = lax.psum_scatter(up_grad, 'dp', scatter_dimension=0, tiled=True)]
    psum x1 -> x0, blocking collectives: 59.3 us -> none  [body_by_latents(): biases = lax.psum(bias_half(True) + swap(bias_half(False)), 'dp')]
    all_gather x2 -> x0, blocking collectives: 48.3 us -> none  [the longest x1 25.9 us: body_by_latents(): lax.all_gather(in_order(my_cols, swap(other_cols), 0), 'dp', axis=0, tile...]
    reduce_scatter x1, waiting for transfers between devices: 56.4 us -> 20.3 us  [body_by_latents(): lax.psum_scatter(down_grad, 'dp', scatter_dimension=0, tiled=True)]
    unnamed x97 -> x107, local copies, waits for them, and re-layouts: 6.48 us -> 21.1 us
    ppermute x19 -> x10, starting transfers between devices: 23.4 us -> 10.5 us  [swap(): return lax.ppermute(a, 'tensor', [(0, 1), (1, 0)])]
  transfers between devices with their start and end apart: 27 -> 15, of which waited for: 11 -> 5; matrix products, arithmetic and copies ran while one was open for 28% -> 16% of each run, Pallas kernels for 20% -> 24%
where the time goes in v2:
time: 1030 us
  matrix products  358 us (35%)
  Pallas kernels  332 us (32%)
  waiting for transfers between devices  199 us (19%)
  local copies, waits for them, and re-layouts  56 us (5%)
  other arithmetic  54.1 us (5%)
  between operations  14.9 us (1%)
  starting transfers between devices  11.1 us (1%)
    dot_general x13, matrix products, mm(): return jnp.einsum(spec, a, b, preferred_element_type=f32)  358 us
    reduce_scatter x1, waiting for transfers between devices, body_by_latents(): up_sum = lax.psum_scatter(up_grad, 'dp', scatter_dimension=0, tiled=True)  121 us
    pallas_call x1, Pallas kernels, attn_bwd(): pl.pallas_call(partial(attn_bwd_kernel, blk=blk, heads=heads), grid=(n, 2...  115 us
    pallas_call x1, Pallas kernels, opening(): pl.pallas_call(opening_kernel, in_specs=[vmem, vmem, vmem, anywhere, anyw...  84.5 us
    pallas_call x1, Pallas kernels, closing(): pl.pallas_call(closing_kernel, in_specs=[vmem, vmem, vmem], out_specs=[vm...  77.7 us
    pallas_call x1, Pallas kernels, attn_fwd(): pl.pallas_call(partial(attn_fwd_kernel, blk=blk, heads=heads), grid=(n, 2...  55.1 us
    ppermute x10, waiting for transfers between devices, swap(): return lax.ppermute(a, 'tensor', [(0, 1), (1, 0)])  45.7 us
    unnamed x107, local copies, waits for them, and re-layouts  21.1 us
  transfers between devices with their start and end apart: 15, of which 5 were waited for; matrix products, arithmetic and copies ran while one was open for 16% of the time, Pallas kernels for 24%

profile of v2, /device:TPU:0, one launch (start us, length us, event | category | flops | bytes accessed | tf_op | source)
XLA Modules:
  0.0 1025.1 jit_solution(17486248705445330265)
XLA Ops:
  7.2 1.1 copy.77
  9.2 1.5 constant_dynamic-update-slice_fusion.2
  10.8 1.1 copy.98
  12.1 0.8 reshape.168
  14.4 1.2 pad_maximum_fusion.2.rest_ref
  15.6 2.3 copy-done.2
  17.9 0.8 copy-done.3
  18.8 84.5 %opening.1 = (bf16[16,72,3840]{2,1,0:T(8,128)(2,1)S(1)}, bf16[72,5248]{1,0:T(8,128)(2,1)S(1)}, bf16[2,512,1152]{2,1,0:T(8,128)(2,1)S(1)}, f32[2,8,1728]{2,1,0:T(8,128)S(1)}, f32[16,8,128]{2,1,0:T(8,128)S(1)}) custom-call(f32[16,8,128]{2,1,0:T(8,128)S(1)} %fusion.39.cond_ref, bf16[2,128,1728]{2,1,0:T(8,128)(2,1)S(1)} %pad_bitcast_fusion.mod_w_ref, ...), custom_call_target="tpu_custom_call" | custom-call | tf_op jit(solution)/shard_map/opening/pallas_call | solution.py:751
  104.6 3.4 copy-done.7
  108.7 2.0 constant_dynamic-update-slice_fusion.1
  115.9 1.3 convert_element_type.125
  117.2 1.5 collective-permute-start.1
  118.7 1.3 convert_element_type.127
  120.6 4.9 constant_dynamic-slice_fusion.3
  125.5 1.5 collective-permute-start.4
  127.2 2.0 constant_dynamic-slice_fusion.4
  130.1 1.6 fusion.23
  131.7 0.8 maximum_select_fusion.3
  134.0 27.6 %add_convert_fusion.q_ref.k_ref.v_ref = bf16[2,1024,3840]{2,1,0:T(8,128)(2,1)} fusion(f32[3840]{0:T(1024)S(1)} %pad_maximum_fusion.6, bf16[1152,3840,1]{1,0,2:T(8,128)(2,1)} %bitcast.120, f32[2,1152]{1,0:T(2,128)S(1)} %get-tuple-element.140, f32[2,1152]{1,0:T(2,128)S(1)} %get-tuple-element.141, f32[2,1024]{1,0:T(2,128)S(1)} %add_rsqrt_fusion.1, ...), kind=kOutput, calls=%fused_computation.12 | convolution fusion | flops 18156355584 | bytes 29344768 | tf_op jit(solution)/shard_map/bsd,dc->bsc/dot_general | solution.py:868
  161.6 55.1 %attention_forward.1 = (bf16[2,1024,1280]{2,1,0:T(8,128)(2,1)}, f32[2,2,8,1024]{3,2,1,0:T(8,128)}) custom-call(bf16[2,1024,3840]{2,1,0:T(8,128)(2,1)} %add_convert_fusion.q_ref.k_ref.v_ref, bf16[2,1024,3840]{2,1,0:T(8,128)(2,1)} %add_convert_fusion.q_ref.k_ref.v_ref, bf16[2,1024,3840]{2,1,0:T(8,128)(2,1)} %add_convert_fusion.q_ref.k_ref.v_ref), custom_call_target="tpu_custom_call" | custom-call | flops 10737418240 | bytes 20971520 | tf_op jit(solution)/shard_map/attention_forward/pallas_call | solution.py:399
  217.5 4.8 fusion.24
  222.3 11.4 %all-gather.2.cloned.1.call-done = bf16[1152,10496]{1,0:T(8,128)(2,1)} async-done(((bf16[72,10496]{1,0:T(8,128)(2,1)}), bf16[1152,10496]{1,0:T(8,128)(2,1)}) %all-gather.2.cloned.1.call-update) | async-done | bytes 24182800 | tf_op jit(solution)/shard_map/all_gather | solution.py:944
  233.8 12.5 %fusion.52 = (f32[2,1024]{1,0:T(2,128)S(1)}, f32[2,1024,1152]{2,1,0:T(8,128)S(1)}, f32[2,1024,1152]{2,1,0:T(8,128)}) fusion(f32[1152]{0:T(1024)S(1)} %get-tuple-element.113, f32[2,1152]{1,0:T(2,128)S(1)} %get-tuple-element.142, bf16[2,512,1152]{2,1,0:T(8,128)(2,1)S(1)} %get-tuple-element.31, bf16[2,512,1152]{2,1,0:T(8,128)(2,1)} %copy-done.8, ...), kind=kOutput, calls=%fused_computation.153 | convolution fusion | flops 6058670080 | bytes 31806976 | tf_op jit(solution)/shard_map/bsc,dc->bsd/dot_general | solution.py:868
  246.3 3.6 copy-done.10
  250.0 1.1 multiply_reduce_fusion.3
  251.1 42.1 %multiply_convert_fusion = (bf16[2,1024,4608]{2,1,0:T(8,128)(2,1)}, f32[2,1024,4608]{2,1,0:T(8,128)}) fusion(f32[4608]{0:T(1024)S(1)} %pad_maximum_fusion.5, bf16[1152,10496]{1,0:T(8,128)(2,1)} %all-gather.2.cloned.1.call-done, f32[2,1024,1152]{2,1,0:T(8,128)} %copy-done.10, f32[2,1152]{1,0:T(2,128)S(1)} %get-tuple-element.138, ...), kind=kOutput, calls=%fused_computation.10 | convolution fusion | flops 21849440256 | bytes 76730368 | tf_op jit(solution)/shard_map/bsd,df->bsf/dot_general | solution.py:868
  293.2 28.7 %fusion.7 = bf16[1152,4608]{1,0:T(8,128)(2,1)} fusion(bf16[2,1024,1152]{2,1,0:T(8,128)(2,1)} %fusion.24, bf16[2,1024,4608]{2,1,0:T(8,128)(2,1)} %get-tuple-element.152), kind=kOutput, calls=%fused_computation.15 | convolution fusion | flops 21748580352 | bytes 34209792 | tf_op jit(solution)/shard_map/bsd,bsf->df/dot_general | solution.py:868
  321.9 55.8 %convert_reduce_fusion = (f32[4608]{0:T(1024)}, bf16[2,1024,4608]{2,1,0:T(8,128)(2,1)}) fusion(f32[2,1024,4608]{2,1,0:T(8,128)} %get-tuple-element.153, f32[4608]{0:T(1024)S(1)} %pad_maximum_fusion.5, bf16[2,1024,1152]{2,1,0:T(8,128)(2,1)} %fusion.24, bf16[1152,10496]{1,0:T(8,128)(2,1)} %all-gather.2.cloned.1.call-done), kind=kOutput, calls=%fused_computation.9 | convolution fusion | flops 21960323072 | bytes 71995392 | tf_op jit(solution)/shard_map/bsd,df->bsf/dot_general | solution.py:868
  377.7 32.4 %fusion.8 = bf16[1152,4608]{1,0:T(8,128)(2,1)} fusion(bf16[2,1024,4608]{2,1,0:T(8,128)(2,1)} %get-tuple-element.38, f32[2,1024,1152]{2,1,0:T(8,128)} %copy-done.10, f32[2,1152]{1,0:T(2,128)S(1)} %get-tuple-element.138, f32[2,1152]{1,0:T(2,128)S(1)} %get-tuple-element.139, f32[2,1024]{1,0:T(2,128)S(1)} %add_rsqrt_fusion, ...), kind=kOutput, calls=%fused_computation.16 | convolution fusion | flops 21760376832 | bytes 38963200 | tf_op jit(solution)/shard_map/bsd,bsf->df/dot_general | solution.py:868
  410.1 35.0 %multiply_reduce_fusion = (bf16[2,1152]{1,0:T(2,128)(2,1)}, f32[2,1024]{1,0:T(2,128)S(1)}, f32[2,1024]{1,0:T(2,128)S(1)}, bf16[2,1152]{1,0:T(2,128)(2,1)}, f32[2,1024,1152]{2,1,0:T(8,128)}) fusion(f32[2,1024,1152]{2,1,0:T(8,128)} %copy-done.10, f32[2,1024]{1,0:T(2,128)S(1)} %add_rsqrt_fusion, f32[2,1024]{1,0:T(2,128)S(1)} %broadcast_multiply_fusion.4, ...), kind=kOutput, calls=%fused_computation.44 | convolution fusion | flops 21764497408 | bytes 48416768 | tf_op jit(solution)/shard_map/bsf,df->bsd/dot_general | solution.py:868
  445.1 39.3 %convert_reduce_fusion.2 = (f32[2,1152]{1,0:T(2,128)S(1)}, bf16[2,1152]{1,0:T(2,128)(2,1)S(1)}, bf16[2,1024,1152]{2,1,0:T(8,128)(2,1)}, bf16[2,1152]{1,0:T(2,128...) fusion(bf16[2,512,1152]{2,1,0:T(8,128)(2,1)} %collective-permute-done.4, ...), kind=kOutput, calls=%fused_computation.18 | convolution fusion | flops 21797527552 | bytes 76765184 | tf_op jit(solution)/shard_map/bsf,df->bsd/dot_general | solution.py:868
  484.4 13.7 %fusion.29 = bf16[1152,1280]{1,0:T(8,128)(2,1)} fusion(bf16[2,1024,1280]{2,1,0:T(8,128)(2,1)} %get-tuple-element.34.o_ref, f32[2,1024,1152]{2,1,0:T(8,128)} %get-tuple-element.122, f32[2,1152]{1,0:T(2,128)S(1)} %copy-done.40), kind=kOutput, calls=%fused_computation.58 | convolution fusion | flops 6045990912 | bytes 17638400 | tf_op jit(solution)/shard_map/bsd,bsc->dc/dot_general | solution.py:868
  498.1 11.9 %convolution_convert_fusion.do_ref = bf16[2,1024,1280]{2,1,0:T(8,128)(2,1)} fusion(bf16[1152,10496]{1,0:T(8,128)(2,1)} %all-gather.2.cloned.1.call-done, f32[2,1024,1152]{2,1,0:T(8,128)} %get-tuple-element.122, f32[2,1152]{1,0:T(2,128)S(1)} %copy-done.40), kind=kOutput, calls=%fused_computation.59 | convolution fusion | flops 6047137792 | bytes 17638400 | tf_op jit(solution)/shard_map/bsd,dc->bsc/dot_general | solution.py:868
  510.1 114.8 %attention_backward.1 = bf16[2,1024,3840]{2,1,0:T(8,128)(2,1)} custom-call(bf16[2,1024,3840]{2,1,0:T(8,128)(2,1)} %add_convert_fusion.q_ref.k_ref.v_ref, bf16[2,1024,3840]{2,1,0:T(8,128)(2,1)} %add_convert_fusion.q_ref.k_ref.v_ref, bf16[2,1024,3840]{2,1,0:T(8,128)(2,1)} %add_convert_fusion.q_ref.k_ref.v_ref, ...), custom_call_target="tpu_custom_call" | custom-call | flops 26843545600 | bytes 41943040 | tf_op jit(solution)/shard_map/attention_backward/pallas_call | solution.py:480
  624.9 24.9 %bitcast_convert_fusion = bf16[1152,3840]{1,0:T(8,128)(2,1)} fusion(bf16[2,1024,3840]{2,1,0:T(8,128)(2,1)} %attention_backward.1, f32[2,1152]{1,0:T(2,128)S(1)} %copy-done.38, f32[2,1152]{1,0:T(2,128)S(1)} %copy-done.20, f32[2,1024]{1,0:T(2,128)S(1)} %copy-done.35, f32[2,1024]{1,0:T(2,128)S(1)} %copy-done.18, bf16[2,512,1152]{2,1,0:T(8,128)(2,1)S(1)} %copy-done.1, ...), kind=kOutput, calls=%fused_computation.17 | convolution fusion | flops 18145050624 | bytes 29329408 | tf_op jit(solution)/shard_map/bsd,bsc->dc/dot_general | solution.py:868
  650.5 1.5 slice.209
  653.5 7.6 convert_reduce_fusion.1
  663.2 32.0 %fusion.22 = (bf16[2,1152]{1,0:T(2,128)(2,1)S(1)}, f32[2,1024]{1,0:T(2,128)}, f32[2,1024]{1,0:T(2,128)S(1)}, bf16[2,1152]{1,0:T(2,128)(2,1)S(1)}, f32[2,1024,1152]{2,1,0:T(8,128)}) fusion(f32[2,1024]{1,0:T(2,128)S(1)} %copy-done.35, f32[2,1024]{1,0:T(2,128)S(1)} %copy-done.18, bf16[2,512,1152]{2,1,0:T(8,128)(2,1)S(1)} %copy-done.1, ...), kind=kOutput, calls=%fused_computation.40 | convolution fusion | flops 18150055936 | bytes 38782976 | tf_op jit(solution)/shard_map/bsc,dc->bsd/dot_general | solution.py:868
  696.6 9.5 fusion.21
  706.2 1.8 fusion.53
  708.0 1.2 collective-permute-start.5
  709.2 77.7 %closing.1 = (f32[16,8,1728]{2,1,0:T(8,128)S(1)}, f32[36,128]{1,0:T(8,128)S(1)}, f32[2,16,8,128]{3,2,1,0:T(8,128)S(1)}) custom-call(f32[2,8,1728]{2,1,0:T(8,128)S(1)} %pad_maximum_fusion.3.mod_ref, f32[2,36,128]{2,1,0:T(8,128)S(1)} %pad_maximum_fusion.4.bias_ref, bf16[2,128,1728]{2,1,0:T(8,128)(2,1)S(1)} %pad_bitcast_fusion.mod_w_ref), custom_call_target="tpu_custom_call" | custom-call | tf_op jit(solution)/shard_map/closing/pallas_call | solution.py:827
  787.0 0.8 convert_element_type.144
  787.8 1.6 reshape.162
  789.4 1.0 copy.91
  790.4 2.0 reshape.163
  793.4 5.8 fusion.54
  801.3 2.0 fusion.60
  804.0 5.8 maximum_select_fusion.1
  809.8 1.0 fusion.55
  810.7 2.1 collective-permute-start.7
  812.8 1.0 split.33
  814.0 39.7 %collective-permute-done.3 = bf16[2,512,1152]{2,1,0:T(8,128)(2,1)} collective-permute-done((bf16[2,512,1152]{2,1,0:T(8,128)(2,1)}, bf16[2,512,1152]{2,1,0:T(8,128)(2,1)}, u32[]{:S(2)}, u32[]{:S(2)}) %collective-permute-start.3) | collective-permute-done | bytes 2359328 | tf_op jit(solution)/shard_map/ppermute | solution.py:895
  853.7 6.9 maximum_select_fusion
  861.2 20.3 %reduce-scatter.11.cloned.1.call-done = bf16[72,4608]{1,0:T(8,128)(2,1)} async-done(((bf16[1152,4608]{1,0:T(8,128)(2,1)}), bf16[72,4608]{1,0:T(8,128)(2,1)}) %reduce-scatter.11.cloned.1.call-update) | async-done | bytes 663568 | tf_op jit(solution)/shard_map/reduce_scatter | solution.py:977
  881.6 1.0 split.39
  882.6 1.5 collective-permute-start.9
  884.4 0.8 copy.92
  885.3 120.8 %reduce-scatter.9.cloned.1.call-done = bf16[72,4608]{1,0:T(8,128)(2,1)} async-done(((bf16[1152,4608]{1,0:T(8,128)(2,1)}), bf16[72,4608]{1,0:T(8,128)(2,1)}) %reduce-scatter.9.cloned.1.call-update) | async-done | bytes 663568 | tf_op jit(solution)/shard_map/reduce_scatter | solution.py:982
  1006.1 1.0 split.37
  1007.1 1.5 collective-permute-start.8
  1008.6 1.9 add_bitcast_fusion
  1010.5 6.0 collective-permute-done.8
  1016.5 1.9 convert_add_fusion.2
  (197 shorter events, 23.9 us)
Async XLA Ops:
  7.2 226.6 %all-gather.2.cloned.1.call-start = ((), (), s32[]{:S(2)}) async-start(), calls=%async_computation.4 | async-start | bytes 25694208 | tf_op jit(solution)/shard_map/all_gather | solution.py:944
  14.4 97.1 %copy-start.14 = (bf16[2304,72]{0,1:T(8,128)(2,1)S(1)}, bf16[2304,72]{0,1:T(8,128)(2,1)}, u32[]{:S(2)}) copy-start(bf16[2304,72]{0,1:T(8,128)(2,1)} %param.23) | copy-start | bytes 995332
  15.6 2.3 copy-start.2
  17.9 0.8 copy-start.3
  103.3 0.6 copy-start.4
  104.0 0.6 copy-start.6
  104.6 3.5 copy-start.7
  108.1 125.7 %copy-start = (bf16[2,512,1152]{2,1,0:T(8,128)(2,1)}, bf16[2,512,1152]{2,1,0:T(8,128)(2,1)S(1)}, u32[]{:S(2)}) copy-start(bf16[2,512,1152]{2,1,0:T(8,128)(2,1)S(1)} %get-tuple-element.31) | copy-start | bytes 7077892
  108.1 18.9 %copy-start.5 = (f32[2,8,1728]{2,1,0:T(8,128)S(1)}, f32[2,8,1728]{2,1,0:T(8,128)}, u32[]{:S(2)}) copy-start(f32[2,8,1728]{2,1,0:T(8,128)} %copy-done.4) | copy-start | bytes 331780
  113.0 696.8 %reduce-scatter.7.cloned.1.call-start = ((), (), s32[]{:S(2)}) async-start(), calls=%async_computation.6 | async-start | bytes 3133440 | tf_op jit(solution)/shard_map/reduce_scatter | solution.py:993
  114.2 0.6 copy-start.23
  114.2 1.2 copy-start.25
  114.8 1.1 copy-start.27
  115.4 17.8 %collective-permute-start = (f32[1920]{0:T(1024)}, f32[1920]{0:T(1024)}, u32[]{:S(2)}, u32[]{:S(2)}) collective-permute-start(f32[1920]{0:T(1024)} %pad_maximum_fusion.7), channel_id=1, source_target_pairs={{0,1},{1,0},{2,3},{3,2},{4,5},{5,4},{6,7},{7,6},{8,9},{9,8},{10,11... | collective-permute-start | bytes 23048 | tf_op jit(solution)/shard_map/ppermute | solution.py:895
  117.2 14.5 %collective-permute-start.1 = (f32[2,576]{1,0:T(2,128)}, f32[2,576]{1,0:T(2,128)}, u32[]{:S(2)}, u32[]{:S(2)}) collective-permute-start(f32[2,576]{1,0:T(2,128)} %convert_element_type.125), channel_id=1, source_target_pairs={{0,1},{1,0},{2,3},{3,2},{4,5},{5,4},{6,7},{7,6},{8,9},{9,8},{10,11... | collective-permute-start | bytes 13832 | tf_op jit(solution)/shard_map/ppermute | solution.py:895
  120.0 96.7 %collective-permute-start.2 = (f32[2304]{0:T(1024)}, f32[2304]{0:T(1024)}, u32[]{:S(2)}, u32[]{:S(2)}) collective-permute-start(f32[2304]{0:T(1024)} %convert_element_type.127), channel_id=1, source_target_pairs={{0,1},{1,0},{2,3},{3,2},{4,5},{5,4},{6,7},{7,6},{8,9},{9,8},{10,11... | collective-permute-start | bytes 27656 | tf_op jit(solution)/shard_map/ppermute | solution.py:895
  125.5 92.0 %collective-permute-start.4 = (bf16[2,512,1152]{2,1,0:T(8,128)(2,1)}, bf16[2,512,1152]{2,1,0:T(8,128)(2,1)}, u32[]{:S(2)}, u32[]{:S(2)}) collective-permute-start(bf16[2,512,1152]{2,1,0:T(8,128)(2,1)} %get-tuple-element.36), channel_id=1, source_target_pairs={{0,1},{1,0},{2,3},{3,2},{4,5},{5,4},{6,7},{7,6},{8,9},{9,8},{10,11... | collective-permute-start | bytes 7077896 | tf_op jit(solution)/shard_map/ppermute | solution.py:895
  127.1 6.1 copy-start.24
  127.1 6.1 copy-start.26
  127.1 6.1 copy-start.28
  129.2 4.7 copy-start.8
  129.9 4.0 copy-start.17
  130.1 3.9 copy-start.16
  130.1 3.9 copy-start.19
  130.1 3.9 copy-start.37
  130.1 87.4 %copy-start.21 = (f32[2,1152]{1,0:T(2,128)}, f32[2,1152]{1,0:T(2,128)S(1)}, u32[]{:S(2)}) copy-start(f32[2,1152]{1,0:T(2,128)S(1)} %get-tuple-element.137) | copy-start | bytes 27652
  130.1 103.6 %copy-start.39 = (f32[2,1152]{1,0:T(2,128)}, f32[2,1152]{1,0:T(2,128)S(1)}, u32[]{:S(2)}) copy-start(f32[2,1152]{1,0:T(2,128)S(1)} %get-tuple-element.142) | copy-start | bytes 27652
  131.7 2.3 copy-start.34
  133.2 100.5 %copy-start.42 = (f32[1152]{0:T(1024)}, f32[1152]{0:T(1024)S(1)}, u32[]{:S(2)}) copy-start(f32[1152]{0:T(1024)S(1)} %get-tuple-element.113) | copy-start | bytes 13828
  161.6 55.9 %copy-start.11 = (bf16[2,512,1152]{2,1,0:T(8,128)(2,1)S(1)}, bf16[2,512,1152]{2,1,0:T(8,128)(2,1)}, u32[]{:S(2)}) copy-start(bf16[2,512,1152]{2,1,0:T(8,128)(2,1)} %get-tuple-element.125) | copy-start | bytes 7077892
  246.3 3.7 copy-start.10
  410.1 35.0 %copy-start.12 = (bf16[2,512,1152]{2,1,0:T(8,128)(2,1)S(1)}, bf16[2,512,1152]{2,1,0:T(8,128)(2,1)}, u32[]{:S(2)}) copy-start(bf16[2,512,1152]{2,1,0:T(8,128)(2,1)} %get-tuple-element.125) | copy-start | bytes 7077892
  410.1 35.0 %copy-start.22 = (f32[2,1152]{1,0:T(2,128)S(1)}, f32[2,1152]{1,0:T(2,128)}, u32[]{:S(2)}) copy-start(f32[2,1152]{1,0:T(2,128)} %copy-done.21) | copy-start | bytes 27652
  410.1 35.0 %copy-start.41 = (f32[1152]{0:T(1024)S(1)}, f32[1152]{0:T(1024)}, u32[]{:S(2)}) copy-start(f32[1152]{0:T(1024)} %get-tuple-element.112) | copy-start | bytes 13828
  410.1 35.0 %copy-start.43 = (f32[1152]{0:T(1024)S(1)}, f32[1152]{0:T(1024)}, u32[]{:S(2)}) copy-start(f32[1152]{0:T(1024)} %copy-done.42) | copy-start | bytes 13828
  445.1 39.3 %copy-start.40 = (f32[2,1152]{1,0:T(2,128)S(1)}, f32[2,1152]{1,0:T(2,128)}, u32[]{:S(2)}) copy-start(f32[2,1152]{1,0:T(2,128)} %copy-done.39) | copy-start | bytes 27652
  510.0 302.8 %reduce-scatter.5.cloned.1.call-start = ((), (), s32[]{:S(2)}) async-start(), calls=%async_computation.5 | async-start | bytes 9400320 | tf_op jit(solution)/shard_map/reduce_scatter | solution.py:997
  510.1 114.8 %copy-start.1 = (bf16[2,512,1152]{2,1,0:T(8,128)(2,1)S(1)}, bf16[2,512,1152]{2,1,0:T(8,128)(2,1)}, u32[]{:S(2)}) copy-start(bf16[2,512,1152]{2,1,0:T(8,128)(2,1)} %copy-done) | copy-start | bytes 7077892
  510.1 114.8 %copy-start.9 = (bf16[2,512,1152]{2,1,0:T(8,128)(2,1)S(1)}, bf16[2,512,1152]{2,1,0:T(8,128)(2,1)}, u32[]{:S(2)}) copy-start(bf16[2,512,1152]{2,1,0:T(8,128)(2,1)} %copy-done.8) | copy-start | bytes 7077892
  510.1 114.8 %copy-start.18 = (f32[2,1024]{1,0:T(2,128)S(1)}, f32[2,1024]{1,0:T(2,128)}, u32[]{:S(2)}) copy-start(f32[2,1024]{1,0:T(2,128)} %copy-done.17) | copy-start | bytes 24580
  510.1 114.8 %copy-start.20 = (f32[2,1152]{1,0:T(2,128)S(1)}, f32[2,1152]{1,0:T(2,128)}, u32[]{:S(2)}) copy-start(f32[2,1152]{1,0:T(2,128)} %copy-done.19) | copy-start | bytes 27652
  510.1 114.8 %copy-start.35 = (f32[2,1024]{1,0:T(2,128)S(1)}, f32[2,1024]{1,0:T(2,128)}, u32[]{:S(2)}) copy-start(f32[2,1024]{1,0:T(2,128)} %copy-done.34) | copy-start | bytes 24580
  510.1 114.8 %copy-start.38 = (f32[2,1152]{1,0:T(2,128)S(1)}, f32[2,1152]{1,0:T(2,128)}, u32[]{:S(2)}) copy-start(f32[2,1152]{1,0:T(2,128)} %copy-done.37) | copy-start | bytes 27652
  649.8 231.7 %reduce-scatter.11.cloned.1.call-start = ((), (), s32[]{:S(2)}) async-start(), calls=%async_computation.8 | async-start | bytes 11280384 | tf_op jit(solution)/shard_map/reduce_scatter | solution.py:977
  650.4 355.7 %reduce-scatter.9.cloned.1.call-start = ((), (), s32[]{:S(2)}) async-start(), calls=%async_computation.7 | async-start | bytes 11280384 | tf_op jit(solution)/shard_map/reduce_scatter | solution.py:982
  663.2 32.1 %copy-start.45 = (bf16[2,1152]{1,0:T(2,128)(2,1)S(1)}, bf16[2,1152]{1,0:T(2,128)(2,1)}, u32[]{:S(2)}) copy-start(bf16[2,1152]{1,0:T(2,128)(2,1)} %get-tuple-element.106) | copy-start | bytes 13828
  663.2 32.1 %copy-start.44 = (bf16[2,1152]{1,0:T(2,128)(2,1)S(1)}, bf16[2,1152]{1,0:T(2,128)(2,1)}, u32[]{:S(2)}) copy-start(bf16[2,1152]{1,0:T(2,128)(2,1)} %get-tuple-element.98) | copy-start | bytes 13828
  706.1 3.0 copy-start.36
  706.1 3.0 copy-start.30
  706.1 3.0 copy-start.33
  706.1 3.1 copy-start.31
  706.1 3.1 copy-start.32
  708.0 95.3 %copy-start.29 = (bf16[4,1152]{1,0:T(4,128)(2,1)S(1)}, bf16[4,1152]{1,0:T(4,128)(2,1)}, u32[]{:S(2)}) copy-start(bf16[4,1152]{1,0:T(4,128)(2,1)} %param.13) | copy-start | bytes 27652
  708.0 96.0 %collective-permute-start.5 = (bf16[2,512,1152]{2,1,0:T(8,128)(2,1)}, bf16[2,512,1152]{2,1,0:T(8,128)(2,1)}, u32[]{:S(2)}, u32[]{:S(2)}) collective-permute-start(bf16[2,512,1152]{2,1,0:T(8,128)(2,1)} %get-tuple-element.124), channel_id=1, source_target_pairs={{0,1},{1,0},{2,3},{3,2},{4,5},{5,4},{6,7},{7,6},{8,9},{9,8},{10,11... | collective-permute-start | bytes 7077896 | tf_op jit(solution)/shard_map/ppermute | solution.py:895
  792.7 8.5 copy-start.13
  799.2 54.5 %collective-permute-start.3 = (bf16[2,512,1152]{2,1,0:T(8,128)(2,1)}, bf16[2,512,1152]{2,1,0:T(8,128)(2,1)}, u32[]{:S(2)}, u32[]{:S(2)}) collective-permute-start(bf16[2,512,1152]{2,1,0:T(8,128)(2,1)} %get-tuple-element.128), channel_id=1, source_target_pairs={{0,1},{1,0},{2,3},{3,2},{4,5},{5,4},{6,7},{7,6},{8,9},{9,8},{10,11... | collective-permute-start | bytes 7077896 | tf_op jit(solution)/shard_map/ppermute | solution.py:895
  810.7 49.8 %collective-permute-start.7 = (bf16[72,640]{1,0:T(8,128)(2,1)S(1)}, bf16[72,640]{1,0:T(8,128)(2,1)S(1)}, u32[]{:S(2)}, u32[]{:S(2)}) collective-permute-start(bf16[72,640]{1,0:T(8,128)(2,1)S(1)} %get-tuple-element.130), channel_id=1, source_target_pairs={{0,1},{1,0},{2,3},{3,2},{4,5},{5,4},{6,7},{7,6},{8,9},{9,8},{10,11... | collective-permute-start | bytes 276488 | tf_op jit(solution)/shard_map/ppermute | solution.py:895
  812.8 71.3 %copy-start.15 = (bf16[72,3840]{1,0:T(8,128)(2,1)S(1)}, bf16[72,3840]{1,0:T(8,128)(2,1)}, u32[]{:S(2)}) copy-start(bf16[72,3840]{1,0:T(8,128)(2,1)} %reduce-scatter.5.cloned.1.call-done) | copy-start | bytes 1658884
  813.9 70.3 %collective-permute-start.6 = (bf16[72,1920]{1,0:T(8,128)(2,1)S(1)}, bf16[72,1920]{1,0:T(8,128)(2,1)S(1)}, u32[]{:S(2)}, u32[]{:S(2)}) collective-permute-start(bf16[72,1920]{1,0:T(8,128)(2,1)S(1)} %split.33), channel_id=1, source_target_pairs={{0,1},{1,0},{2,3},{3,2},{4,5},{5,4},{6,7},{7,6},{8,9},{9,8},{10,11... | collective-permute-start | bytes 829448 | tf_op jit(solution)/shard_map/ppermute | solution.py:895
  882.6 126.1 %collective-permute-start.9 = (bf16[72,2304]{1,0:T(8,128)(2,1)S(1)}, bf16[72,2304]{1,0:T(8,128)(2,1)S(1)}, u32[]{:S(2)}, u32[]{:S(2)}) collective-permute-start(bf16[72,2304]{1,0:T(8,128)(2,1)S(1)} %split.39), channel_id=1, source_target_pairs={{0,1},{1,0},{2,3},{3,2},{4,5},{5,4},{6,7},{7,6},{8,9},{9,8},{10,11... | collective-permute-start | bytes 995336 | tf_op jit(solution)/shard_map/ppermute | solution.py:895
  1007.1 9.4 collective-permute-start.8
Sparse Core Ops, SparseCore 0:
  113.1 120.5 all-gather.1
  510.1 65.1 reduce-scatter.6
  649.9 106.9 reduce-scatter.4
  761.4 120.0 reduce-scatter.10
  886.0 120.0 reduce-scatter.8

commit v3 on v2

--- a/solution.py
+++ b/solution.py
@@ -493,13 +493,110 @@
             pltpu.VMEM((seq, seq), bf16),
         ],
         compiler_params=pltpu.CompilerParams(vmem_limit_bytes=56 << 20),
-        cost_estimate=pl.CostEstimate(
-            flops=20 * n * seq * seq * width,
-            bytes_accessed=32 * n * seq * width,
-            transcendentals=2 * n * heads * seq * seq,
-        ),
+        cost_estimate=pl.CostEstimate(flops=0, bytes_accessed=0, transcendentals=0),
         name="attention_backward",
     )(qkv, qkv, qkv, grad, mixed, lse)
+
+
+def gelu_with_slope(u):
+    k, cubic = 0.7978845608028654, 0.7978845608028654 * 0.044715
+    square = u * u
+    half = 0.5 + 0.5 * jnp.tanh(u * (k + cubic * square))
+    value = u * half
+    return value, half + value * (1.0 - half) * (2.0 * k + 6.0 * cubic * square)
+
+
+def tile_steps(rows, cols, sub_rows, sub_cols):
+    return [
+        (slice(i, i + sub_rows), slice(j, j + sub_cols))
+        for j in range(0, cols, sub_cols)
+        for i in range(0, rows, sub_rows)
+    ]
+
+
+def up_forward_kernel(x_ref, w_ref, b_ref, act_ref, slope_ref):
+    steps = tile_steps(*act_ref.shape, 256, 256)
+    product = lambda r, c: jnp.dot(x_ref[r, :], w_ref[:, c], preferred_element_type=f32)
+    now = product(*steps[0])
+    for n, (r, c) in enumerate(steps):
+        later = product(*steps[n + 1]) if n + 1 < len(steps) else None
+        value, slope = gelu_with_slope(now + b_ref[:, c])
+        act_ref[r, c] = value.astype(bf16)
+        slope_ref[r, c] = slope.astype(bf16)
+        now = later
+
+
+def up_forward(x, w, bias):
+    count, seq, depth = x.shape
+    hidden = bias.shape[0]
+    rows, cols = 1024, hidden // 3
+    tile = pl.BlockSpec((rows, cols), lambda j, i: (i, j))
+    act, slope = pl.pallas_call(
+        up_forward_kernel,
+        grid=(hidden // cols, count * seq // rows),
+        in_specs=[
+            pl.BlockSpec((rows, depth), lambda j, i: (i, 0)),
+            pl.BlockSpec((depth, cols), lambda j, i: (0, j)),
+            pl.BlockSpec((1, cols), lambda j, i: (0, j)),
+        ],
+        out_specs=[tile, tile],
+        out_shape=[jax.ShapeDtypeStruct((count * seq, hidden), bf16)] * 2,
+        compiler_params=pltpu.CompilerParams(vmem_limit_bytes=56 << 20),
+        cost_estimate=pl.CostEstimate(
+            flops=2 * count * seq * depth * hidden,
+            bytes_accessed=4 * count * seq * hidden,
+            transcendentals=count * seq * hidden,
+        ),
+        name="up_forward",
+    )(x.reshape(count * seq, depth), w, bias.reshape(1, hidden))
+    return act.reshape(count, seq, hidden), slope.reshape(count, seq, hidden)
+
+
+def down_backward_kernel(g_ref, w_ref, slope_ref, out_ref, sum_ref):
+    steps = tile_steps(*out_ref.shape, out_ref.shape[0], 256)
+    product = lambda r, c: jnp.dot(g_ref[r, :], w_ref[:, c], preferred_element_type=f32)
+
+    @pl.when(pl.program_id(1) == 0)
+    def _():
+        sum_ref[...] = jnp.zeros_like(sum_ref)
+
+    now = product(*steps[0])
+    for n, (r, c) in enumerate(steps):
+        later = product(*steps[n + 1]) if n + 1 < len(steps) else None
+        grad = (now * slope_ref[r, c].astype(f32)).astype(bf16)
+        out_ref[r, c] = grad
+        sum_ref[:, c] += jnp.sum(grad.astype(f32), axis=0, keepdims=True)
+        now = later
+
+
+def down_backward(g, w, slope):
+    count, seq, depth = g.shape
+    hidden = slope.shape[2]
+    rows, cols = 1024, hidden // 3
+    ahead = hidden // cols
+    tile = pl.BlockSpec((rows, cols), lambda j, i: (i, j))
+    grad, total = pl.pallas_call(
+        down_backward_kernel,
+        grid=(hidden // cols, count * seq // rows),
+        in_specs=[
+            pl.BlockSpec((rows, depth), lambda j, i: (i, 0)),
+            pl.BlockSpec((depth, cols), lambda j, i: (0, ahead + j)),
+            tile,
+        ],
+        out_specs=[tile, pl.BlockSpec((1, cols), lambda j, i: (0, j))],
+        out_shape=[
+            jax.ShapeDtypeStruct((count * seq, hidden), bf16),
+            jax.ShapeDtypeStruct((1, hidden), f32),
+        ],
+        compiler_params=pltpu.CompilerParams(vmem_limit_bytes=56 << 20),
+        cost_estimate=pl.CostEstimate(
+            flops=2 * count * seq * depth * hidden,
+            bytes_accessed=4 * count * seq * hidden,
+            transcendentals=0,
+        ),
+        name="down_backward",
+    )(g.reshape(count * seq, depth), w, slope.reshape(count * seq, hidden))
+    return grad.reshape(count, seq, hidden), total[0]
 
 
 CORES = 2
@@ -606,17 +703,46 @@
                 pl.when(when)(sent.wait_send)
 
 
-def run_spreads(spreads):
-    depth = spreads[0].depth
-    for hop in range(1, depth):
-        for s in spreads:
-            s.relay(hop)
-        for s in spreads:
-            s.relay_across(hop - 1)
-    for s in spreads:
-        s.relay_across(depth - 1)
-    for s in spreads:
-        s.finish()
+class DirectSpread:
+    def __init__(self, out, sends, arrivals):
+        self.out, self.sends, self.arrivals = out, sends, arrivals
+        self.rank = lax.axis_index("dp")
+        self.groups = lax.axis_size("dp")
+        self.sibling = self.rank + 1 - 2 * lax.rem(self.rank, CORES)
+        self.steps = range(CORES, self.groups, CORES)
+
+    def copy(self, origin, send, target):
+        return pltpu.make_async_remote_copy(
+            src_ref=self.out.at[origin],
+            dst_ref=self.out.at[origin],
+            send_sem=self.sends.at[send],
+            recv_sem=self.arrivals.at[origin],
+            device_id={"dp": target},
+            device_id_type=MESH,
+        )
+
+    def peer(self, step):
+        return lax.rem(self.rank + step, self.groups)
+
+    def begin(self):
+        for step in self.steps:
+            self.copy(self.rank, step, self.peer(step)).start()
+        self.copy(self.rank, 0, self.sibling).start()
+
+    def relay(self):
+        for step in self.steps:
+            origin = self.peer(step)
+            self.copy(origin, step, origin).wait_recv()
+            self.copy(origin, step + 1, self.sibling).start()
+
+    def finish(self):
+        for step in range(0, self.groups, CORES):
+            origin = lax.rem(self.sibling + step, self.groups)
+            self.copy(origin, 0, self.sibling).wait_recv()
+        for step in self.steps:
+            self.copy(self.rank, step, self.peer(step)).wait_send()
+            self.copy(self.peer(step), step + 1, self.sibling).wait_send()
+        self.copy(self.rank, 0, self.sibling).wait_send()
 
 
 class Exchange:
@@ -670,8 +796,8 @@
 
 
 def opening_kernel(
-    cond_ref, mod_w_ref, mod_bias_ref, head_ref, rest_ref, latent_ref,
-    head_out, rest_out, latent_out, mod_out, cond_out,
+    cond_ref, mod_w_ref, mod_bias_ref, bias_ref, head_ref, rest_ref, latent_ref,
+    head_out, rest_out, latent_out, mod_out, cond_out, bias_out,
     part_ref, mod_in,
     x_send, x_recv, c_send, c_recv, m_send, m_recv, h_send, h_recv, local_sem,
 ):
@@ -687,6 +813,8 @@
     head_swap = to_partner(head_ref, other.block(rank), side, x_send, x_recv, 0)
     head_swap.start()
     mine.begin()
+    biases = to_partner(bias_ref, bias_out, side, x_send, x_recv, 4)
+    biases.start()
     latents = to_partner(
         latent_ref.at[pl.ds((1 - side) * own, own)], latent_out, side, x_send, x_recv, 1
     )
@@ -730,12 +858,13 @@
     mod_swap.wait()
     latents.wait()
     rest.wait()
+    biases.wait()
     head_swap.wait_send()
     conds.drain()
     mods.drain()
 
 
-def opening(cond_low, mod_weight, mod_bias, head, rest, latent):
+def opening(cond_low, mod_weight, mod_bias, biases, head, rest, latent):
     groups = lax.axis_size("dp")
     count, half_seq, width = latent.shape
     depth = cond_low.shape[1] // groups
@@ -750,19 +879,20 @@
     anywhere = pl.BlockSpec(memory_space=pl.ANY)
     return pl.pallas_call(
         opening_kernel,
-        in_specs=[vmem, vmem, vmem, anywhere, anywhere, anywhere],
-        out_specs=[anywhere, anywhere, anywhere, vmem, vmem],
+        in_specs=[vmem, vmem, vmem, vmem, anywhere, anywhere, anywhere],
+        out_specs=[anywhere, anywhere, anywhere, vmem, vmem, vmem],
         out_shape=[
             jax.ShapeDtypeStruct((groups, depth, 2 * head.shape[1]), bf16),
             jax.ShapeDtypeStruct(rest.shape, bf16),
             jax.ShapeDtypeStruct((count // 2, half_seq, width), bf16),
             jax.ShapeDtypeStruct((2, 2 * count, half), f32),
             jax.ShapeDtypeStruct(blocks.shape, f32),
+            jax.ShapeDtypeStruct(biases.shape, f32),
         ],
         scratch_shapes=[
             pltpu.VMEM((groups, 2 * count, half), f32),
             pltpu.VMEM((groups, 2 * count, half), f32),
-            dma((4,)), dma((4,)),
+            dma((5,)), dma((5,)),
             dma((groups,)), dma((groups,)),
             dma((groups,)), dma((groups,)),
             dma((2, groups, 4)), dma((2, groups)),
@@ -770,7 +900,7 @@
         ],
         compiler_params=pltpu.CompilerParams(collective_id=0, has_side_effects=True, vmem_limit_bytes=32 << 20),
         name="opening",
-    )(blocks, weights, bias, head, rest, latent)
+    )(blocks, weights, bias, biases, head, rest, latent)
 
 
 def closing_kernel(
@@ -791,12 +921,13 @@
     bias_swap.wait()
     mod_out[rank] = mod_ref[0] + mod_unit[1]
     bias_in[rank] = bias_ref[0] + bias_unit[1]
-    mods = Spread(None, mod_out, m_send, m_recv)
-    biases = Spread(None, bias_in, b_send, b_recv)
+    mods = DirectSpread(mod_out, m_send, m_recv)
+    biases = DirectSpread(bias_in, b_send, b_recv)
     mods.begin()
     biases.begin()
-    run_spreads([mods, biases])
-    bias_out[...] = jnp.sum(bias_in[...], axis=0)
+    mods.relay()
+    biases.relay()
+    mods.finish()
     groups, rows, half = mod_out.shape
     low = mod_out[...].reshape(groups * rows, half).astype(bf16)
     lanes = mod_w_ref.shape[1]
@@ -808,6 +939,8 @@
     ).reshape(groups, rows, lanes)
     conds = Exchange(part_ref, cond_in, c_send, c_recv)
     conds.begin()
+    biases.finish()
+    bias_out[...] = jnp.sum(bias_in[...], axis=0)
     conds.finish()
     cond_out[0] = cond_in[...]
     cond_swap = to_partner(cond_out.at[0], cond_out.at[1], side, x_send, x_recv, 2)
@@ -840,11 +973,12 @@
             pltpu.VMEM((groups, rows, 128), f32),
             pltpu.VMEM((groups, rows, 128), f32),
             dma((3,)), dma((3,)),
-            dma((groups, 4)), dma((groups,)),
-            dma((groups, 4)), dma((groups,)),
+            dma((groups,)), dma((groups,)),
+            dma((groups,)), dma((groups,)),
             dma((groups,)), dma((groups,)),
         ],
         compiler_params=pltpu.CompilerParams(collective_id=1, has_side_effects=True, vmem_limit_bytes=32 << 20),
+        cost_estimate=pl.CostEstimate(flops=0, bytes_accessed=0, transcendentals=0),
         name="closing",
     )(mod_pair, bias_pair, weights)
 
@@ -894,9 +1028,6 @@
     def swap(a):
         return lax.ppermute(a, "tensor", [(0, 1), (1, 0)])
 
-    def with_other(a, axis):
-        return jnp.concatenate([a, swap(a)], axis=axis)
-
     def in_order(mine, other, axis):
         return jnp.where(
             side == 0,
@@ -910,11 +1041,10 @@
     def other_latents(a, axis=0):
         return lax.dynamic_slice_in_dim(a, (1 - side) * own, own, axis)
 
-    def take(a):
-        return jnp.concatenate([own_latents(a), swap(other_latents(a))], axis=1)
-
-    def give(a):
-        return in_order(a[:, :half_seq], swap(a[:, half_seq:]), 0)
+    def placed(a, arrived):
+        mine = lax.broadcasted_iota(jnp.int32, (2, 1, 1, 1), 0) == side
+        whole = jnp.where(mine, a[None, :, :half_seq], arrived[None])
+        return whole.reshape(count, half_seq, width)
 
     cond_f = condition.astype(f32)
     cond_low = jax.nn.silu(cond_f).astype(bf16)
@@ -925,48 +1055,58 @@
         return jnp.pad(a, [(0, 0)] * (a.ndim - 1) + [(0, room - cols)])
 
     head_shard = roomy(head_weight).reshape(depth, 3 * room)
-    shards = jnp.concatenate([roomy(mix_weight.T), up_weight, down_weight.T], axis=1)
-    head_all, shards_in, latent_in, mod_parts, cond_blocks = opening(
-        cond_low, mod_weight, mod_bias, head_shard, shards, latent
-    )
+    shards = jnp.concatenate([up_weight, down_weight.T, roomy(mix_weight.T)], axis=1)
+    branch = branch_bias.astype(f32)
+    flat = [a.astype(f32).reshape(-1) for a in (head_bias, branch, up_bias)]
+    head_all, shards_in, latent_in, mod_parts, cond_blocks, biases_in = opening(
+        cond_low,
+        mod_weight,
+        mod_bias,
+        jnp.concatenate(flat).reshape(-1, 128),
+        head_shard,
+        shards,
+        latent,
+    )
+    biases_in = biases_in.reshape(-1)
+    head_bias_in = biases_in[: 2 * cols].reshape(2, cols)
+    branch_in = biases_in[2 * cols : 4 * cols].reshape(2, cols)
     head_all = head_all.reshape(width, 6 * room)
     mod_parts = mod_parts.reshape(2, 2, count, 3, cols)
     mod_parts = own_latents(mod_parts, 2).transpose(0, 2, 1, 3, 4).reshape(2, own, 6, cols)
     modulation = in_order(mod_parts[0], mod_parts[1], 2)
     cond_cols = cond_blocks[:, :count, :depth].reshape(groups * count, depth).astype(bf16)
-    branch = branch_bias.astype(f32)
-    branch_all = in_order(branch, swap(branch), 1)
+    branch_all = in_order(branch, branch_in, 1)
     row = lambda k: modulation[:, k][:, None, :]
     shift_a, scale_a, gate_a, shift_m, scale_m, gate_m = [row(k) for k in range(6)]
 
-    cuts = (0, room, room + hidden // 2, room + hidden)
+    cuts = (0, hidden // 2, hidden, hidden + room)
     pieces = [a[:, lo:hi] for lo, hi in zip(cuts, cuts[1:]) for a in (shards, shards_in)]
     rest_all = lax.all_gather(jnp.concatenate(pieces, axis=1), "dp", axis=0, tiled=True)
-    mix_t = rest_all[:, : 2 * room]
-    up_all = rest_all[:, 2 * room : 2 * room + hidden]
-    down_t = rest_all[:, 2 * room + hidden :]
-    up_bias_f = with_other(up_bias.astype(f32), 0)
+    up_all = rest_all[:, :hidden]
+    down_t = rest_all[:, hidden : 2 * hidden]
+    mix_t = rest_all[:, 2 * hidden :]
+    up_bias_f = jnp.concatenate([flat[2], biases_in[4 * cols :]])
 
     lat = jnp.concatenate([own_latents(latent), latent_in], axis=1)
-    later, _ = lax.optimization_barrier((other_latents(cotangent), latent_in))
-    upstream_low = jnp.concatenate([own_latents(cotangent), swap(later)], axis=1)
     lat_f = lat.astype(f32)
     norm1, inv1 = normed(lat_f)
     attn_in = (norm1 * (1.0 + scale_a) + shift_a).astype(bf16)
-    head_bias_f = roomy(head_bias.astype(f32))
     empty = jnp.zeros((room,), f32)
-    qkv_bias = with_other(jnp.concatenate([head_bias_f[0], empty, head_bias_f[1]]), 0)
+    qkv_bias = jnp.concatenate(
+        [c for b in (roomy(head_bias.astype(f32)), roomy(head_bias_in)) for c in (b[0], empty, b[1])]
+    )
     qkv = (mm("bsd,dc->bsc", attn_in, head_all) + qkv_bias).astype(bf16)
+    later, qkv = lax.optimization_barrier((other_latents(cotangent), qkv))
+    upstream_low = jnp.concatenate([own_latents(cotangent), swap(later)], axis=1)
     mixed, logsum = attn_fwd(qkv, heads)
     attn_out = mm("bsc,dc->bsd", mixed, mix_t) + branch_all[0]
     first = lat_f + gate_a * attn_out
     norm2, inv2 = normed(first)
     mlp_in = (norm2 * (1.0 + scale_m) + shift_m).astype(bf16)
-    pre_act = mm("bsd,df->bsf", mlp_in, up_all) + up_bias_f
-    act, gelu_back = jax.vjp(gelu_tanh, pre_act)
-    act = act.astype(bf16)
+    act, slope = up_forward(mlp_in, rest_all, up_bias_f)
     mlp_out = mm("bsf,df->bsd", act, down_t) + branch_all[1]
-    block_out = give((first + gate_m * mlp_out).astype(bf16))
+    block = (first + gate_m * mlp_out).astype(bf16)
+    block_in = swap(block[:, half_seq:])
 
     upstream = upstream_low.astype(f32)
     gate_m_grad = jnp.sum(upstream * mlp_out, axis=1)
@@ -975,11 +1115,9 @@
     down_grad = mm("bsd,bsf->df", mlp_grad, act).astype(bf16)
     down_grad, mlp_grad = lax.optimization_barrier((down_grad, mlp_grad))
     down_sum = lax.psum_scatter(down_grad, "dp", scatter_dimension=0, tiled=True)
-    pre_grad = gelu_back(mm("bsd,df->bsf", mlp_grad, down_t))[0].astype(bf16)
-    up_bias_term = jnp.sum(pre_grad, axis=(0, 1), dtype=f32)
+    pre_grad, up_bias_term = down_backward(mlp_grad, rest_all, slope)
     up_grad = mm("bsd,bsf->df", mlp_in, pre_grad).astype(bf16)
     up_grad, pre_grad = lax.optimization_barrier((up_grad, pre_grad))
-    up_sum = lax.psum_scatter(up_grad, "dp", scatter_dimension=0, tiled=True)
     mlp_in_grad = mm("bsf,df->bsd", pre_grad, up_all)
     shift_m_grad = jnp.sum(mlp_in_grad, axis=1)
     scale_m_grad = jnp.sum(mlp_in_grad * norm2, axis=1)
@@ -989,18 +1127,23 @@
     attn_grad = (gate_a * first_grad).astype(bf16)
     mixed_grad = mm("bsd,dc->bsc", attn_grad, mix_t).astype(bf16)
     mix_grad = mm("bsd,bsc->dc", attn_grad, mixed).astype(bf16)
-    mix_grad, mixed_grad = lax.optimization_barrier((mix_grad, mixed_grad))
-    mix_sum = lax.psum_scatter(mix_grad, "dp", scatter_dimension=0, tiled=True)
+    up_grad = jnp.concatenate([up_grad, mix_grad], axis=1)
+    up_grad, mixed_grad = lax.optimization_barrier((up_grad, mixed_grad))
+    up_sum = lax.psum_scatter(up_grad, "dp", scatter_dimension=0, tiled=True)
+    mixed_grad, down_sum = lax.optimization_barrier((mixed_grad, down_sum))
     qkv_grad = attn_bwd(qkv, mixed_grad, mixed, logsum, heads)
     head_grad = mm("bsd,bsc->dc", attn_in, qkv_grad).astype(bf16)
     head_grad, qkv_grad = lax.optimization_barrier((head_grad, qkv_grad))
     head_sum = lax.psum_scatter(head_grad, "dp", scatter_dimension=0, tiled=True)
+    qkv_grad, up_sum, block_in = lax.optimization_barrier((qkv_grad, up_sum, block_in))
+    block_out = placed(block, block_in)
     qkv_bias_term = jnp.sum(qkv_grad, axis=(0, 1), dtype=f32)
     attn_in_grad = mm("bsc,dc->bsd", qkv_grad, head_all)
     shift_a_grad = jnp.sum(attn_in_grad, axis=1)
     scale_a_grad = jnp.sum(attn_in_grad * norm1, axis=1)
     lat_grad = first_grad + normed_back(attn_in_grad * (1.0 + scale_a), norm1, inv1)
-    latent_grad = give(lat_grad.astype(bf16))
+    lat_grad = lat_grad.astype(bf16)
+    lat_grad_in = swap(lat_grad[:, half_seq:])
 
     mod_low = jnp.stack(
         [shift_a_grad, scale_a_grad, gate_a_grad, shift_m_grad, scale_m_grad, gate_m_grad], axis=1
@@ -1020,11 +1163,14 @@
         flat = jnp.concatenate([head_term[k].reshape(-1), branch_cols.reshape(-1), ups[k]])
         return flat.reshape(-1, 128)
 
+    mod_pair = jnp.stack([mod_share(side), mod_share(1 - side)])
+    mod_pair, lat_grad = lax.optimization_barrier((mod_pair, lat_grad))
     mod_blocks, biases, cond_parts = closing(
-        jnp.stack([mod_share(side), mod_share(1 - side)]),
+        mod_pair,
         jnp.stack([bias_share(side, 0), bias_share(1 - side, 1)]),
         mod_weight,
     )
+    latent_grad = placed(lat_grad, lat_grad_in)
     biases = biases.reshape(-1)
     mod_rows = mod_blocks.astype(bf16).reshape(groups, 2, count, 3, cols)
     mod_rows = mod_rows.transpose(0, 2, 1, 3, 4).reshape(groups * count, 6, cols)
@@ -1040,8 +1186,8 @@
         return mine.astype(f32) + swap(other).astype(f32)
 
     head_weight_grad = joined(head_sum, 1).reshape(depth, 3, room)[..., :cols]
-    mix_weight_grad = joined(mix_sum, 1)[:, :cols].T
-    up_weight_grad = joined(up_sum, 1)
+    mix_weight_grad = joined(up_sum[:, hidden:], 1)[:, :cols].T
+    up_weight_grad = joined(up_sum[:, :hidden], 1)
     down_weight_grad = joined(down_sum, 1).T
     return (
         block_out,

time: 1030 us -> 830 us (0.81)
  waiting for transfers between devices: 199 us -> 73.5 us
  matrix products: 358 us -> 250 us
  Pallas kernels: 332 us -> 356 us
    reduce_scatter x1, waiting for transfers between devices: 121 us -> 2.27 us  [body_by_latents(): up_sum = lax.psum_scatter(up_grad, 'dp', scatter_dimension=0, tiled=True)]
    dot_general x13 -> x11, matrix products: 358 us -> 250 us  [mm(): return jnp.einsum(spec, a, b, preferred_element_type=f32)]
    pallas_call x1 -> x3, Pallas kernels: 84.5 us -> 161 us  [the longest x1 85 us: opening(): pl.pallas_call(opening_kernel, in_specs=[vmem, vmem, vmem, vmem, anywhere...]
    pallas_call x1, Pallas kernels: 77.7 us -> 35.1 us  [closing(): pl.pallas_call(closing_kernel, in_specs=[vmem, vmem, vmem], out_specs=[vm...]
    reduce_scatter x1, waiting for transfers between devices: 20.3 us -> 0.92 us  [body_by_latents(): lax.psum_scatter(down_grad, 'dp', scatter_dimension=0, tiled=True)]
    select_n x4 -> x2, other arithmetic: 13.7 us -> 0.21 us  [in_order(): jnp.where(side == 0, jnp.concatenate([mine, other], axis=axis), jnp.conca...]
    all_gather x1, waiting for transfers between devices: 11.4 us -> 23.5 us  [body_by_latents(): lax.all_gather(jnp.concatenate(pieces, axis=1), 'dp', axis=0, tiled=True)]
    reduce_scatter x1, waiting for transfers between devices: 0.01 us -> 11.1 us  [body_by_latents(): lax.psum_scatter(head_grad, 'dp', scatter_dimension=0, tiled=True)]
  transfers between devices with their start and end apart: 15 -> 11, of which waited for: 5 -> 6; matrix products, arithmetic and copies ran while one was open for 16% -> 33% of each run, Pallas kernels for 24% -> 24%
where the time goes in v3:
time: 830 us; the launch traced here: 823 us
  Pallas kernels  356 us (43%)
  matrix products  250 us (30%)
  waiting for transfers between devices  73.5 us (9%)
  local copies, waits for them, and re-layouts  60.3 us (7%)
  other arithmetic  59.8 us (7%)
  between operations  15.1 us (2%)
    dot_general x11, matrix products, mm(): return jnp.einsum(spec, a, b, preferred_element_type=f32)  250 us
    pallas_call x1, Pallas kernels, attn_bwd(): pl.pallas_call(partial(attn_bwd_kernel, blk=blk, heads=heads), grid=(n, 2...  114 us
    pallas_call x1, Pallas kernels, opening(): pl.pallas_call(opening_kernel, in_specs=[vmem, vmem, vmem, vmem, anywhere...  85 us
    pallas_call x1, Pallas kernels, attn_fwd(): pl.pallas_call(partial(attn_fwd_kernel, blk=blk, heads=heads), grid=(n, 2...  46.2 us
    pallas_call x1, Pallas kernels, up_forward(): pl.pallas_call(up_forward_kernel, grid=(hidden // cols, count * seq // ro...  43.2 us
    ppermute x7, waiting for transfers between devices, swap(): return lax.ppermute(a, 'tensor', [(0, 1), (1, 0)])  35.7 us
    pallas_call x1, Pallas kernels, closing(): pl.pallas_call(closing_kernel, in_specs=[vmem, vmem, vmem], out_specs=[vm...  35.1 us
    pallas_call x1, Pallas kernels, down_backward(): pl.pallas_call(down_backward_kernel, grid=(hidden // cols, count * seq //...  32.5 us
  transfers between devices with their start and end apart: 11, of which 6 were waited for; matrix products, arithmetic and copies ran while one was open for 33% of the time, Pallas kernels for 24%

profile of v3, /device:TPU:0, one launch (start us, length us, event | category | flops | bytes accessed | tf_op | source)
XLA Modules:
  0.0 823.4 jit_solution(6247454788307561468)
XLA Ops:
  7.2 1.1 copy.77
  11.5 1.1 copy.98
  12.6 0.9 pad.30
  13.7 0.8 reshape.229
  16.0 1.8 constant_dynamic-update-slice_fusion.3
  17.8 1.1 pad_maximum_fusion.3.rest_ref
  19.0 2.3 copy-done.2
  21.3 0.8 copy-done.3
  22.1 85.0 %opening.1 = (bf16[16,72,3840]{2,1,0:T(8,128)(2,1)S(1)}, bf16[72,5248]{1,0:T(8,128)(2,1)S(1)}, bf16[2,512,1152]{2,1,0:T(8,128)(2,1)S(1)}, f32[2,8,1728]{2,1,0:T(...) custom-call(f32[16,8,128]{2,1,0:T(8,128)S(1)} %fusion.28.cond_ref, ...), custom_call_target="tpu_custom_call" | custom-call | tf_op jit(solution)/shard_map/opening/pallas_call | solution.py:880
  109.0 3.5 copy-done.8
  113.2 0.8 constant_dynamic-update-slice_fusion.2
  116.9 1.0 reshape.208
  119.0 6.7 constant_dynamic-slice_fusion.2
  126.4 1.7 fusion.18
  128.5 26.5 %add_convert_fusion.q_ref.k_ref.v_ref = bf16[2,1024,3840]{2,1,0:T(8,128)(2,1)} fusion(f32[3840]{0:T(1024)S(1)} %constant_dynamic-update-slice_fusion.10, bf16[1152,3840,1]{1,0,2:T(8,128)(2,1)S(1)} %bitcast.133, f32[2,1152]{1,0:T(2,128)S(1)} %get-tuple-element.166, f32[2,1152]{1,0:T(2,128)S(1)} %get-tuple-element.167, f32[2,1024]{1,0:T(2,128)S(1)} %add_rsqrt_fusion.1, ...), kind=kOutput, calls=%fused_computation.1 | convolution fusion | flops 18156355584 | bytes 29344768 | tf_op jit(solution)/shard_map/bsd,dc->bsc/dot_general | solution.py:1002
  155.0 1.1 collective-permute-start
  157.5 46.2 %attention_forward.1 = (bf16[2,1024,1280]{2,1,0:T(8,128)(2,1)}, f32[2,2,8,1024]{3,2,1,0:T(8,128)}) custom-call(bf16[2,1024,3840]{2,1,0:T(8,128)(2,1)} %add_convert_fusion.q_ref.k_ref.v_ref, bf16[2,1024,3840]{2,1,0:T(8,128)(2,1)} %add_convert_fusion.q_ref.k_ref.v_ref, bf16[2,1024,3840]{2,1,0:T(8,128)(2,1)} %add_convert_fusion.q_ref.k_ref.v_ref), custom_call_target="tpu_custom_call" | custom-call | flops 10737418240 | bytes 20971520 | tf_op jit(solution)/shard_map/attention_forward/pallas_call | solution.py:399
  203.8 4.9 collective-permute-done
  208.7 4.8 fusion.19
  213.4 23.5 %all-gather.2.cloned.1.call-done.w_ref = bf16[1152,10496]{1,0:T(8,128)(2,1)} async-done(((bf16[72,10496]{1,0:T(8,128)(2,1)}), bf16[1152,10496]{1,0:T(8,128)(2,1)}) %all-gather.2.cloned.1.call-update) | async-done | bytes 24182800 | tf_op jit(solution)/shard_map/all_gather | solution.py:1084
  236.9 12.6 %fusion.45 = (f32[2,1024]{1,0:T(2,128)S(1)}, f32[2,1024,1152]{2,1,0:T(8,128)S(1)}, f32[2,1024,1152]{2,1,0:T(8,128)}) fusion(f32[1152]{0:T(1024)S(1)} %get-tuple-element.141, f32[2,1152]{1,0:T(2,128)S(1)} %get-tuple-element.168, bf16[2,512,1152]{2,1,0:T(8,128)(2,1)S(1)} %get-tuple-element.44, bf16[2,512,1152]{2,1,0:T(8,128)(2,1)} %copy-done.10, ...), kind=kOutput, calls=%fused_computation.155 | convolution fusion | flops 6058670080 | bytes 31806976 | tf_op jit(solution)/shard_map/bsc,dc->bsd/dot_general | solution.py:1002
  249.5 1.1 multiply_reduce_fusion.3
  250.6 3.7 add_convert_fusion.2
  254.5 43.2 %up_forward.1 = (bf16[2048,4608]{1,0:T(8,128)(2,1)}, bf16[2048,4608]{1,0:T(8,128)(2,1)}) custom-call(bf16[2048,1152]{1,0:T(8,128)(2,1)} %bitcast.138, bf16[1152,10496]{1,0:T(8,128)(2,1)} %all-gather.2.cloned.1.call-done.w_ref, f32[1,4608]{1,0:T(1,128)} %reshape.213.b_ref), custom_call_target="tpu_custom_call" | custom-call | flops 21743271936 | bytes 37748736 | tf_op jit(solution)/shard_map/up_forward/pallas_call | solution.py:534
  297.8 27.8 %fusion = bf16[1152,4608]{1,0:T(8,128)(2,1)} fusion(bf16[2,1024,1152]{2,1,0:T(8,128)(2,1)S(1)} %bitcast.137, bf16[2,1024,4608]{2,1,0:T(8,128)(2,1)} %bitcast.152), kind=kOutput, calls=%fused_computation.4 | convolution fusion | flops 21748580352 | bytes 34209792 | tf_op jit(solution)/shard_map/bsd,bsf->df/dot_general | solution.py:1002
  325.6 32.5 %down_backward.1 = (bf16[2048,4608]{1,0:T(8,128)(2,1)}, f32[1,4608]{1,0:T(1,128)}) custom-call(bf16[2048,1152]{1,0:T(8,128)(2,1)} %bitcast.135, bf16[1152,10496]{1,0:T(8,128)(2,1)} %all-gather.2.cloned.1.call-done.w_ref, bf16[2048,4608]{1,0:T(8,128)(2,1)} %get-tuple-element.54.slope_ref), custom_call_target="tpu_custom_call" | custom-call | flops 21743271936 | bytes 37748736 | tf_op jit(solution)/shard_map/down_backward/pallas_call | solution.py:578
  358.1 27.5 %fusion.1 = bf16[1152,4608]{1,0:T(8,128)(2,1)} fusion(bf16[2,1024,1152]{2,1,0:T(8,128)(2,1)S(1)} %copy-done.16, bf16[2,1024,4608]{2,1,0:T(8,128)(2,1)} %bitcast.154), kind=kOutput, calls=%fused_computation.5 | convolution fusion | flops 21748580352 | bytes 34209792 | tf_op jit(solution)/shard_map/bsd,bsf->df/dot_general | solution.py:1002
  385.7 35.4 %multiply_reduce_fusion = (bf16[2,1152]{1,0:T(2,128)(2,1)}, f32[2,1024]{1,0:T(2,128)S(1)}, f32[2,1024]{1,0:T(2,128)S(1)}, bf16[2,1152]{1,0:T(2,128)(2,1)}, f32[2,1024,1152]{2,1,0:T(8,128)}) fusion(f32[2,1024,1152]{2,1,0:T(8,128)} %copy-done.9, f32[2,1024]{1,0:T(2,128)S(1)} %add_rsqrt_fusion, f32[2,1024]{1,0:T(2,128)S(1)} %broadcast_multiply_fusion.4, ...), kind=kOutput, calls=%fused_computation.36 | convolution fusion | flops 21764497408 | bytes 48416768 | tf_op jit(solution)/shard_map/bsf,df->bsd/dot_general | solution.py:1002
  421.2 39.4 %convert_reduce_fusion.1 = (f32[2,1152]{1,0:T(2,128)S(1)}, bf16[2,1152]{1,0:T(2,128)(2,1)S(1)}, bf16[2,1024,1152]{2,1,0:T(8,128)(2,1)}, bf16[2,1152]{1,0:T(2,128...) fusion(bf16[2,512,1152]{2,1,0:T(8,128)(2,1)} %collective-permute-done, ...), kind=kOutput, calls=%fused_computation.7 | convolution fusion | flops 21797527552 | bytes 76765184 | tf_op jit(solution)/shard_map/bsf,df->bsd/dot_general | solution.py:1002
  460.6 12.5 %convolution_convert_fusion.do_ref = bf16[2,1024,1280]{2,1,0:T(8,128)(2,1)} fusion(bf16[1152,10496]{1,0:T(8,128)(2,1)} %all-gather.2.cloned.1.call-done.w_ref, f32[2,1024,1152]{2,1,0:T(8,128)} %get-tuple-element.152, f32[2,1152]{1,0:T(2,128)S(1)} %copy-done.44), kind=kOutput, calls=%fused_computation.48 | convolution fusion | flops 6047137792 | bytes 17638400 | tf_op jit(solution)/shard_map/bsd,dc->bsc/dot_general | solution.py:1002
  473.1 9.2 %fusion.21 = bf16[1152,1280]{1,0:T(8,128)(2,1)S(1)} fusion(bf16[2,1024,1280]{2,1,0:T(8,128)(2,1)} %get-tuple-element.49.o_ref, f32[2,1024,1152]{2,1,0:T(8,128)S(1)} %copy-done.15, f32[2,1152]{1,0:T(2,128)S(1)} %copy-done.44), kind=kOutput, calls=%fused_computation.47 | convolution fusion | flops 6045990912 | bytes 17638400 | tf_op jit(solution)/shard_map/bsd,bsc->dc/dot_general | solution.py:1002
  482.3 11.8 %pad_maximum_fusion = bf16[1152,5888]{1,0:T(8,128)(2,1)} fusion(bf16[1152,1280]{1,0:T(8,128)(2,1)S(1)} %fusion.21, bf16[1152,4608]{1,0:T(8,128)(2,1)} %fusion.1), kind=kLoop, calls=%fused_computation.14 | loop fusion | flops 27131904 | bytes 27131904 | tf_op jit(solution)/shard_map/concatenate | solution.py:1130
  494.2 1.5 slice.247
  495.8 5.0 fusion.46
  500.8 1.4 collective-permute-start.1
  505.1 0.9 reduce-scatter.4.cloned.1.call-done
  506.0 1.7 split.31
  507.8 1.5 collective-permute-start.6
  509.3 114.3 %attention_backward.1 = bf16[2,1024,3840]{2,1,0:T(8,128)(2,1)} custom-call(bf16[2,1024,3840]{2,1,0:T(8,128)(2,1)} %add_convert_fusion.q_ref.k_ref.v_ref, bf16[2,1024,3840]{2,1,0:T(8,128)(2,1)} %add_convert_fusion.q_ref.k_ref.v_ref, bf16[2,1024,3840]{2,1,0:T(8,128)(2,1)} %add_convert_fusion.q_ref.k_ref.v_ref, ...), custom_call_target="tpu_custom_call" | custom-call | tf_op jit(solution)/shard_map/attention_backward/pallas_call | solution.py:480
  623.7 24.8 %bitcast_convert_fusion = bf16[1152,3840]{1,0:T(8,128)(2,1)} fusion(bf16[2,1024,3840]{2,1,0:T(8,128)(2,1)} %attention_backward.1, f32[2,1152]{1,0:T(2,128)S(1)} %copy-done.42, f32[2,1152]{1,0:T(2,128)S(1)} %copy-done.29, f32[2,1024]{1,0:T(2,128)S(1)} %copy-done.38, f32[2,1024]{1,0:T(2,128)S(1)} %copy-done.24, bf16[2,512,1152]{2,1,0:T(8,128)(2,1)S(1)} %copy-done.1, ...), kind=kOutput, calls=%fused_computation.6 | convolution fusion | flops 18145050624 | bytes 29329408 | tf_op jit(solution)/shard_map/bsd,bsc->dc/dot_general | solution.py:1002
  648.5 2.0 add_bitcast_fusion
  650.5 2.3 reduce-scatter.6.cloned.1.call-done
  652.8 1.6 fusion.47
  654.4 1.7 split.29
  656.1 1.5 collective-permute-start.5
  658.1 6.9 convert_reduce_fusion
  666.4 32.1 %fusion.12 = (bf16[2,1152]{1,0:T(2,128)(2,1)S(1)}, f32[2,1024]{1,0:T(2,128)}, f32[2,1024]{1,0:T(2,128)}, bf16[2,1152]{1,0:T(2,128)(2,1)S(1)}, f32[2,1024,1152]{2,1,0:T(8,128)}) fusion(f32[2,1024]{1,0:T(2,128)S(1)} %copy-done.38, f32[2,1024]{1,0:T(2,128)S(1)} %copy-done.24, bf16[2,512,1152]{2,1,0:T(8,128)(2,1)S(1)} %copy-done.1, ...), kind=kOutput, calls=%fused_computation.27 | convolution fusion | flops 18150055936 | bytes 38782976 | tf_op jit(solution)/shard_map/bsc,dc->bsd/dot_general | solution.py:1002
  700.4 0.8 stack_reshape.13
  702.7 9.5 %fusion.17 = bf16[2,1024,1152]{2,1,0:T(8,128)(2,1)S(1)} fusion(f32[2,1024,1152]{2,1,0:T(8,128)} %get-tuple-element.152, f32[2,1024,1152]{2,1,0:T(8,128)} %get-tuple-element.181, f32[2,1024]{1,0:T(2,128)S(1)} %broadcast_multiply_fusion, f32[2,1024]{1,0:T(2,128)S(1)} %broadcast_multiply_fusion.1, f32[2,1152]{1,0:T(2,128)} %copy-done.28, ...), kind=kLoop, calls=%fused_computation.32 | loop fusion | flops 30670848 | bytes 28353536 | tf_op jit(solution)/shard_map/convert_element_type | solution.py:1145
  712.2 1.7 slice.194
  714.1 35.1 %closing.1 = (f32[16,8,1728]{2,1,0:T(8,128)S(1)}, f32[36,128]{1,0:T(8,128)S(1)}, f32[2,16,8,128]{3,2,1,0:T(8,128)S(1)}) custom-call(f32[2,8,1728]{2,1,0:T(8,128)S(1)} %pad_maximum_fusion.4.mod_ref, f32[2,36,128]{2,1,0:T(8,128)S(1)} %pad_maximum_fusion.5.bias_ref, bf16[2,128,1728]{2,1,0:T(8,128)(2,1)S(1)} %pad_bitcast_fusion.mod_w_ref), custom_call_target="tpu_custom_call" | custom-call | tf_op jit(solution)/shard_map/closing/pallas_call | solution.py:960
  749.2 0.8 convert_element_type.137
  750.0 1.7 reshape.223
  751.7 1.0 copy.91
  752.7 2.1 reshape.224
  756.0 2.4 fusion.52
  761.2 1.6 add_bitcast_fusion.1
  762.8 11.1 %reduce-scatter.8.cloned.1.call-done = bf16[72,3840]{1,0:T(8,128)(2,1)} async-done(((bf16[1152,3840]{1,0:T(8,128)(2,1)}), bf16[72,3840]{1,0:T(8,128)(2,1)}) %reduce-scatter.8.cloned.1.call-update) | async-done | bytes 552976 | tf_op jit(solution)/shard_map/reduce_scatter | solution.py:1137
  773.9 1.0 split.33
  774.9 1.5 collective-permute-start.3
  776.4 2.0 convert_add_fusion.2
  778.4 30.8 %collective-permute-done.2 = bf16[2,512,1152]{2,1,0:T(8,128)(2,1)} collective-permute-done((bf16[2,512,1152]{2,1,0:T(8,128)(2,1)}, bf16[2,512,1152]{2,1,0:T(8,128)(2,1)}, u32[]{:S(2)}, u32[]{:S(2)}) %collective-permute-start.2) | collective-permute-done | bytes 2359328 | tf_op jit(solution)/shard_map/ppermute | solution.py:1029
  809.2 6.3 bitcast_select_fusion
  815.8 0.8 copy.92
  (224 shorter events, 26.6 us)
Async XLA Ops:
  7.2 229.7 %all-gather.2.cloned.1.call-start = ((), (), s32[]{:S(2)}) async-start(), calls=%async_computation.3 | async-start | bytes 25694208 | tf_op jit(solution)/shard_map/all_gather | solution.py:1084
  9.9 9.0 %copy-start.21 = (f32[2304]{0:T(1024)}, f32[2304]{0:T(1024)S(1)}, u32[]{:S(2)}) copy-start(f32[2304]{0:T(1024)S(1)} %convert_element_type.119) | copy-start | bytes 27652
  16.0 97.3 %copy-start.17 = (bf16[2304,72]{0,1:T(8,128)(2,1)S(1)}, bf16[2304,72]{0,1:T(8,128)(2,1)}, u32[]{:S(2)}) copy-start(bf16[2304,72]{0,1:T(8,128)(2,1)} %param.23) | copy-start | bytes 995332
  16.0 98.8 %copy-start.19 = (bf16[576,72]{0,1:T(8,128)(2,1)S(1)}, bf16[576,72]{0,1:T(8,128)(2,1)}, u32[]{:S(2)}) copy-start(bf16[576,72]{0,1:T(8,128)(2,1)} %param.19) | copy-start | bytes 248836
  19.0 2.3 copy-start.2
  21.3 0.8 copy-start.3
  107.1 0.6 copy-start.4
  108.3 0.6 copy-start.7
  109.0 3.5 copy-start.8
  112.4 124.4 %copy-start = (bf16[2,512,1152]{2,1,0:T(8,128)(2,1)}, bf16[2,512,1152]{2,1,0:T(8,128)(2,1)S(1)}, u32[]{:S(2)}) copy-start(bf16[2,512,1152]{2,1,0:T(8,128)(2,1)S(1)} %get-tuple-element.44) | copy-start | bytes 7077892
  116.1 389.9 %reduce-scatter.4.cloned.1.call-start = ((), (), s32[]{:S(2)}) async-start(), calls=%async_computation.4 | async-start | bytes 11280384 | tf_op jit(solution)/shard_map/reduce_scatter | solution.py:1117
  119.0 9.4 %slice-start = ((s8[8847360]{0:T(1024)(128)(4,1)}), s8[4194304]{0:T(1024)(128)(4,1)S(1)}, s32[]{:S(2)}) async-start(s8[8847360]{0:T(1024)(128)(4,1)} %bitcast.131), calls=%async_computation.7 | async-start | bytes 8388608
  119.0 9.4 %slice-start.1 = ((s8[8847360]{0:T(1024)(128)(4,1)}), s8[4194304]{0:T(1024)(128)(4,1)S(1)}, s32[]{:S(2)}) async-start(s8[8847360]{0:T(1024)(128)(4,1)} %bitcast.131), calls=%async_computation.8 | async-start | bytes 8388608
  125.7 2.7 copy-start.10
  125.7 2.7 slice-start.2
  126.4 28.5 %copy-start.23 = (f32[2,1024]{1,0:T(2,128)}, f32[2,1024]{1,0:T(2,128)S(1)}, u32[]{:S(2)}) copy-start(f32[2,1024]{1,0:T(2,128)S(1)} %broadcast_multiply_fusion.5) | copy-start | bytes 24580
  128.2 26.8 %copy-start.37 = (f32[2,1024]{1,0:T(2,128)}, f32[2,1024]{1,0:T(2,128)S(1)}, u32[]{:S(2)}) copy-start(f32[2,1024]{1,0:T(2,128)S(1)} %add_rsqrt_fusion.1) | copy-start | bytes 24580
  128.3 26.6 %copy-start.20 = (f32[2,6,1152]{2,0,1:T(2,128)}, f32[2,6,1152]{2,0,1:T(2,128)S(1)}, u32[]{:S(2)}) copy-start(f32[2,6,1152]{2,0,1:T(2,128)S(1)} %maximum_select_fusion) | copy-start | bytes 165892
  128.3 26.6 %copy-start.28 = (f32[2,1152]{1,0:T(2,128)}, f32[2,1152]{1,0:T(2,128)S(1)}, u32[]{:S(2)}) copy-start(f32[2,1152]{1,0:T(2,128)S(1)} %get-tuple-element.167) | copy-start | bytes 27652
  128.4 26.6 %copy-start.41 = (f32[2,1152]{1,0:T(2,128)}, f32[2,1152]{1,0:T(2,128)S(1)}, u32[]{:S(2)}) copy-start(f32[2,1152]{1,0:T(2,128)S(1)} %get-tuple-element.166) | copy-start | bytes 27652
  128.4 80.3 %copy-start.30 = (f32[2,1152]{1,0:T(2,128)}, f32[2,1152]{1,0:T(2,128)S(1)}, u32[]{:S(2)}) copy-start(f32[2,1152]{1,0:T(2,128)S(1)} %get-tuple-element.163) | copy-start | bytes 27652
  128.4 108.5 %copy-start.43 = (f32[2,1152]{1,0:T(2,128)}, f32[2,1152]{1,0:T(2,128)S(1)}, u32[]{:S(2)}) copy-start(f32[2,1152]{1,0:T(2,128)S(1)} %get-tuple-element.168) | copy-start | bytes 27652
  128.4 27.7 %copy-start.40 = (bf16[2,576]{1,0:T(2,128)(2,1)S(1)}, bf16[2,576]{1,0:T(2,128)(2,1)}, u32[]{:S(2)}) copy-start(bf16[2,576]{1,0:T(2,128)(2,1)} %param.20) | copy-start | bytes 6916
  128.5 27.7 %copy-start.6 = (f32[36,128]{1,0:T(8,128)S(1)}, f32[36,128]{1,0:T(8,128)}, u32[]{:S(2)}) copy-start(f32[36,128]{1,0:T(8,128)} %copy-done.5) | copy-start | bytes 55300
  128.5 27.7 %copy-start.22 = (f32[2304]{0:T(1024)S(1)}, f32[2304]{0:T(1024)}, u32[]{:S(2)}) copy-start(f32[2304]{0:T(1024)} %copy-done.21) | copy-start | bytes 27652
  155.0 53.7 %collective-permute-start = (bf16[2,512,1152]{2,1,0:T(8,128)(2,1)}, bf16[2,512,1152]{2,1,0:T(8,128)(2,1)}, u32[]{:S(2)}, u32[]{:S(2)}) collective-permute-start(bf16[2,512,1152]{2,1,0:T(8,128)(2,1)} %get-tuple-element.52), channel_id=1, source_target_pairs={{0,1},{1,0},{2,3},{3,2},{4,5},{5,4},{6,7},{7,6},{8,9},{9,8},{10,11... | collective-permute-start | bytes 7077896 | tf_op jit(solution)/shard_map/ppermute | solution.py:1029
  157.5 51.1 %copy-start.13 = (bf16[2,512,1152]{2,1,0:T(8,128)(2,1)S(1)}, bf16[2,512,1152]{2,1,0:T(8,128)(2,1)}, u32[]{:S(2)}) copy-start(bf16[2,512,1152]{2,1,0:T(8,128)(2,1)} %get-tuple-element.155) | copy-start | bytes 7077892
  249.5 5.0 copy-start.9
  250.6 47.1 %slice-start.4 = ((s8[4718592]{0:T(1024)(128)(4,1)}), s8[524288]{0:T(1024)(128)(4,1)S(1)}, s32[]{:S(2)}) async-start(s8[4718592]{0:T(1024)(128)(4,1)} %bitcast.136), calls=%async_computation.11 | async-start | bytes 1048576
  254.5 43.3 %slice-start.5 = ((s8[4718592]{0:T(1024)(128)(4,1)}), s8[4194304]{0:T(1024)(128)(4,1)S(1)}, s32[]{:S(2)}) async-start(s8[4718592]{0:T(1024)(128)(4,1)} %bitcast.136), calls=%async_computation.12 | async-start | bytes 8388608
  325.6 32.5 %copy-start.16 = (bf16[2,1024,1152]{2,1,0:T(8,128)(2,1)S(1)}, bf16[2,1024,1152]{2,1,0:T(8,128)(2,1)}, u32[]{:S(2)}) copy-start(bf16[2,1024,1152]{2,1,0:T(8,128)(2,1)} %add_convert_fusion.2) | copy-start | bytes 14155780
  385.6 35.5 %copy-start.14 = (bf16[2,512,1152]{2,1,0:T(8,128)(2,1)S(1)}, bf16[2,512,1152]{2,1,0:T(8,128)(2,1)}, u32[]{:S(2)}) copy-start(bf16[2,512,1152]{2,1,0:T(8,128)(2,1)} %get-tuple-element.155) | copy-start | bytes 7077892
  385.7 35.5 %copy-start.31 = (f32[2,1152]{1,0:T(2,128)S(1)}, f32[2,1152]{1,0:T(2,128)}, u32[]{:S(2)}) copy-start(f32[2,1152]{1,0:T(2,128)} %copy-done.30) | copy-start | bytes 27652
  385.7 35.5 %copy-start.45 = (f32[1152]{0:T(1024)S(1)}, f32[1152]{0:T(1024)}, u32[]{:S(2)}) copy-start(f32[1152]{0:T(1024)} %get-tuple-element.140) | copy-start | bytes 13828
  385.7 267.1 %reduce-scatter.6.cloned.1.call-start = ((), (), s32[]{:S(2)}) async-start(), calls=%async_computation.5 | async-start | bytes 14413824 | tf_op jit(solution)/shard_map/reduce_scatter | solution.py:1132
  421.2 39.4 %copy-start.44 = (f32[2,1152]{1,0:T(2,128)S(1)}, f32[2,1152]{1,0:T(2,128)}, u32[]{:S(2)}) copy-start(f32[2,1152]{1,0:T(2,128)} %copy-done.43) | copy-start | bytes 27652
  460.6 12.5 %copy-start.15 = (f32[2,1024,1152]{2,1,0:T(8,128)S(1)}, f32[2,1024,1152]{2,1,0:T(8,128)}, u32[]{:S(2)}) copy-start(f32[2,1024,1152]{2,1,0:T(8,128)} %get-tuple-element.152) | copy-start | bytes 28311556
  494.1 10.3 %copy-start.39 = (f32[1,4608]{1,0:T(1,128)S(1)}, f32[1,4608]{1,0:T(1,128)}, u32[]{:S(2)}) copy-start(f32[1,4608]{1,0:T(1,128)} %get-tuple-element.68) | copy-start | bytes 55300
  494.2 279.7 %reduce-scatter.8.cloned.1.call-start = ((), (), s32[]{:S(2)}) async-start(), calls=%async_computation.6 | async-start | bytes 9400320 | tf_op jit(solution)/shard_map/reduce_scatter | solution.py:1137
  500.8 149.7 %collective-permute-start.1 = (bf16[2,512,1152]{2,1,0:T(8,128)(2,1)}, bf16[2,512,1152]{2,1,0:T(8,128)(2,1)}, u32[]{:S(2)}, u32[]{:S(2)}) collective-permute-start(bf16[2,512,1152]{2,1,0:T(8,128)(2,1)} %get-tuple-element.154), channel_id=1, source_target_pairs={{0,1},{1,0},{2,3},{3,2},{4,5},{5,4},{6,7},{7,6},{8,9},{9,8},{10,11... | collective-permute-start | bytes 7077896 | tf_op jit(solution)/shard_map/ppermute | solution.py:1029
  507.8 140.8 %collective-permute-start.6 = (bf16[72,2304]{1,0:T(8,128)(2,1)}, bf16[72,2304]{1,0:T(8,128)(2,1)}, u32[]{:S(2)}, u32[]{:S(2)}) collective-permute-start(bf16[72,2304]{1,0:T(8,128)(2,1)} %split.31), channel_id=1, source_target_pairs={{0,1},{1,0},{2,3},{3,2},{4,5},{5,4},{6,7},{7,6},{8,9},{9,8},{10,11... | collective-permute-start | bytes 995336 | tf_op jit(solution)/shard_map/ppermute | solution.py:1029
  509.2 114.4 %copy-start.1 = (bf16[2,512,1152]{2,1,0:T(8,128)(2,1)S(1)}, bf16[2,512,1152]{2,1,0:T(8,128)(2,1)}, u32[]{:S(2)}) copy-start(bf16[2,512,1152]{2,1,0:T(8,128)(2,1)} %copy-done) | copy-start | bytes 7077892
  509.2 114.4 %copy-start.11 = (bf16[2,512,1152]{2,1,0:T(8,128)(2,1)S(1)}, bf16[2,512,1152]{2,1,0:T(8,128)(2,1)}, u32[]{:S(2)}) copy-start(bf16[2,512,1152]{2,1,0:T(8,128)(2,1)} %copy-done.10) | copy-start | bytes 7077892
  509.2 114.4 %copy-start.24 = (f32[2,1024]{1,0:T(2,128)S(1)}, f32[2,1024]{1,0:T(2,128)}, u32[]{:S(2)}) copy-start(f32[2,1024]{1,0:T(2,128)} %copy-done.23) | copy-start | bytes 24580
  509.2 114.4 %copy-start.29 = (f32[2,1152]{1,0:T(2,128)S(1)}, f32[2,1152]{1,0:T(2,128)}, u32[]{:S(2)}) copy-start(f32[2,1152]{1,0:T(2,128)} %copy-done.28) | copy-start | bytes 27652
  509.3 114.4 %copy-start.38 = (f32[2,1024]{1,0:T(2,128)S(1)}, f32[2,1024]{1,0:T(2,128)}, u32[]{:S(2)}) copy-start(f32[2,1024]{1,0:T(2,128)} %copy-done.37) | copy-start | bytes 24580
  509.3 114.4 %copy-start.42 = (f32[2,1152]{1,0:T(2,128)S(1)}, f32[2,1152]{1,0:T(2,128)}, u32[]{:S(2)}) copy-start(f32[2,1152]{1,0:T(2,128)} %copy-done.41) | copy-start | bytes 27652
  656.1 120.3 %collective-permute-start.5 = (bf16[72,2304]{1,0:T(8,128)(2,1)}, bf16[72,2304]{1,0:T(8,128)(2,1)}, u32[]{:S(2)}, u32[]{:S(2)}) collective-permute-start(bf16[72,2304]{1,0:T(8,128)(2,1)} %split.29), channel_id=1, source_target_pairs={{0,1},{1,0},{2,3},{3,2},{4,5},{5,4},{6,7},{7,6},{8,9},{9,8},{10,11... | collective-permute-start | bytes 995336 | tf_op jit(solution)/shard_map/ppermute | solution.py:1029
  657.6 103.6 %collective-permute-start.4 = (bf16[72,640]{1,0:T(8,128)(2,1)}, bf16[72,640]{1,0:T(8,128)(2,1)}, u32[]{:S(2)}, u32[]{:S(2)}) collective-permute-start(bf16[72,640]{1,0:T(8,128)(2,1)} %get-tuple-element.158), channel_id=1, source_target_pairs={{0,1},{1,0},{2,3},{3,2},{4,5},{5,4},{6,7},{7,6},{8,9},{9,8},{10,11... | collective-permute-start | bytes 276488 | tf_op jit(solution)/shard_map/ppermute | solution.py:1029
  666.4 32.2 %copy-start.47 = (bf16[2,1152]{1,0:T(2,128)(2,1)S(1)}, bf16[2,1152]{1,0:T(2,128)(2,1)}, u32[]{:S(2)}) copy-start(bf16[2,1152]{1,0:T(2,128)(2,1)} %get-tuple-element.132) | copy-start | bytes 13828
  666.4 32.2 %copy-start.46 = (bf16[2,1152]{1,0:T(2,128)(2,1)S(1)}, bf16[2,1152]{1,0:T(2,128)(2,1)}, u32[]{:S(2)}) copy-start(bf16[2,1152]{1,0:T(2,128)(2,1)} %get-tuple-element.124) | copy-start | bytes 13828
  702.6 11.3 %copy-start.27 = (f32[2304]{0:T(1024)S(1)}, f32[2304]{0:T(1024)}, u32[]{:S(2)}) copy-start(f32[2304]{0:T(1024)} %get-tuple-element.138) | copy-start | bytes 27652
  702.6 11.3 %copy-start.34 = (f32[1152]{0:T(1024)S(1)}, f32[1152]{0:T(1024)}, u32[]{:S(2)}) copy-start(f32[1152]{0:T(1024)} %reshape.220) | copy-start | bytes 13828
  702.6 11.3 %copy-start.36 = (f32[1152]{0:T(1024)S(1)}, f32[1152]{0:T(1024)}, u32[]{:S(2)}) copy-start(f32[1152]{0:T(1024)} %reshape_squeeze.7) | copy-start | bytes 13828
  702.7 11.4 %copy-start.26 = (f32[2304]{0:T(1024)S(1)}, f32[2304]{0:T(1024)}, u32[]{:S(2)}) copy-start(f32[2304]{0:T(1024)} %get-tuple-element.139) | copy-start | bytes 27652
  702.7 11.4 %copy-start.33 = (f32[1152]{0:T(1024)S(1)}, f32[1152]{0:T(1024)}, u32[]{:S(2)}) copy-start(f32[1152]{0:T(1024)} %reshape.221) | copy-start | bytes 13828
  702.7 11.4 %copy-start.35 = (f32[1152]{0:T(1024)S(1)}, f32[1152]{0:T(1024)}, u32[]{:S(2)}) copy-start(f32[1152]{0:T(1024)} %reshape_squeeze.8) | copy-start | bytes 13828
  712.2 37.0 %copy-start.12 = (bf16[2,1024,1152]{2,1,0:T(8,128)(2,1)}, bf16[2,1024,1152]{2,1,0:T(8,128)(2,1)S(1)}, u32[]{:S(2)}) copy-start(bf16[2,1024,1152]{2,1,0:T(8,128)(2,1)S(1)} %fusion.17) | copy-start | bytes 14155780
  712.2 43.8 %copy-start.25 = (bf16[16,4,72]{2,1,0:T(4,128)(2,1)S(1)}, bf16[16,4,72]{2,1,0:T(4,128)(2,1)}, u32[]{:S(2)}) copy-start(bf16[16,4,72]{2,1,0:T(4,128)(2,1)} %slice.247) | copy-start | bytes 27652
  712.2 46.1 %copy-start.32 = (bf16[4,1152]{1,0:T(4,128)(2,1)S(1)}, bf16[4,1152]{1,0:T(4,128)(2,1)}, u32[]{:S(2)}) copy-start(bf16[4,1152]{1,0:T(4,128)(2,1)} %param.13) | copy-start | bytes 27652
  749.2 60.0 %slice-start.3 = ((bf16[2,1024,1152]{2,1,0:T(8,128)(2,1)}), bf16[2,512,1152]{2,1,0:T(8,128)(2,1)S(1)}, s32[]{:S(2)}) async-start(bf16[2,1024,1152]{2,1,0:T(8,128)(2,1)} %copy-done.12), calls=%async_computation.10 | async-start | bytes 4718592 | tf_op jit(solution)/shard_map/slice | solution.py:1046
  754.8 54.5 %collective-permute-start.2 = (bf16[2,512,1152]{2,1,0:T(8,128)(2,1)}, bf16[2,512,1152]{2,1,0:T(8,128)(2,1)}, u32[]{:S(2)}, u32[]{:S(2)}) collective-permute-start(bf16[2,512,1152]{2,1,0:T(8,128)(2,1)} %slice.194), channel_id=1, source_target_pairs={{0,1},{1,0},{2,3},{3,2},{4,5},{5,4},{6,7},{7,6},{8,9},{9,8},{10,11... | collective-permute-start | bytes 7077896 | tf_op jit(solution)/shard_map/ppermute | solution.py:1029
  774.9 40.7 %collective-permute-start.3 = (bf16[72,1920]{1,0:T(8,128)(2,1)S(1)}, bf16[72,1920]{1,0:T(8,128)(2,1)S(1)}, u32[]{:S(2)}, u32[]{:S(2)}) collective-permute-start(bf16[72,1920]{1,0:T(8,128)(2,1)S(1)} %split.33), channel_id=1, source_target_pairs={{0,1},{1,0},{2,3},{3,2},{4,5},{5,4},{6,7},{7,6},{8,9},{9,8},{10,11... | collective-permute-start | bytes 829448 | tf_op jit(solution)/shard_map/ppermute | solution.py:1029
  809.2 6.3 copy-start.18
  (1 other events, 0.6 us)
Sparse Core Ops, SparseCore 0:
  116.2 120.5 all-gather.1
  385.8 120.2 reduce-scatter.3
  510.2 142.5 reduce-scatter.5
  657.3 116.4 reduce-scatter.7

commit v4 on v3

--- a/solution.py
+++ b/solution.py
@@ -420,7 +420,7 @@
 
 
 def attn_bwd_kernel(
-    q_ref, k_ref, v_ref, do_ref, o_ref, lse_ref, dqkv_ref,
+    q_ref, k_ref, v_ref, do_ref, o_ref, lse_ref, dqkv_ref, sum_ref,
     dqt_ref, delta_ref, pt_ref, dst_ref, *, blk, heads
 ):
     seq, width = q_ref.shape[1:]
@@ -451,15 +451,22 @@
         dom = jnp.where(mask, dom, jnp.zeros_like(dom))
         mine = pl.ds(pl.multiple_of(head * HEAD_DIM, 8), HEAD_DIM)
         kt = dqt_ref[mine, :].astype(bf16)
+        def products(b):
+            rows = slice(b * blk, (b + 1) * blk)
+            st = lax.dot_general(keys, qm[rows], NT, preferred_element_type=f32)
+            return st, lax.dot_general(values, dom[rows], NT, preferred_element_type=f32)
+
+        now = products(0)
         for b in range(seq // blk):
             rows = slice(b * blk, (b + 1) * blk)
-            st = lax.dot_general(keys, qm[rows], NT, preferred_element_type=f32)
-            dpt = lax.dot_general(values, dom[rows], NT, preferred_element_type=f32)
+            later = products(b + 1) if b + 1 < seq // blk else None
+            st, dpt = now
             p = jnp.exp2(st * c - lse_ref[0, 0, pl.ds(head, 1), rows])
             dst = (p * (dpt - delta_ref[pl.ds(head, 1), rows])).astype(bf16)
             pt_ref[:, rows] = p.astype(bf16)
             dst_ref[:, rows] = dst
             dqt_ref[mine, rows] = jnp.dot(kt, dst, preferred_element_type=f32) * scale
+            now = later
         dk = jnp.dot(dst_ref[...], qm, preferred_element_type=f32) * scale
         dv = jnp.dot(pt_ref[...], dom, preferred_element_type=f32)
         kwin = pl.ds(pl.multiple_of(width + start, 128), WINDOW)
@@ -470,6 +477,7 @@
 
     lax.fori_loop(0, heads, one, 0)
     dqkv_ref[0, :, :width] = dqt_ref[...].T.astype(bf16)
+    sum_ref[0, 0] = jnp.sum(dqkv_ref[0].astype(f32), axis=0, keepdims=True)
 
 
 def attn_bwd(qkv, grad, mixed, lse, heads, blk=256):
@@ -484,8 +492,14 @@
             spec(0), spec(1), spec(2), out, out,
             pl.BlockSpec((1, 1, heads, seq), lambda b, h: (b, h, 0, 0)),
         ],
-        out_specs=pl.BlockSpec((1, seq, 3 * width), lambda b, h: (b, 0, h)),
-        out_shape=jax.ShapeDtypeStruct(qkv.shape, bf16),
+        out_specs=[
+            pl.BlockSpec((1, seq, 3 * width), lambda b, h: (b, 0, h)),
+            pl.BlockSpec((1, 1, 1, 3 * width), lambda b, h: (b, h, 0, 0)),
+        ],
+        out_shape=[
+            jax.ShapeDtypeStruct(qkv.shape, bf16),
+            jax.ShapeDtypeStruct((n, 2, 1, 3 * width), f32),
+        ],
         scratch_shapes=[
             pltpu.VMEM((width, seq), f32),
             pltpu.VMEM((heads, seq), f32),
@@ -573,14 +587,13 @@
     count, seq, depth = g.shape
     hidden = slope.shape[2]
     rows, cols = 1024, hidden // 3
-    ahead = hidden // cols
     tile = pl.BlockSpec((rows, cols), lambda j, i: (i, j))
     grad, total = pl.pallas_call(
         down_backward_kernel,
         grid=(hidden // cols, count * seq // rows),
         in_specs=[
             pl.BlockSpec((rows, depth), lambda j, i: (i, 0)),
-            pl.BlockSpec((depth, cols), lambda j, i: (0, ahead + j)),
+            pl.BlockSpec((depth, cols), lambda j, i: (0, j)),
             tile,
         ],
         out_specs=[tile, pl.BlockSpec((1, cols), lambda j, i: (0, j))],
@@ -803,7 +816,6 @@
 ):
     side = lax.axis_index("tensor")
     rank = lax.axis_index("dp")
-    own = latent_out.shape[0]
     greet(side)
     conds = Exchange(cond_ref, cond_out, c_send, c_recv)
     conds.begin()
@@ -813,14 +825,15 @@
     head_swap = to_partner(head_ref, other.block(rank), side, x_send, x_recv, 0)
     head_swap.start()
     mine.begin()
-    biases = to_partner(bias_ref, bias_out, side, x_send, x_recv, 4)
+    biases = to_partner(bias_ref, bias_out, side, x_send, x_recv, 3)
     biases.start()
+    rest = to_partner(rest_ref, rest_out, side, x_send, x_recv, 1)
+    rest.start()
+    own = latent_out.shape[0]
     latents = to_partner(
-        latent_ref.at[pl.ds((1 - side) * own, own)], latent_out, side, x_send, x_recv, 1
+        latent_ref.at[pl.ds((1 - side) * own, own)], latent_out, side, x_send, x_recv, 4
     )
     latents.start()
-    rest = to_partner(rest_ref, rest_out, side, x_send, x_recv, 3)
-    rest.start()
     keep = pltpu.make_async_copy(head_ref, mine.block(rank), local_sem)
     keep.start()
     conds.finish()
@@ -856,8 +869,8 @@
     mine.finish()
     other.finish()
     mod_swap.wait()
+    rest.wait()
     latents.wait()
-    rest.wait()
     biases.wait()
     head_swap.wait_send()
     conds.drain()
@@ -866,7 +879,7 @@
 
 def opening(cond_low, mod_weight, mod_bias, biases, head, rest, latent):
     groups = lax.axis_size("dp")
-    count, half_seq, width = latent.shape
+    count = cond_low.shape[0]
     depth = cond_low.shape[1] // groups
     half = mod_weight.shape[1] * mod_weight.shape[2] // 2
     blocks = cond_low.astype(f32).reshape(count, groups, depth).transpose(1, 0, 2)
@@ -884,7 +897,7 @@
         out_shape=[
             jax.ShapeDtypeStruct((groups, depth, 2 * head.shape[1]), bf16),
             jax.ShapeDtypeStruct(rest.shape, bf16),
-            jax.ShapeDtypeStruct((count // 2, half_seq, width), bf16),
+            jax.ShapeDtypeStruct((count // 2,) + latent.shape[1:], bf16),
             jax.ShapeDtypeStruct((2, 2 * count, half), f32),
             jax.ShapeDtypeStruct(blocks.shape, f32),
             jax.ShapeDtypeStruct(biases.shape, f32),
@@ -899,6 +912,7 @@
             dma,
         ],
         compiler_params=pltpu.CompilerParams(collective_id=0, has_side_effects=True, vmem_limit_bytes=32 << 20),
+        cost_estimate=pl.CostEstimate(flops=0, bytes_accessed=0, transcendentals=0),
         name="opening",
     )(blocks, weights, bias, biases, head, rest, latent)
 
@@ -983,6 +997,305 @@
     )(mod_pair, bias_pair, weights)
 
 
+class Collect:
+    def __init__(self, grads, totals, from_core, from_row, from_z, terms, row_out, z_out, *sems):
+        self.grads, self.totals = grads, totals
+        self.from_core, self.from_row, self.from_z = from_core, from_row, from_z
+        self.terms, self.row_out, self.z_out = terms, row_out, z_out
+        (self.core_send, self.core_recv, self.row_send, self.row_recv, self.z_send, self.z_recv, self.local) = sems
+        self.rank = lax.axis_index("dp")
+        self.z, self.y, self.core = place(self.rank)
+        self.depth = lax.axis_size("dp") // (ROWS * CORES)
+        self.pieces, _, _, self.width = from_core.shape
+        self.outer = (self.z == 0) | (self.z == self.depth - 1)
+
+    def lanes(self, n):
+        return pl.ds(pl.multiple_of(n * self.width, 128), self.width)
+
+    def block(self, n, rank):
+        return self.grads.at[rank, :, self.lanes(n)]
+
+    def level(self, k):
+        falling = self.depth - 1 - k
+        falling = falling - jnp.where(falling <= self.z, 1, 0)
+        rising = k + jnp.where(k >= self.z, 1, 0)
+        there = jnp.where(self.z < self.depth // 2, falling, rising)
+        return jnp.where(k == self.depth - 1, self.z, there)
+
+    def core_copy(self, n, level, y):
+        k = level * ROWS + y
+        return pltpu.make_async_remote_copy(
+            src_ref=self.block(n, rank_of(level, y, 1 - self.core)),
+            dst_ref=self.from_core.at[n, k],
+            send_sem=self.core_send.at[n, k],
+            recv_sem=self.core_recv.at[n, k],
+            device_id={"dp": rank_of(self.z, self.y, 1 - self.core)},
+            device_id_type=MESH,
+        )
+
+    def row_copy(self, n, k):
+        level = self.level(k)
+        return pltpu.make_async_remote_copy(
+            src_ref=self.row_out.at[k],
+            dst_ref=self.from_row.at[n, level],
+            send_sem=self.row_send.at[n, k],
+            recv_sem=self.row_recv.at[n, level],
+            device_id={"dp": rank_of(self.z, 1 - self.y, self.core)},
+            device_id_type=MESH,
+        )
+
+    def z_copy(self, n, k):
+        level = self.level(k)
+        above = jnp.where(level > self.z, 1, 0)
+        return pltpu.make_async_remote_copy(
+            src_ref=self.z_out.at[k],
+            dst_ref=self.from_z.at[n, 1 - above, level],
+            send_sem=self.z_send.at[n, k],
+            recv_sem=self.z_recv.at[n, 1 - above, level],
+            device_id={"dp": rank_of(self.z + 2 * above - 1, self.y, self.core)},
+            device_id_type=MESH,
+        )
+
+    def z_arrival(self, n, way, level):
+        return pltpu.make_async_remote_copy(
+            src_ref=self.z_out.at[0],
+            dst_ref=self.from_z.at[n, way, level],
+            send_sem=self.z_send.at[n, 0],
+            recv_sem=self.z_recv.at[n, way, level],
+            device_id={"dp": rank_of(self.z, 1 - self.y, self.core)},
+            device_id_type=MESH,
+        )
+
+    def each_core_copy(self, act):
+        def some(i, carry):
+            n, level = i // self.depth, self.level(i % self.depth)
+            act(self.core_copy(n, level, 1 - self.y))
+            act(self.core_copy(n, level, self.y))
+            return carry
+
+        lax.fori_loop(0, self.pieces * self.depth, some, 0)
+
+    def begin(self):
+        self.each_core_copy(lambda copy: copy.start())
+
+    def fetches(self, kind, n, k):
+        level = self.level(k)
+        y = 1 - self.y if kind == "row" else self.y
+        slot = k if kind == "row" else self.depth + k
+
+        def get(j, ref):
+            return pltpu.make_async_copy(ref, self.terms.at[slot, j], self.local.at[slot, j])
+
+        found = [
+            (get(0, self.block(n, rank_of(level, y, self.core))), None),
+            (get(1, self.from_core.at[n, level * ROWS + y]), None),
+        ]
+        if kind == "z":
+            below = (level >= self.z) & (self.z > 0)
+            above = (level <= self.z) & (self.z < self.depth - 1)
+            found.append((get(2, self.from_row.at[n, level]), None))
+            found.append((get(3, self.from_z.at[n, 0, level]), below))
+            found.append((get(4, self.from_z.at[n, 1, level]), above))
+        return found
+
+    def load(self, kind, n, k):
+        level = self.level(k)
+        y = 1 - self.y if kind == "row" else self.y
+        self.core_copy(n, level, y).wait_recv()
+        if kind == "z":
+            self.row_copy(n, k).wait_recv()
+        for j, (fetch, when) in enumerate(self.fetches(kind, n, k)):
+            if when is None:
+                fetch.start()
+            else:
+
+                def arrived(j=j, fetch=fetch):
+                    self.z_arrival(n, j - 3, level).wait_recv()
+                    fetch.start()
+
+                pl.when(when)(arrived)
+
+    def finish(self, kind, n, k, last=False):
+        total = None
+        slot = k if kind == "row" else self.depth + k
+        for j, (fetch, when) in enumerate(self.fetches(kind, n, k)):
+            if when is None:
+                fetch.wait()
+            else:
+                pl.when(when)(fetch.wait)
+            term = self.terms[slot, j].astype(f32)
+            if when is not None:
+                term = jnp.where(when, term, 0.0)
+            total = term if total is None else total + term
+        if last:
+            self.totals[:, self.lanes(n)] = total
+            return
+        copy = self.row_copy if kind == "row" else self.z_copy
+        out = self.row_out if kind == "row" else self.z_out
+        pl.when(n > 0)(lambda: copy(n - 1, k).wait_send())
+        out[k] = total.astype(bf16)
+        copy(n, k).start()
+
+    def units(self, r):
+        found = []
+        final = self.depth - 1
+        valid = lambda n: (n >= 0) & (n < self.pieces)
+        for k in range(self.depth):
+            found.append((valid(r), "row", r, k, False))
+        for k in range(final):
+            age = jnp.where(self.outer, 2, 3 if k < final - 1 else 4)
+            found.append((valid(r - age), "z", r - age, k, False))
+        found.append((valid(r - 5), "z", r - 5, final, True))
+        return found
+
+    def rounds(self):
+        return self.pieces + 5
+
+    def load_round(self, r):
+        for when, kind, n, k, _ in self.units(r):
+            pl.when(when)(lambda kind=kind, n=n, k=k: self.load(kind, n, k))
+
+    def finish_round(self, r):
+        for when, kind, n, k, last in self.units(r):
+            pl.when(when)(lambda kind=kind, n=n, k=k, last=last: self.finish(kind, n, k, last))
+
+    def end(self):
+        n = self.pieces - 1
+        for k in range(self.depth):
+            self.row_copy(n, k).wait_send()
+        for k in range(self.depth - 1):
+            self.z_copy(n, k).wait_send()
+        self.each_core_copy(lambda copy: copy.wait_send())
+
+
+def collect_shapes(pieces, width, groups, depth):
+    levels = groups // (ROWS * CORES)
+    dma = pltpu.SemaphoreType.DMA
+    arrivals = [
+        jax.ShapeDtypeStruct((pieces, levels * ROWS, depth, width), bf16),
+        jax.ShapeDtypeStruct((pieces, levels, depth, width), bf16),
+        jax.ShapeDtypeStruct((pieces, 2, levels, depth, width), bf16),
+    ]
+    scratch = [
+        pltpu.VMEM((2 * levels, 5, depth, width), bf16),
+        pltpu.VMEM((levels, depth, width), bf16),
+        pltpu.VMEM((levels - 1, depth, width), bf16),
+        dma((pieces, levels * ROWS)), dma((pieces, levels * ROWS)),
+        dma((pieces, levels)), dma((pieces, levels)),
+        dma((pieces, levels)), dma((pieces, 2, levels)),
+        dma((2 * levels, 5)),
+    ]
+    return arrivals, scratch
+
+
+TILE = 256
+
+
+def latents_backward_kernel(
+    dqkv_ref, w_ref, lat_ref, first_ref, scale_ref, grads_ref,
+    out_ref, sums_ref, totals_ref, rows_in, from_core, from_row, from_z,
+    rows_out, x_send, x_recv, *collect,
+):
+    side = lax.axis_index("tensor")
+    r = pl.program_id(0)
+    engine = Collect(grads_ref, totals_ref, from_core, from_row, from_z, *collect)
+    count, half_seq, _ = rows_in.shape
+    per_half = half_seq // TILE
+    sent = count * per_half
+
+    def row_copy(i):
+        return to_partner(
+            rows_out.at[i],
+            rows_in.at[i // per_half, pl.ds(pl.multiple_of(i % per_half * TILE, TILE), TILE)],
+            side, x_send, x_recv, i,
+        )
+
+    @pl.when(r == 0)
+    def _():
+        greet(side)
+        engine.begin()
+        sums_ref[...] = jnp.zeros_like(sums_ref)
+
+    engine.load_round(r)
+
+    @pl.when(r < 2 * sent)
+    def _():
+        grad = lax.dot_general(dqkv_ref[...], w_ref[...], NT, preferred_element_type=f32)
+        norm, inverse = normed(lat_ref[...].astype(f32))
+        latent = r % sent // per_half
+        sums_ref[latent] += jnp.concatenate(
+            [jnp.sum(grad, axis=0, keepdims=True), jnp.sum(grad * norm, axis=0, keepdims=True)], axis=0
+        )
+        back = normed_back(grad * (1.0 + scale_ref[0]), norm, inverse)
+        result = (first_ref[...] + back).astype(bf16)
+        out_ref[...] = result
+
+        @pl.when(r < sent)
+        def _():
+            rows_out[r] = result
+            row_copy(r).start()
+
+    engine.finish_round(r)
+
+    @pl.when(r == pl.num_programs(0) - 1)
+    def _():
+        engine.end()
+        for i in range(sent):
+            row_copy(i).wait()
+
+
+def latents_backward(dqkv, w, lat, first_grad, scale, grads):
+    count, seq, wide = dqkv.shape
+    width = lat.shape[2]
+    groups = lax.axis_size("dp")
+    depth = grads.shape[0] // groups
+    per_half = seq // 2 // TILE
+    sent = count * per_half
+    pieces, piece = 6, wide // 6
+    arrivals, scratch = collect_shapes(pieces, piece, groups, depth)
+
+    def tile(r):
+        r = jnp.minimum(r, 2 * sent - 1)
+        i = r % sent
+        return i // per_half * 2 * per_half + i % per_half + jnp.where(r < sent, per_half, 0)
+
+    rows = lambda cols: pl.BlockSpec((TILE, cols), lambda r: (tile(r), 0))
+    anywhere = pl.BlockSpec(memory_space=pl.ANY)
+    flat = lambda a: a.reshape(count * seq, a.shape[2])
+    dma = pltpu.SemaphoreType.DMA
+    return pl.pallas_call(
+        latents_backward_kernel,
+        grid=(max(pieces + 5, 2 * sent),),
+        in_specs=[
+            rows(wide),
+            pl.BlockSpec((width, wide), lambda r: (0, 0), pipeline_mode=pl.Buffered(1)),
+            rows(width),
+            rows(width),
+            pl.BlockSpec((1, 1, width), lambda r: (tile(r) // (2 * per_half), 0, 0)),
+            anywhere,
+        ],
+        out_specs=[
+            rows(width),
+            pl.BlockSpec((count, 2, width), lambda r: (0, 0, 0)),
+            pl.BlockSpec((depth, wide), lambda r: (0, 0)),
+        ]
+        + [anywhere] * 4,
+        out_shape=[
+            jax.ShapeDtypeStruct((count * seq, width), bf16),
+            jax.ShapeDtypeStruct((count, 2, width), f32),
+            jax.ShapeDtypeStruct((depth, wide), f32),
+            jax.ShapeDtypeStruct((count, seq // 2, width), bf16),
+        ]
+        + arrivals,
+        scratch_shapes=[pltpu.VMEM((sent, TILE, width), bf16), dma((sent,)), dma((sent,))] + scratch,
+        compiler_params=pltpu.CompilerParams(
+            collective_id=2, has_side_effects=True, vmem_limit_bytes=56 << 20
+        ),
+        cost_estimate=pl.CostEstimate(flops=0, bytes_accessed=0, transcendentals=0),
+        name="latents_backward",
+    )(flat(dqkv), w, flat(lat), flat(first_grad), scale, grads.reshape(groups, depth, wide))[:4]
+
+
 def normed(values):
     centred = values - jnp.mean(values, axis=-1, keepdims=True)
     variance = jnp.mean(centred * centred, axis=-1, keepdims=True)
@@ -1055,7 +1368,7 @@
         return jnp.pad(a, [(0, 0)] * (a.ndim - 1) + [(0, room - cols)])
 
     head_shard = roomy(head_weight).reshape(depth, 3 * room)
-    shards = jnp.concatenate([up_weight, down_weight.T, roomy(mix_weight.T)], axis=1)
+    shards = jnp.concatenate([up_weight, roomy(mix_weight.T)], axis=1)
     branch = branch_bias.astype(f32)
     flat = [a.astype(f32).reshape(-1) for a in (head_bias, branch, up_bias)]
     head_all, shards_in, latent_in, mod_parts, cond_blocks, biases_in = opening(
@@ -1079,12 +1392,15 @@
     row = lambda k: modulation[:, k][:, None, :]
     shift_a, scale_a, gate_a, shift_m, scale_m, gate_m = [row(k) for k in range(6)]
 
-    cuts = (0, hidden // 2, hidden, hidden + room)
+    cuts = (0, hidden // 2, hidden // 2 + room)
     pieces = [a[:, lo:hi] for lo, hi in zip(cuts, cuts[1:]) for a in (shards, shards_in)]
-    rest_all = lax.all_gather(jnp.concatenate(pieces, axis=1), "dp", axis=0, tiled=True)
-    up_all = rest_all[:, :hidden]
-    down_t = rest_all[:, hidden : 2 * hidden]
-    mix_t = rest_all[:, 2 * hidden :]
+    up_mix = lax.all_gather(jnp.concatenate(pieces, axis=1), "dp", axis=0, tiled=True)
+    up_all = up_mix[:, :hidden]
+    mix_t = up_mix[:, hidden:]
+    down_mine, _ = lax.optimization_barrier((down_weight.T, latent_in))
+    down_t = lax.all_gather(
+        jnp.concatenate([down_mine, swap(down_mine)], axis=1), "dp", axis=0, tiled=True
+    )
     up_bias_f = jnp.concatenate([flat[2], biases_in[4 * cols :]])
 
     lat = jnp.concatenate([own_latents(latent), latent_in], axis=1)
@@ -1103,19 +1419,19 @@
     first = lat_f + gate_a * attn_out
     norm2, inv2 = normed(first)
     mlp_in = (norm2 * (1.0 + scale_m) + shift_m).astype(bf16)
-    act, slope = up_forward(mlp_in, rest_all, up_bias_f)
+    act, slope = up_forward(mlp_in, up_mix, up_bias_f)
+    upstream = upstream_low.astype(f32)
+    mlp_grad = (gate_m * upstream).astype(bf16)
+    down_grad = mm("bsd,bsf->df", mlp_grad, act).astype(bf16)
+    down_grad, mlp_grad, act = lax.optimization_barrier((down_grad, mlp_grad, act))
+    down_sum = lax.psum_scatter(down_grad, "dp", scatter_dimension=0, tiled=True)
     mlp_out = mm("bsf,df->bsd", act, down_t) + branch_all[1]
     block = (first + gate_m * mlp_out).astype(bf16)
     block_in = swap(block[:, half_seq:])
 
-    upstream = upstream_low.astype(f32)
     gate_m_grad = jnp.sum(upstream * mlp_out, axis=1)
     tail_bias_grad = jnp.sum(gate_m[:, 0] * jnp.sum(upstream, axis=1), axis=0)
-    mlp_grad = (gate_m * upstream).astype(bf16)
-    down_grad = mm("bsd,bsf->df", mlp_grad, act).astype(bf16)
-    down_grad, mlp_grad = lax.optimization_barrier((down_grad, mlp_grad))
-    down_sum = lax.psum_scatter(down_grad, "dp", scatter_dimension=0, tiled=True)
-    pre_grad, up_bias_term = down_backward(mlp_grad, rest_all, slope)
+    pre_grad, up_bias_term = down_backward(mlp_grad, down_t, slope)
     up_grad = mm("bsd,bsf->df", mlp_in, pre_grad).astype(bf16)
     up_grad, pre_grad = lax.optimization_barrier((up_grad, pre_grad))
     mlp_in_grad = mm("bsf,df->bsd", pre_grad, up_all)
@@ -1125,25 +1441,21 @@
     gate_a_grad = jnp.sum(first_grad * attn_out, axis=1)
     attn_bias_grad = jnp.sum(gate_a[:, 0] * jnp.sum(first_grad, axis=1), axis=0)
     attn_grad = (gate_a * first_grad).astype(bf16)
+    attn_grad, down_sum = lax.optimization_barrier((attn_grad, down_sum))
     mixed_grad = mm("bsd,dc->bsc", attn_grad, mix_t).astype(bf16)
     mix_grad = mm("bsd,bsc->dc", attn_grad, mixed).astype(bf16)
     up_grad = jnp.concatenate([up_grad, mix_grad], axis=1)
     up_grad, mixed_grad = lax.optimization_barrier((up_grad, mixed_grad))
     up_sum = lax.psum_scatter(up_grad, "dp", scatter_dimension=0, tiled=True)
-    mixed_grad, down_sum = lax.optimization_barrier((mixed_grad, down_sum))
-    qkv_grad = attn_bwd(qkv, mixed_grad, mixed, logsum, heads)
+    qkv_grad, qkv_bias_term = attn_bwd(qkv, mixed_grad, mixed, logsum, heads)
+    qkv_bias_term = jnp.sum(qkv_bias_term, axis=0)
     head_grad = mm("bsd,bsc->dc", attn_in, qkv_grad).astype(bf16)
-    head_grad, qkv_grad = lax.optimization_barrier((head_grad, qkv_grad))
-    head_sum = lax.psum_scatter(head_grad, "dp", scatter_dimension=0, tiled=True)
-    qkv_grad, up_sum, block_in = lax.optimization_barrier((qkv_grad, up_sum, block_in))
+    head_grad, up_sum, block_in = lax.optimization_barrier((head_grad, up_sum, block_in))
     block_out = placed(block, block_in)
-    qkv_bias_term = jnp.sum(qkv_grad, axis=(0, 1), dtype=f32)
-    attn_in_grad = mm("bsc,dc->bsd", qkv_grad, head_all)
-    shift_a_grad = jnp.sum(attn_in_grad, axis=1)
-    scale_a_grad = jnp.sum(attn_in_grad * norm1, axis=1)
-    lat_grad = first_grad + normed_back(attn_in_grad * (1.0 + scale_a), norm1, inv1)
-    lat_grad = lat_grad.astype(bf16)
-    lat_grad_in = swap(lat_grad[:, half_seq:])
+    lat_grad, sums, head_sum, lat_grad_in = latents_backward(
+        qkv_grad, head_all, lat, first_grad, scale_a, head_grad
+    )
+    shift_a_grad, scale_a_grad = sums[:, 0], sums[:, 1]
 
     mod_low = jnp.stack(
         [shift_a_grad, scale_a_grad, gate_a_grad, shift_m_grad, scale_m_grad, gate_m_grad], axis=1
@@ -1164,13 +1476,12 @@
         return flat.reshape(-1, 128)
 
     mod_pair = jnp.stack([mod_share(side), mod_share(1 - side)])
-    mod_pair, lat_grad = lax.optimization_barrier((mod_pair, lat_grad))
     mod_blocks, biases, cond_parts = closing(
         mod_pair,
         jnp.stack([bias_share(side, 0), bias_share(1 - side, 1)]),
         mod_weight,
     )
-    latent_grad = placed(lat_grad, lat_grad_in)
+    latent_grad = placed(lat_grad.reshape(own, 2 * half_seq, width), lat_grad_in)
     biases = biases.reshape(-1)
     mod_rows = mod_blocks.astype(bf16).reshape(groups, 2, count, 3, cols)
     mod_rows = mod_rows.transpose(0, 2, 1, 3, 4).reshape(groups * count, 6, cols)
@@ -1183,7 +1494,7 @@
 
     def joined(summed, axis):
         mine, other = jnp.split(summed, 2, axis=axis)
-        return mine.astype(f32) + swap(other).astype(f32)
+        return mine.astype(f32) + swap(other.astype(bf16)).astype(f32)
 
     head_weight_grad = joined(head_sum, 1).reshape(depth, 3, room)[..., :cols]
     mix_weight_grad = joined(up_sum[:, hidden:], 1)[:, :cols].T

time: 830 us -> 811 us (0.977)
  Pallas kernels: 356 us -> 434 us
  waiting for transfers between devices: 73.5 us -> 11.2 us
  matrix products: 250 us -> 219 us
    pallas_call x0 -> x1, Pallas kernels: none -> 98.2 us  [latents_backward(): pl.pallas_call(latents_backward_kernel, grid=(max(pieces + 5, 2 * sent),)...]
    dot_general x11 -> x10, matrix products: 250 us -> 219 us  [mm(): return jnp.einsum(spec, a, b, preferred_element_type=f32)]
    ppermute x7, waiting for transfers between devices: 35.7 us -> 6.41 us  [swap(): return lax.ppermute(a, 'tensor', [(0, 1), (1, 0)])]
    all_gather x1, waiting for transfers between devices: 23.5 us -> 0.01 us  [body_by_latents(): lax.all_gather(jnp.concatenate(pieces, axis=1), 'dp', axis=0, tiled=True)]
    reduce_scatter x1 -> x0, waiting for transfers between devices: 11.1 us -> none  [body_by_latents(): lax.psum_scatter(head_grad, 'dp', scatter_dimension=0, tiled=True)]
    pallas_call x1, Pallas kernels: 114 us -> 104 us  [attn_bwd(): pl.pallas_call(partial(attn_bwd_kernel, blk=blk, heads=heads), grid=(n, 2...]
    concatenate x1 -> x4, other arithmetic: 1.13 us -> 9.56 us  [the longest x1 4.25 us: body_by_latents(): lat = jnp.concatenate([own_latents(latent), latent_in], axis=1)]
    unnamed x126 -> x108, local copies, waits for them, and re-layouts: 16.9 us -> 12.1 us
  transfers between devices with their start and end apart: 11 -> 11, of which waited for: 6 -> 3; matrix products, arithmetic and copies ran while one was open for 33% -> 34% of each run, Pallas kernels for 24% -> 28%
where the time goes in v4:
time: 811 us; the launch traced here: 808 us
  Pallas kernels  434 us (54%)
  matrix products  219 us (27%)
  other arithmetic  61.2 us (8%)
  local copies, waits for them, and re-layouts  59.1 us (7%)
  between operations  15.1 us (2%)
  waiting for transfers between devices  11.2 us (1%)
    dot_general x10, matrix products, mm(): return jnp.einsum(spec, a, b, preferred_element_type=f32)  219 us
    pallas_call x1, Pallas kernels, attn_bwd(): pl.pallas_call(partial(attn_bwd_kernel, blk=blk, heads=heads), grid=(n, 2...  104 us
    pallas_call x1, Pallas kernels, latents_backward(): pl.pallas_call(latents_backward_kernel, grid=(max(pieces + 5, 2 * sent),)...  98.2 us
    pallas_call x1, Pallas kernels, opening(): pl.pallas_call(opening_kernel, in_specs=[vmem, vmem, vmem, vmem, anywhere...  77.9 us
    pallas_call x1, Pallas kernels, attn_fwd(): pl.pallas_call(partial(attn_fwd_kernel, blk=blk, heads=heads), grid=(n, 2...  46.6 us
    pallas_call x1, Pallas kernels, up_forward(): pl.pallas_call(up_forward_kernel, grid=(hidden // cols, count * seq // ro...  43.5 us
    pallas_call x1, Pallas kernels, down_backward(): pl.pallas_call(down_backward_kernel, grid=(hidden // cols, count * seq //...  34.7 us
    pallas_call x1, Pallas kernels, closing(): pl.pallas_call(closing_kernel, in_specs=[vmem, vmem, vmem], out_specs=[vm...  29.9 us
  transfers between devices with their start and end apart: 11, of which 3 were waited for; matrix products, arithmetic and copies ran while one was open for 34% of the time, Pallas kernels for 28%

profile of v4, /device:TPU:0, one launch (start us, length us, event | category | flops | bytes accessed | tf_op | source)
XLA Modules:
  0.0 808.2 jit_solution(9263051081943504289)
XLA Ops:
  7.2 1.1 copy.98
  11.5 1.1 copy.131
  12.6 0.9 pad.30
  13.7 0.8 reshape.243
  16.0 1.0 pad_maximum_fusion.5.rest_ref
  17.1 2.3 copy-done.2
  19.4 0.8 copy-done.4
  20.2 77.9 %opening.1 = (bf16[16,72,3840]{2,1,0:T(8,128)(2,1)S(1)}, bf16[72,2944]{1,0:T(8,128)(2,1)S(1)}, bf16[2,512,1152]{2,1,0:T(8,128)(2,1)S(1)}, f32[2,8,1728]{2,1,0:T(...) custom-call(f32[16,8,128]{2,1,0:T(8,128)S(1)} %fusion.20.cond_ref, ...), custom_call_target="tpu_custom_call" | custom-call | tf_op jit(solution)/shard_map/opening/pallas_call | solution.py:893
  98.1 3.4 copy-done.3
  103.4 2.3 pad_maximum_fusion.3
  107.2 1.0 reshape.217
  109.2 3.5 constant_dynamic-slice_fusion.4
  112.7 2.9 collective-permute-done.1
  115.6 2.0 pad_maximum_fusion.4
  118.0 2.5 convert_reduce_fusion.1
  120.5 2.8 fusion.7
  123.5 4.9 constant_dynamic-slice_fusion.2
  129.1 27.7 %add_convert_fusion.q_ref.k_ref.v_ref = bf16[2,1024,3840]{2,1,0:T(8,128)(2,1)} fusion(f32[3840]{0:T(1024)S(1)} %constant_dynamic-update-slice_fusion, bf16[1152,3840,1]{1,0,2:T(8,128)(2,1)} %bitcast.135, f32[2,1152]{1,0:T(2,128)S(1)} %get-tuple-element.186, f32[2,1152]{1,0:T(2,128)S(1)} %get-tuple-element.187, f32[2,1024]{1,0:T(2,128)S(1)} %add_rsqrt_fusion.1, ...), kind=kOutput, calls=%fused_computation | convolution fusion | flops 18156355584 | bytes 29344768 | tf_op jit(solution)/shard_map/bsd,dc->bsc/dot_general | solution.py:1315
  158.9 46.6 %attention_forward.1 = (bf16[2,1024,1280]{2,1,0:T(8,128)(2,1)}, f32[2,2,8,1024]{3,2,1,0:T(8,128)}) custom-call(bf16[2,1024,3840]{2,1,0:T(8,128)(2,1)} %add_convert_fusion.q_ref.k_ref.v_ref, bf16[2,1024,3840]{2,1,0:T(8,128)(2,1)} %add_convert_fusion.q_ref.k_ref.v_ref, bf16[2,1024,3840]{2,1,0:T(8,128)(2,1)} %add_convert_fusion.q_ref.k_ref.v_ref), custom_call_target="tpu_custom_call" | custom-call | flops 10737418240 | bytes 20971520 | tf_op jit(solution)/shard_map/attention_forward/pallas_call | solution.py:399
  205.5 3.5 collective-permute-done
  209.1 4.7 fusion.11
  213.8 12.6 %fusion.35 = (f32[2,1024]{1,0:T(2,128)S(1)}, f32[2,1024,1152]{2,1,0:T(8,128)S(1)}, f32[2,1024,1152]{2,1,0:T(8,128)}) fusion(f32[1152]{0:T(1024)S(1)} %get-tuple-element.143, f32[2,1152]{1,0:T(2,128)S(1)} %get-tuple-element.185, bf16[2,512,1152]{2,1,0:T(8,128)(2,1)S(1)} %get-tuple-element.48, bf16[2,512,1152]{2,1,0:T(8,128)(2,1)} %constant_dynamic-slice_fusion.4, ...), kind=kOutput, calls=%fused_computation.137 | convolution fusion | flops 6058670080 | bytes 31806976 | tf_op jit(solution)/shard_map/bsc,dc->bsd/dot_general | solution.py:1315
  226.4 1.1 multiply_reduce_fusion.3
  227.5 3.7 add_convert_fusion.2
  231.5 43.5 %up_forward.1 = (bf16[2048,4608]{1,0:T(8,128)(2,1)}, bf16[2048,4608]{1,0:T(8,128)(2,1)}) custom-call(bf16[2048,1152]{1,0:T(8,128)(2,1)} %bitcast.146, bf16[1152,5888]{1,0:T(8,128)(2,1)} %all-gather.3.cloned.1.call-done.w_ref, f32[1,4608]{1,0:T(1,128)} %reshape.222.b_ref), custom_call_target="tpu_custom_call" | custom-call | flops 21743271936 | bytes 37748736 | tf_op jit(solution)/shard_map/up_forward/pallas_call | solution.py:548
  275.0 27.3 %fusion = bf16[1152,4608]{1,0:T(8,128)(2,1)} fusion(bf16[2,1024,1152]{2,1,0:T(8,128)(2,1)S(1)} %bitcast.145, bf16[2,1024,4608]{2,1,0:T(8,128)(2,1)} %bitcast.170), kind=kOutput, calls=%fused_computation.3 | convolution fusion | flops 21748580352 | bytes 34209792 | tf_op jit(solution)/shard_map/bsd,bsf->df/dot_general | solution.py:1315
  302.4 34.7 %down_backward.1 = (bf16[2048,4608]{1,0:T(8,128)(2,1)}, f32[1,4608]{1,0:T(1,128)}) custom-call(bf16[2048,1152]{1,0:T(8,128)(2,1)} %bitcast.143, bf16[1152,4608]{1,0:T(8,128)(2,1)} %all-gather.5.cloned.1.call-done.w_ref, bf16[2048,4608]{1,0:T(8,128)(2,1)} %get-tuple-element.60.slope_ref), custom_call_target="tpu_custom_call" | custom-call | flops 21743271936 | bytes 37748736 | tf_op jit(solution)/shard_map/down_backward/pallas_call | solution.py:591
  337.1 27.5 %fusion.1 = bf16[1152,4608]{1,0:T(8,128)(2,1)} fusion(bf16[2,1024,1152]{2,1,0:T(8,128)(2,1)S(1)} %bitcast.148, bf16[2,1024,4608]{2,1,0:T(8,128)(2,1)} %bitcast.172), kind=kOutput, calls=%fused_computation.4 | convolution fusion | flops 21748580352 | bytes 34209792 | tf_op jit(solution)/shard_map/bsd,bsf->df/dot_general | solution.py:1315
  364.7 34.7 %multiply_reduce_fusion = (bf16[2,1152]{1,0:T(2,128)(2,1)S(1)}, f32[2,1024]{1,0:T(2,128)S(1)}, f32[2,1024]{1,0:T(2,128)S(1)}, bf16[2,1152]{1,0:T(2,128)(2,1)S(1)}, f32[2,1024,1152]{2,1,0:T(8,128)}) fusion(f32[2,1024,1152]{2,1,0:T(8,128)} %copy-done.9, f32[2,1024]{1,0:T(2,128)S(1)} %add_rsqrt_fusion, f32[2,1024]{1,0:T(2,128)S(1)} %broadcast_multiply_fusion.2, ...), kind=kOutput, calls=%fused_computation.26 | convolution fusion | flops 21764497408 | bytes 48416768 | tf_op jit(solution)/shard_map/bsf,df->bsd/dot_general | solution.py:1315
  399.5 39.7 %convert_reduce_fusion = (f32[2,1152]{1,0:T(2,128)S(1)}, bf16[2,1152]{1,0:T(2,128)(2,1)S(1)}, bf16[2,1024,1152]{2,1,0:T(8,128)(2,1)}, bf16[2,1152]{1,0:T(2,128)(...) fusion(bf16[2,512,1152]{2,1,0:T(8,128)(2,1)} %collective-permute-done, ...), kind=kOutput, calls=%fused_computation.6 | convolution fusion | flops 21797527552 | bytes 76765184 | tf_op jit(solution)/shard_map/bsf,df->bsd/dot_general | solution.py:1315
  439.2 6.6 multiply_convert_fusion
  445.8 10.3 %fusion.13 = bf16[1152,1280]{1,0:T(8,128)(2,1)S(1)} fusion(bf16[2,1024,1152]{2,1,0:T(8,128)(2,1)} %multiply_convert_fusion, bf16[2,1024,1280]{2,1,0:T(8,128)(2,1)} %get-tuple-element.53.o_ref), kind=kOutput, calls=%fused_computation.36 | convolution fusion | flops 6041272320 | bytes 12910592 | tf_op jit(solution)/shard_map/bsd,bsc->dc/dot_general | solution.py:1315
  456.1 11.9 %pad_maximum_fusion = bf16[1152,5888]{1,0:T(8,128)(2,1)} fusion(bf16[1152,1280]{1,0:T(8,128)(2,1)S(1)} %fusion.13, bf16[1152,4608]{1,0:T(8,128)(2,1)} %fusion.1), kind=kLoop, calls=%fused_computation.13 | loop fusion | flops 27131904 | bytes 27131904 | tf_op jit(solution)/shard_map/concatenate | solution.py:1447
  467.9 11.2 %convolution_convert_fusion.do_ref = bf16[2,1024,1280]{2,1,0:T(8,128)(2,1)} fusion(bf16[2,1024,1152]{2,1,0:T(8,128)(2,1)} %multiply_convert_fusion, bf16[1152,5888]{1,0:T(8,128)(2,1)} %all-gather.3.cloned.1.call-done.w_ref), kind=kOutput, calls=%fused_computation.37 | convolution fusion | flops 6042419200 | bytes 12910592 | tf_op jit(solution)/shard_map/bsd,dc->bsc/dot_general | solution.py:1315
  479.1 1.6 slice.220
  481.5 4.2 pad_maximum_fusion.1
  485.7 4.9 fusion.36
  493.6 1.7 split.32
  495.4 1.8 collective-permute-start.6
  497.2 103.6 %attention_backward.1 = (bf16[2,1024,3840]{2,1,0:T(8,128)(2,1)}, f32[2,2,1,1920]{3,2,1,0:T(1,128)}) custom-call(bf16[2,1024,3840]{2,1,0:T(8,128)(2,1)} %add_convert_fusion.q_ref.k_ref.v_ref, bf16[2,1024,3840]{2,1,0:T(8,128)(2,1)} %add_convert_fusion.q_ref.k_ref.v_ref, bf16[2,1024,3840]{2,1,0:T(8,128)(2,1)} %add_convert_fusion.q_ref.k_ref.v_ref, ...), custom_call_target="tpu_custom_call" | custom-call | tf_op jit(solution)/shard_map/attention_backward/pallas_call | solution.py:488
  600.8 0.8 reduce_sum.172
  601.8 26.1 %bitcast_convert_fusion = bf16[1152,3840]{1,0:T(8,128)(2,1)} fusion(bf16[2,1024,3840]{2,1,0:T(8,128)(2,1)} %get-tuple-element.68, f32[2,1152]{1,0:T(2,128)S(1)} %copy-done.37, f32[2,1152]{1,0:T(2,128)S(1)} %copy-done.39, f32[2,1024]{1,0:T(2,128)S(1)} %copy-done.42, f32[2,1024]{1,0:T(2,128)S(1)} %copy-done.33, bf16[2,512,1152]{2,1,0:T(8,128)(2,1)S(1)} %copy-done.1, ...), kind=kOutput, calls=%fused_computation.5 | convolution fusion | flops 18145050624 | bytes 29329408 | tf_op jit(solution)/shard_map/bsd,bsc->dc/dot_general | solution.py:1315
  628.0 1.9 add_bitcast_fusion
  629.9 4.7 reduce-scatter.5.cloned.1.call-done
  634.6 1.8 split.30
  636.4 1.6 fusion.37
  638.0 98.2 %latents_backward.1 = (bf16[2048,1152]{1,0:T(8,128)(2,1)}, f32[2,2,1152]{2,1,0:T(2,128)}, f32[72,3840]{1,0:T(8,128)}, bf16[2,512,1152]{2,1,0:T(8,128)(2,1)}, bf1...) custom-call(bf16[2048,3840]{1,0:T(8,128)(2,1)} %bitcast.140, ...), custom_call_target="tpu_custom_call" | custom-call | tf_op jit(solution)/shard_map/latents_backward/pallas_call | solution.py:1266
  736.2 0.9 convert.31
  738.1 0.9 reshape.232
  740.2 0.8 stack_reshape.13
  741.1 29.9 %closing.1 = (f32[16,8,1728]{2,1,0:T(8,128)S(1)}, f32[36,128]{1,0:T(8,128)S(1)}, f32[2,16,8,128]{3,2,1,0:T(8,128)S(1)}) custom-call(f32[2,8,1728]{2,1,0:T(8,128)S(1)} %pad_maximum_fusion.6.mod_ref, f32[2,36,128]{2,1,0:T(8,128)S(1)} %pad_maximum_fusion.7.bias_ref, bf16[2,128,1728]{2,1,0:T(8,128)(2,1)S(1)} %pad_bitcast_fusion.mod_w_ref), custom_call_target="tpu_custom_call" | custom-call | tf_op jit(solution)/shard_map/closing/pallas_call | solution.py:974
  771.6 2.2 collective-permute-start.5
  773.8 1.8 split.38
  775.6 2.0 collective-permute-start.3
  777.6 0.8 convert_element_type.127
  778.5 1.6 reshape.237
  780.1 1.0 copy.118
  781.1 2.0 reshape.238
  783.9 2.4 fusion.43
  788.5 1.8 slice.184
  790.4 6.0 bitcast_select_fusion
  797.1 1.0 convert_add_fusion.3
  798.4 0.8 copy.119
  799.2 2.0 convert_add_fusion.2
  (213 shorter events, 23.4 us)
Async XLA Ops:
  7.2 206.6 %all-gather.3.cloned.1.call-start = ((), (), s32[]{:S(2)}) async-start(), calls=%async_computation.2 | async-start | bytes 14413824 | tf_op jit(solution)/shard_map/all_gather | solution.py:1397
  9.9 7.1 copy-start.17
  13.5 3.6 copy-start.14
  17.1 2.3 copy-start.2
  19.4 0.8 copy-start.4
  98.1 3.4 copy-start.3
  101.5 0.6 copy-start.5
  102.2 0.6 copy-start.6
  102.8 0.6 copy-start.8
  103.4 110.4 %copy-start = (bf16[2,512,1152]{2,1,0:T(8,128)(2,1)}, bf16[2,512,1152]{2,1,0:T(8,128)(2,1)S(1)}, u32[]{:S(2)}) copy-start(bf16[2,512,1152]{2,1,0:T(8,128)(2,1)S(1)} %get-tuple-element.48) | copy-start | bytes 7077892
  105.8 196.6 %all-gather.5.cloned.1.call-start = ((), (), s32[]{:S(2)}) async-start(), calls=%async_computation.3 | async-start | bytes 11280384 | tf_op jit(solution)/shard_map/all_gather | solution.py:1401
  105.9 9.7 %collective-permute-start.1 = (bf16[72,2304]{1,0:T(8,128)(2,1)}, bf16[72,2304]{1,0:T(8,128)(2,1)}, u32[]{:S(2)}, u32[]{:S(2)}) collective-permute-start(bf16[72,2304]{1,0:T(8,128)(2,1)} %bitcast.152), channel_id=1, source_target_pairs={{0,1},{1,0},{2,3},{3,2},{4,5},{5,4},{6,7},{7,6},{8,9},{9,8},{10,11... | collective-permute-start | bytes 995336 | tf_op jit(solution)/shard_map/ppermute | solution.py:1342
  117.6 328.2 %reduce-scatter.3.cloned.1.call-start = ((), (), s32[]{:S(2)}) async-start(), calls=%async_computation.4 | async-start | bytes 11280384 | tf_op jit(solution)/shard_map/reduce_scatter | solution.py:1427
  118.0 11.1 %copy-start.10 = (bf16[2,512,1152]{2,1,0:T(8,128)(2,1)S(1)}, bf16[2,512,1152]{2,1,0:T(8,128)(2,1)}, u32[]{:S(2)}) copy-start(bf16[2,512,1152]{2,1,0:T(8,128)(2,1)} %constant_dynamic-slice_fusion.4) | copy-start | bytes 7077892
  120.5 36.3 %copy-start.32 = (f32[2,1024]{1,0:T(2,128)}, f32[2,1024]{1,0:T(2,128)S(1)}, u32[]{:S(2)}) copy-start(f32[2,1024]{1,0:T(2,128)S(1)} %broadcast_multiply_fusion.3) | copy-start | bytes 24580
  123.4 33.4 %copy-start.41 = (f32[2,1024]{1,0:T(2,128)}, f32[2,1024]{1,0:T(2,128)S(1)}, u32[]{:S(2)}) copy-start(f32[2,1024]{1,0:T(2,128)S(1)} %add_rsqrt_fusion.1) | copy-start | bytes 24580
  129.1 29.1 %copy-start.19 = (f32[2,1,1152]{2,1,0:T(1,128)}, f32[2,1,1152]{2,1,0:T(1,128)S(1)}, u32[]{:S(2)}) copy-start(f32[2,1,1152]{2,1,0:T(1,128)S(1)} %get-tuple-element.169) | copy-start | bytes 27652
  129.1 29.8 %copy-start.21 = (f32[2,1,1152]{2,1,0:T(1,128)}, f32[2,1,1152]{2,1,0:T(1,128)S(1)}, u32[]{:S(2)}) copy-start(f32[2,1,1152]{2,1,0:T(1,128)S(1)} %get-tuple-element.171) | copy-start | bytes 27652
  129.1 27.7 %copy-start.36 = (f32[2,1152]{1,0:T(2,128)}, f32[2,1152]{1,0:T(2,128)S(1)}, u32[]{:S(2)}) copy-start(f32[2,1152]{1,0:T(2,128)S(1)} %get-tuple-element.186) | copy-start | bytes 27652
  129.1 27.7 %copy-start.38 = (f32[2,1152]{1,0:T(2,128)}, f32[2,1152]{1,0:T(2,128)S(1)}, u32[]{:S(2)}) copy-start(f32[2,1152]{1,0:T(2,128)S(1)} %get-tuple-element.187) | copy-start | bytes 27652
  129.1 28.3 %copy-start.35 = (bf16[2,576]{1,0:T(2,128)(2,1)S(1)}, bf16[2,576]{1,0:T(2,128)(2,1)}, u32[]{:S(2)}) copy-start(bf16[2,576]{1,0:T(2,128)(2,1)} %param.20) | copy-start | bytes 6916
  129.1 28.4 %copy-start.7 = (f32[36,128]{1,0:T(8,128)S(1)}, f32[36,128]{1,0:T(8,128)}, u32[]{:S(2)}) copy-start(f32[36,128]{1,0:T(8,128)} %copy-done.6) | copy-start | bytes 55300
  129.1 28.4 %copy-start.18 = (f32[2304]{0:T(1024)S(1)}, f32[2304]{0:T(1024)}, u32[]{:S(2)}) copy-start(f32[2304]{0:T(1024)} %copy-done.17) | copy-start | bytes 27652
  156.8 52.2 %collective-permute-start = (bf16[2,512,1152]{2,1,0:T(8,128)(2,1)}, bf16[2,512,1152]{2,1,0:T(8,128)(2,1)}, u32[]{:S(2)}, u32[]{:S(2)}) collective-permute-start(bf16[2,512,1152]{2,1,0:T(8,128)(2,1)} %get-tuple-element.55), channel_id=1, source_target_pairs={{0,1},{1,0},{2,3},{3,2},{4,5},{5,4},{6,7},{7,6},{8,9},{9,8},{10,11... | collective-permute-start | bytes 7077896 | tf_op jit(solution)/shard_map/ppermute | solution.py:1342
  158.2 50.9 %copy-start.23 = (f32[2,1,1152]{2,0,1:T(2,128)}, f32[2,1,1152]{2,0,1:T(2,128)S(1)}, u32[]{:S(2)}) copy-start(f32[2,1,1152]{2,0,1:T(2,128)S(1)} %copy.150) | copy-start | bytes 27652
  158.9 54.9 %copy-start.25 = (f32[2,1152]{1,0:T(2,128)}, f32[2,1152]{1,0:T(2,128)S(1)}, u32[]{:S(2)}) copy-start(f32[2,1152]{1,0:T(2,128)S(1)} %get-tuple-element.185) | copy-start | bytes 27652
  158.9 50.2 %copy-start.11 = (bf16[2,512,1152]{2,1,0:T(8,128)(2,1)S(1)}, bf16[2,512,1152]{2,1,0:T(8,128)(2,1)}, u32[]{:S(2)}) copy-start(bf16[2,512,1152]{2,1,0:T(8,128)(2,1)} %get-tuple-element.157) | copy-start | bytes 7077892
  226.4 5.1 copy-start.9
  227.5 47.5 %slice-start = ((s8[4718592]{0:T(1024)(128)(4,1)}), s8[524288]{0:T(1024)(128)(4,1)S(1)}, s32[]{:S(2)}) async-start(s8[4718592]{0:T(1024)(128)(4,1)} %bitcast.144), calls=%async_computation.6 | async-start | bytes 1048576
  231.5 43.5 %slice-start.1 = ((s8[4718592]{0:T(1024)(128)(4,1)}), s8[4194304]{0:T(1024)(128)(4,1)S(1)}, s32[]{:S(2)}) async-start(s8[4718592]{0:T(1024)(128)(4,1)} %bitcast.144), calls=%async_computation.7 | async-start | bytes 8388608
  302.3 34.8 %slice-start.2 = ((s8[4718592]{0:T(1024)(128)(4,1)}), s8[524288]{0:T(1024)(128)(4,1)S(1)}, s32[]{:S(2)}) async-start(s8[4718592]{0:T(1024)(128)(4,1)} %bitcast.147), calls=%async_computation.8 | async-start | bytes 1048576
  302.3 332.3 %reduce-scatter.5.cloned.1.call-start = ((), (), s32[]{:S(2)}) async-start(), calls=%async_computation.5 | async-start | bytes 14413824 | tf_op jit(solution)/shard_map/reduce_scatter | solution.py:1449
  302.4 34.7 %slice-start.3 = ((s8[4718592]{0:T(1024)(128)(4,1)}), s8[4194304]{0:T(1024)(128)(4,1)S(1)}, s32[]{:S(2)}) async-start(s8[4718592]{0:T(1024)(128)(4,1)} %bitcast.147), calls=%async_computation.9 | async-start | bytes 8388608
  364.6 34.8 %copy-start.12 = (bf16[2,512,1152]{2,1,0:T(8,128)(2,1)S(1)}, bf16[2,512,1152]{2,1,0:T(8,128)(2,1)}, u32[]{:S(2)}) copy-start(bf16[2,512,1152]{2,1,0:T(8,128)(2,1)} %get-tuple-element.157) | copy-start | bytes 7077892
  364.7 34.8 %copy-start.24 = (f32[2,1,1152]{2,0,1:T(2,128)S(1)}, f32[2,1,1152]{2,0,1:T(2,128)}, u32[]{:S(2)}) copy-start(f32[2,1,1152]{2,0,1:T(2,128)} %copy-done.23) | copy-start | bytes 27652
  364.7 34.8 %copy-start.40 = (f32[1152]{0:T(1024)S(1)}, f32[1152]{0:T(1024)}, u32[]{:S(2)}) copy-start(f32[1152]{0:T(1024)} %get-tuple-element.142) | copy-start | bytes 13828
  399.5 39.7 %copy-start.26 = (f32[2,1152]{1,0:T(2,128)S(1)}, f32[2,1152]{1,0:T(2,128)}, u32[]{:S(2)}) copy-start(f32[2,1152]{1,0:T(2,128)} %copy-done.25) | copy-start | bytes 27652
  479.1 2.3 copy-start.1
  481.5 9.4 %copy-start.22 = (f32[2,1,1152]{2,1,0:T(1,128)S(1)}, f32[2,1,1152]{2,1,0:T(1,128)}, u32[]{:S(2)}) copy-start(f32[2,1,1152]{2,1,0:T(1,128)} %copy-done.21) | copy-start | bytes 27652
  481.5 9.4 %copy-start.20 = (f32[2,1,1152]{2,1,0:T(1,128)S(1)}, f32[2,1,1152]{2,1,0:T(1,128)}, u32[]{:S(2)}) copy-start(f32[2,1,1152]{2,1,0:T(1,128)} %copy-done.19) | copy-start | bytes 27652
  481.5 12.1 %copy-start.34 = (f32[1,4608]{1,0:T(1,128)S(1)}, f32[1,4608]{1,0:T(1,128)}, u32[]{:S(2)}) copy-start(f32[1,4608]{1,0:T(1,128)} %get-tuple-element.76) | copy-start | bytes 55300
  490.6 139.3 %collective-permute-start.2 = (bf16[2,512,1152]{2,1,0:T(8,128)(2,1)}, bf16[2,512,1152]{2,1,0:T(8,128)(2,1)}, u32[]{:S(2)}, u32[]{:S(2)}) collective-permute-start(bf16[2,512,1152]{2,1,0:T(8,128)(2,1)} %get-tuple-element.156), channel_id=1, source_target_pairs={{0,1},{1,0},{2,3},{3,2},{4,5},{5,4},{6,7},{7,6},{8,9},{9,8},{10,11... | collective-permute-start | bytes 7077896 | tf_op jit(solution)/shard_map/ppermute | solution.py:1342
  495.4 132.7 %collective-permute-start.6 = (bf16[72,2304]{1,0:T(8,128)(2,1)}, bf16[72,2304]{1,0:T(8,128)(2,1)}, u32[]{:S(2)}, u32[]{:S(2)}) collective-permute-start(bf16[72,2304]{1,0:T(8,128)(2,1)} %split.32), channel_id=1, source_target_pairs={{0,1},{1,0},{2,3},{3,2},{4,5},{5,4},{6,7},{7,6},{8,9},{9,8},{10,11... | collective-permute-start | bytes 995336 | tf_op jit(solution)/shard_map/ppermute | solution.py:1342
  497.2 104.6 %copy-start.33 = (f32[2,1024]{1,0:T(2,128)S(1)}, f32[2,1024]{1,0:T(2,128)}, u32[]{:S(2)}) copy-start(f32[2,1024]{1,0:T(2,128)} %copy-done.32) | copy-start | bytes 24580
  497.2 104.6 %copy-start.37 = (f32[2,1152]{1,0:T(2,128)S(1)}, f32[2,1152]{1,0:T(2,128)}, u32[]{:S(2)}) copy-start(f32[2,1152]{1,0:T(2,128)} %copy-done.36) | copy-start | bytes 27652
  497.2 104.6 %copy-start.39 = (f32[2,1152]{1,0:T(2,128)S(1)}, f32[2,1152]{1,0:T(2,128)}, u32[]{:S(2)}) copy-start(f32[2,1152]{1,0:T(2,128)} %copy-done.38) | copy-start | bytes 27652
  497.2 104.6 %copy-start.42 = (f32[2,1024]{1,0:T(2,128)S(1)}, f32[2,1024]{1,0:T(2,128)}, u32[]{:S(2)}) copy-start(f32[2,1024]{1,0:T(2,128)} %copy-done.41) | copy-start | bytes 24580
  601.8 26.2 %copy-start.15 = (bf16[72,4608]{1,0:T(8,128)(2,1)S(1)}, bf16[72,4608]{1,0:T(8,128)(2,1)}, u32[]{:S(2)}) copy-start(bf16[72,4608]{1,0:T(8,128)(2,1)} %reduce-scatter.3.cloned.1.call-done) | copy-start | bytes 1990660
  638.0 99.1 %copy-start.28 = (bf16[2,1,1152]{2,1,0:T(2,128)(2,1)S(1)}, bf16[2,1,1152]{2,1,0:T(2,128)(2,1)}, u32[]{:S(2)}) copy-start(bf16[2,1,1152]{2,1,0:T(2,128)(2,1)} %copy.111) | copy-start | bytes 13828
  638.0 99.1 %copy-start.29 = (bf16[2,1,1152]{2,1,0:T(2,128)(2,1)S(1)}, bf16[2,1,1152]{2,1,0:T(2,128)(2,1)}, u32[]{:S(2)}) copy-start(bf16[2,1,1152]{2,1,0:T(2,128)(2,1)} %copy.114) | copy-start | bytes 13828
  638.0 99.1 %copy-start.30 = (bf16[2,1,1152]{2,1,0:T(2,128)(2,1)S(1)}, bf16[2,1,1152]{2,1,0:T(2,128)(2,1)}, u32[]{:S(2)}) copy-start(bf16[2,1,1152]{2,1,0:T(2,128)(2,1)} %copy.112) | copy-start | bytes 13828
  638.0 99.1 %copy-start.31 = (bf16[2,1,1152]{2,1,0:T(2,128)(2,1)S(1)}, bf16[2,1,1152]{2,1,0:T(2,128)(2,1)}, u32[]{:S(2)}) copy-start(bf16[2,1,1152]{2,1,0:T(2,128)(2,1)} %copy.113) | copy-start | bytes 13828
  638.0 145.3 %copy-start.27 = (bf16[4,1152]{1,0:T(4,128)(2,1)S(1)}, bf16[4,1152]{1,0:T(4,128)(2,1)}, u32[]{:S(2)}) copy-start(bf16[4,1152]{1,0:T(4,128)(2,1)} %param.13) | copy-start | bytes 27652
  736.2 54.2 %copy-start.13 = (bf16[2,512,1152]{2,1,0:T(8,128)(2,1)S(1)}, bf16[2,512,1152]{2,1,0:T(8,128)(2,1)}, u32[]{:S(2)}) copy-start(bf16[2,512,1152]{2,1,0:T(8,128)(2,1)} %get-tuple-element.155) | copy-start | bytes 7077892
  771.6 27.6 %collective-permute-start.5 = (bf16[72,2304]{1,0:T(8,128)(2,1)}, bf16[72,2304]{1,0:T(8,128)(2,1)}, u32[]{:S(2)}, u32[]{:S(2)}) collective-permute-start(bf16[72,2304]{1,0:T(8,128)(2,1)} %split.30), channel_id=1, source_target_pairs={{0,1},{1,0},{2,3},{3,2},{4,5},{5,4},{6,7},{7,6},{8,9},{9,8},{10,11... | collective-permute-start | bytes 995336 | tf_op jit(solution)/shard_map/ppermute | solution.py:1342
  773.8 22.6 %collective-permute-start.4 = (bf16[72,640]{1,0:T(8,128)(2,1)}, bf16[72,640]{1,0:T(8,128)(2,1)S(1)}, u32[]{:S(2)}, u32[]{:S(2)}) collective-permute-start(bf16[72,640]{1,0:T(8,128)(2,1)} %get-tuple-element.160), channel_id=1, source_target_pairs={{0,1},{1,0},{2,3},{3,2},{4,5},{5,4},{6,7},{7,6},{8,9},{9,8},{10,11... | collective-permute-start | bytes 276488 | tf_op jit(solution)/shard_map/ppermute | solution.py:1342
  775.6 21.5 %collective-permute-start.3 = (bf16[72,1920]{1,0:T(8,128)(2,1)}, bf16[72,1920]{1,0:T(8,128)(2,1)}, u32[]{:S(2)}, u32[]{:S(2)}) collective-permute-start(bf16[72,1920]{1,0:T(8,128)(2,1)} %split.38), channel_id=1, source_target_pairs={{0,1},{1,0},{2,3},{3,2},{4,5},{5,4},{6,7},{7,6},{8,9},{9,8},{10,11... | collective-permute-start | bytes 829448 | tf_op jit(solution)/shard_map/ppermute | solution.py:1342
  790.4 6.7 copy-start.16
Sparse Core Ops, SparseCore 0:
  105.9 103.5 all-gather.2
  212.4 86.9 all-gather.4
  303.4 131.2 reduce-scatter.2
  479.3 155.3 reduce-scatter.4

commit v5 on v4

--- a/solution.py
+++ b/solution.py
@@ -15,6 +15,7 @@
 f32 = jnp.float32
 bf16 = jnp.bfloat16
 NT = (((1,), (1,)), ((), ()))
+TN = (((0,), (0,)), ((), ()))
 MESH = pl.DeviceIdType.MESH
 
 
@@ -350,10 +351,11 @@
         )
         for ref in (q_ref, k_ref)
     ]
-    small = jnp.max(longest[0] * longest[1]) * (1.1 * c * c) < 60.0 * 60.0
-
-    def run(shifted):
-        def pair(i, carry):
+    bound = longest[0] * longest[1] * (1.1 * c * c)
+    which = lax.broadcasted_iota(jnp.int32, bound.shape, 0) // 2
+
+    def pair(i, carry):
+        def run(shifted):
             steps = [(2 * i + odd, b) for odd in range(2) for b in range(seq // blk)]
 
             def scores(head, b):
@@ -383,12 +385,13 @@
                 ot_ref[mine, rows] = ot[:HEAD_DIM] * (1.0 / l)
                 lse_ref[0, 0, pl.ds(head, 1), rows] = jnp.log2(l) + m * c if shifted else jnp.log2(l)
                 st = after
-            return carry
-
-        lax.fori_loop(0, heads // 2, pair, 0)
-
-    pl.when(small)(lambda: run(False))
-    pl.when(jnp.logical_not(small))(lambda: run(True))
+
+        small = jnp.max(jnp.where(which == i, bound, 0.0)) < 85.0 * 85.0
+        pl.when(small)(lambda: run(False))
+        pl.when(jnp.logical_not(small))(lambda: run(True))
+        return carry
+
+    lax.fori_loop(0, heads // 2, pair, 0)
     o_ref[0] = ot_ref[...].T.astype(bf16)
 
 
@@ -918,9 +921,9 @@
 
 
 def closing_kernel(
-    mod_ref, bias_ref, mod_w_ref,
-    mod_out, bias_out, cond_out,
-    mod_unit, bias_unit, bias_in, part_ref, cond_in,
+    mod_ref, bias_ref, mod_w_ref, conds_ref,
+    bias_out, cond_out, weight_out, sum_out,
+    mod_out, mod_unit, bias_unit, bias_in, part_ref, cond_in,
     x_send, x_recv, m_send, m_recv, b_send, b_recv, c_send, c_recv,
 ):
     side = lax.axis_index("tensor")
@@ -953,6 +956,17 @@
     ).reshape(groups, rows, lanes)
     conds = Exchange(part_ref, cond_in, c_send, c_recv)
     conds.begin()
+    values = conds_ref[...].reshape(groups * rows, conds_ref.shape[2]).astype(bf16)
+    ahead = lax.broadcasted_iota(jnp.int32, values.shape, 0) % rows < rows // 2
+    depth, cols = weight_out.shape[1:]
+    whole = jnp.sum(mod_out[...], axis=0)
+    for k in range(2):
+        picked = jnp.where(ahead == (k == 0), values, jnp.zeros_like(values))
+        grad = lax.dot_general(picked, low, TN, preferred_element_type=f32)[:depth]
+        total = jnp.sum(whole[k * (rows // 2) : (k + 1) * (rows // 2)], axis=0, keepdims=True)
+        for j in range(3):
+            weight_out[3 * k + j] = grad[:, j * cols : (j + 1) * cols]
+            sum_out[3 * k + j] = total[:, j * cols : (j + 1) * cols]
     biases.finish()
     bias_out[...] = jnp.sum(bias_in[...], axis=0)
     conds.finish()
@@ -963,7 +977,7 @@
     conds.drain()
 
 
-def closing(mod_pair, bias_pair, mod_weight):
+def closing(mod_pair, bias_pair, mod_weight, conds):
     groups = lax.axis_size("dp")
     rows, half = mod_pair.shape[1:]
     depth = mod_weight.shape[0]
@@ -973,14 +987,16 @@
     lines = bias_pair.shape[1]
     return pl.pallas_call(
         closing_kernel,
-        in_specs=[vmem, vmem, vmem],
-        out_specs=[vmem, vmem, vmem],
+        in_specs=[vmem] * 4,
+        out_specs=[vmem] * 4,
         out_shape=[
-            jax.ShapeDtypeStruct((groups, rows, half), f32),
             jax.ShapeDtypeStruct((lines, 128), f32),
             jax.ShapeDtypeStruct((2, groups, rows, 128), f32),
+            jax.ShapeDtypeStruct((6, depth, half // 3), f32),
+            jax.ShapeDtypeStruct((6, 1, half // 3), f32),
         ],
         scratch_shapes=[
+            pltpu.VMEM((groups, rows, half), f32),
             pltpu.VMEM((2, rows, half), f32),
             pltpu.VMEM((2, lines, 128), f32),
             pltpu.VMEM((groups, lines, 128), f32),
@@ -994,7 +1010,7 @@
         compiler_params=pltpu.CompilerParams(collective_id=1, has_side_effects=True, vmem_limit_bytes=32 << 20),
         cost_estimate=pl.CostEstimate(flops=0, bytes_accessed=0, transcendentals=0),
         name="closing",
-    )(mod_pair, bias_pair, weights)
+    )(mod_pair, bias_pair, weights, conds)
 
 
 class Collect:
@@ -1193,22 +1209,26 @@
 
 def latents_backward_kernel(
     dqkv_ref, w_ref, lat_ref, first_ref, scale_ref, grads_ref,
-    out_ref, sums_ref, totals_ref, rows_in, from_core, from_row, from_z,
-    rows_out, x_send, x_recv, *collect,
+    out_ref, sums_ref, totals_ref, from_core, from_row, from_z,
+    tiles, x_send, x_recv, kept, *collect,
 ):
     side = lax.axis_index("tensor")
     r = pl.program_id(0)
     engine = Collect(grads_ref, totals_ref, from_core, from_row, from_z, *collect)
-    count, half_seq, _ = rows_in.shape
+    both, half_seq, _ = out_ref.shape
+    count = both // 2
     per_half = half_seq // TILE
     sent = count * per_half
 
+    def place_of(i):
+        rows = pl.ds(pl.multiple_of(i % per_half * TILE, TILE), TILE)
+        return out_ref.at[side * count + i // per_half, rows]
+
     def row_copy(i):
-        return to_partner(
-            rows_out.at[i],
-            rows_in.at[i // per_half, pl.ds(pl.multiple_of(i % per_half * TILE, TILE), TILE)],
-            side, x_send, x_recv, i,
-        )
+        return to_partner(tiles.at[i], place_of(i), side, x_send, x_recv, i)
+
+    def keep_copy(i):
+        return pltpu.make_async_copy(tiles.at[sent + i], place_of(i), kept.at[i])
 
     @pl.when(r == 0)
     def _():
@@ -1227,13 +1247,9 @@
             [jnp.sum(grad, axis=0, keepdims=True), jnp.sum(grad * norm, axis=0, keepdims=True)], axis=0
         )
         back = normed_back(grad * (1.0 + scale_ref[0]), norm, inverse)
-        result = (first_ref[...] + back).astype(bf16)
-        out_ref[...] = result
-
-        @pl.when(r < sent)
-        def _():
-            rows_out[r] = result
-            row_copy(r).start()
+        tiles[r] = (first_ref[...] + back).astype(bf16)
+        pl.when(r < sent)(lambda: row_copy(r).start())
+        pl.when(r >= sent)(lambda: keep_copy(r - sent).start())
 
     engine.finish_round(r)
 
@@ -1242,6 +1258,7 @@
         engine.end()
         for i in range(sent):
             row_copy(i).wait()
+            keep_copy(i).wait()
 
 
 def latents_backward(dqkv, w, lat, first_grad, scale, grads):
@@ -1275,25 +1292,25 @@
             anywhere,
         ],
         out_specs=[
-            rows(width),
+            anywhere,
             pl.BlockSpec((count, 2, width), lambda r: (0, 0, 0)),
             pl.BlockSpec((depth, wide), lambda r: (0, 0)),
         ]
-        + [anywhere] * 4,
+        + [anywhere] * 3,
         out_shape=[
-            jax.ShapeDtypeStruct((count * seq, width), bf16),
+            jax.ShapeDtypeStruct((2 * count, seq // 2, width), bf16),
             jax.ShapeDtypeStruct((count, 2, width), f32),
             jax.ShapeDtypeStruct((depth, wide), f32),
-            jax.ShapeDtypeStruct((count, seq // 2, width), bf16),
         ]
         + arrivals,
-        scratch_shapes=[pltpu.VMEM((sent, TILE, width), bf16), dma((sent,)), dma((sent,))] + scratch,
+        scratch_shapes=[pltpu.VMEM((2 * sent, TILE, width), bf16), dma((sent,)), dma((sent,)), dma((sent,))]
+        + scratch,
         compiler_params=pltpu.CompilerParams(
             collective_id=2, has_side_effects=True, vmem_limit_bytes=56 << 20
         ),
         cost_estimate=pl.CostEstimate(flops=0, bytes_accessed=0, transcendentals=0),
         name="latents_backward",
-    )(flat(dqkv), w, flat(lat), flat(first_grad), scale, grads.reshape(groups, depth, wide))[:4]
+    )(flat(dqkv), w, flat(lat), flat(first_grad), scale, grads.reshape(groups, depth, wide))[:3]
 
 
 def normed(values):
@@ -1387,7 +1404,6 @@
     mod_parts = mod_parts.reshape(2, 2, count, 3, cols)
     mod_parts = own_latents(mod_parts, 2).transpose(0, 2, 1, 3, 4).reshape(2, own, 6, cols)
     modulation = in_order(mod_parts[0], mod_parts[1], 2)
-    cond_cols = cond_blocks[:, :count, :depth].reshape(groups * count, depth).astype(bf16)
     branch_all = in_order(branch, branch_in, 1)
     row = lambda k: modulation[:, k][:, None, :]
     shift_a, scale_a, gate_a, shift_m, scale_m, gate_m = [row(k) for k in range(6)]
@@ -1397,10 +1413,6 @@
     up_mix = lax.all_gather(jnp.concatenate(pieces, axis=1), "dp", axis=0, tiled=True)
     up_all = up_mix[:, :hidden]
     mix_t = up_mix[:, hidden:]
-    down_mine, _ = lax.optimization_barrier((down_weight.T, latent_in))
-    down_t = lax.all_gather(
-        jnp.concatenate([down_mine, swap(down_mine)], axis=1), "dp", axis=0, tiled=True
-    )
     up_bias_f = jnp.concatenate([flat[2], biases_in[4 * cols :]])
 
     lat = jnp.concatenate([own_latents(latent), latent_in], axis=1)
@@ -1412,7 +1424,10 @@
         [c for b in (roomy(head_bias.astype(f32)), roomy(head_bias_in)) for c in (b[0], empty, b[1])]
     )
     qkv = (mm("bsd,dc->bsc", attn_in, head_all) + qkv_bias).astype(bf16)
-    later, qkv = lax.optimization_barrier((other_latents(cotangent), qkv))
+    later, down_mine, qkv = lax.optimization_barrier((other_latents(cotangent), down_weight.T, qkv))
+    down_t = lax.all_gather(
+        jnp.concatenate([down_mine, swap(down_mine)], axis=1), "dp", axis=0, tiled=True
+    )
     upstream_low = jnp.concatenate([own_latents(cotangent), swap(later)], axis=1)
     mixed, logsum = attn_fwd(qkv, heads)
     attn_out = mm("bsc,dc->bsd", mixed, mix_t) + branch_all[0]
@@ -1452,7 +1467,7 @@
     head_grad = mm("bsd,bsc->dc", attn_in, qkv_grad).astype(bf16)
     head_grad, up_sum, block_in = lax.optimization_barrier((head_grad, up_sum, block_in))
     block_out = placed(block, block_in)
-    lat_grad, sums, head_sum, lat_grad_in = latents_backward(
+    latent_grad, sums, head_sum = latents_backward(
         qkv_grad, head_all, lat, first_grad, scale_a, head_grad
     )
     shift_a_grad, scale_a_grad = sums[:, 0], sums[:, 1]
@@ -1476,17 +1491,15 @@
         return flat.reshape(-1, 128)
 
     mod_pair = jnp.stack([mod_share(side), mod_share(1 - side)])
-    mod_blocks, biases, cond_parts = closing(
+    biases, cond_parts, mod_weight_grad, mod_bias_grad = closing(
         mod_pair,
         jnp.stack([bias_share(side, 0), bias_share(1 - side, 1)]),
         mod_weight,
-    )
-    latent_grad = placed(lat_grad.reshape(own, 2 * half_seq, width), lat_grad_in)
+        cond_blocks,
+    )
     biases = biases.reshape(-1)
-    mod_rows = mod_blocks.astype(bf16).reshape(groups, 2, count, 3, cols)
-    mod_rows = mod_rows.transpose(0, 2, 1, 3, 4).reshape(groups * count, 6, cols)
-    mod_weight_grad = mm("bd,bkc->dkc", cond_cols, mod_rows)
-    mod_bias_grad = jnp.sum(mod_rows, axis=0, dtype=f32)
+    mod_weight_grad = mod_weight_grad.transpose(1, 0, 2)
+    mod_bias_grad = mod_bias_grad[:, 0]
     cond_act = jnp.sum(cond_parts[..., :depth].reshape(2, groups, 2, count, depth), axis=(0, 2))
     cond_act = cond_act.transpose(1, 0, 2).reshape(count, groups * depth)
     gate = jax.nn.sigmoid(cond_f)

time: 811 us -> 792 us (0.977)
  local copies, waits for them, and re-layouts: 59.1 us -> 49 us
    pallas_call x1, Pallas kernels: 98.2 us -> 87.6 us  [latents_backward(): pl.pallas_call(latents_backward_kernel, grid=(max(pieces + 5, 2 * sent),)...]
    pallas_call x1, Pallas kernels: 46.6 us -> 55.7 us  [attn_fwd(): pl.pallas_call(partial(attn_fwd_kernel, blk=blk, heads=heads), grid=(n, 2...]
    unnamed x108 -> x111, local copies, waits for them, and re-layouts: 12.1 us -> 20 us
    dot_general x10 -> x9, matrix products: 219 us -> 216 us  [mm(): return jnp.einsum(spec, a, b, preferred_element_type=f32)]
  transfers between devices with their start and end apart: 11 -> 11, of which waited for: 3 -> 1; matrix products, arithmetic and copies ran while one was open for 34% -> 32% of each run, Pallas kernels for 28% -> 45%
where the time goes in v5:
time: 792 us; the launch traced here: 785 us
  Pallas kernels  434 us (55%)
  matrix products  216 us (27%)
  other arithmetic  55.4 us (7%)
  local copies, waits for them, and re-layouts  49 us (6%)
  between operations  15.2 us (2%)
  waiting for transfers between devices  9.12 us (1%)
    dot_general x9, matrix products, mm(): return jnp.einsum(spec, a, b, preferred_element_type=f32)  216 us
    pallas_call x1, Pallas kernels, attn_bwd(): pl.pallas_call(partial(attn_bwd_kernel, blk=blk, heads=heads), grid=(n, 2...  104 us
    pallas_call x1, Pallas kernels, latents_backward(): pl.pallas_call(latents_backward_kernel, grid=(max(pieces + 5, 2 * sent),)...  87.6 us
    pallas_call x1, Pallas kernels, opening(): pl.pallas_call(opening_kernel, in_specs=[vmem, vmem, vmem, vmem, anywhere...  77.9 us
    pallas_call x1, Pallas kernels, attn_fwd(): pl.pallas_call(partial(attn_fwd_kernel, blk=blk, heads=heads), grid=(n, 2...  55.7 us
    pallas_call x1, Pallas kernels, up_forward(): pl.pallas_call(up_forward_kernel, grid=(hidden // cols, count * seq // ro...  43.5 us
    pallas_call x1, Pallas kernels, down_backward(): pl.pallas_call(down_backward_kernel, grid=(hidden // cols, count * seq //...  35.4 us
    pallas_call x1, Pallas kernels, closing(): pl.pallas_call(closing_kernel, in_specs=[vmem] * 4, out_specs=[vmem] * 4,...  29.8 us
  transfers between devices with their start and end apart: 11, of which 1 were waited for; matrix products, arithmetic and copies ran while one was open for 32% of the time, Pallas kernels for 45%

profile of v5, /device:TPU:0, one launch (start us, length us, event | category | flops | bytes accessed | tf_op | source)
XLA Modules:
  0.0 785.2 jit_solution(15851281347783206818)
XLA Ops:
  7.2 1.1 copy.74
  8.4 0.7 reshape.191
  9.2 0.7 convert_element_type.100
  9.9 0.8 reshape.195
  10.7 0.8 reshape.196
  11.5 1.1 copy.107
  12.6 0.9 pad.30
  13.7 0.8 reshape.222
  15.1 0.7 fusion.24
  16.0 1.0 pad_maximum_fusion.5.rest_ref
  17.1 2.3 copy-done.2
  19.4 0.8 copy-done.4
  20.2 77.9 %opening.1 = (bf16[16,72,3840]{2,1,0:T(8,128)(2,1)S(1)}, bf16[72,2944]{1,0:T(8,128)(2,1)S(1)}, bf16[2,512,1152]{2,1,0:T(8,128)(2,1)S(1)}, f32[2,8,1728]{2,1,0:T(...) custom-call(f32[16,8,128]{2,1,0:T(8,128)S(1)} %fusion.20.cond_ref, ...), custom_call_target="tpu_custom_call" | custom-call | tf_op jit(solution)/shard_map/opening/pallas_call | solution.py:896
  98.1 3.4 copy-done.3
  103.4 2.3 pad_maximum_fusion.3
  105.9 0.7 convert_element_type.98
  106.6 1.0 reshape.199
  107.7 0.8 fusion.41
  108.7 6.8 constant_dynamic-slice_fusion.2
  115.5 0.7 convert_reduce_fusion.1
  116.2 1.6 fusion.7
  118.7 26.5 %add_convert_fusion.q_ref.k_ref.v_ref = bf16[2,1024,3840]{2,1,0:T(8,128)(2,1)} fusion(f32[3840]{0:T(1024)S(1)} %constant_dynamic-update-slice_fusion, bf16[1152,3840,1]{1,0,2:T(8,128)(2,1)S(1)} %bitcast.128, f32[2,1152]{1,0:T(2,128)S(1)} %get-tuple-element.173, f32[2,1152]{1,0:T(2,128)S(1)} %get-tuple-element.174, f32[2,1024]{1,0:T(2,128)S(1)} %add_rsqrt_fusion.1, ...), kind=kOutput, calls=%fused_computation | convolution fusion | flops 18156355584 | bytes 29344768 | tf_op jit(solution)/shard_map/bsd,dc->bsc/dot_general | solution.py:1332
  145.6 9.0 %collective-permute-done.1 = bf16[72,2304]{1,0:T(8,128)(2,1)S(1)} collective-permute-done((bf16[72,2304]{1,0:T(8,128)(2,1)S(1)}, bf16[72,2304]{1,0:T(8,128)(2,1)S(1)}, u32[]{:S(2)}, u32[]{:S(2)}) %collective-permute-start.1) | collective-permute-done | bytes 331808 | tf_op jit(solution)/shard_map/ppermute | solution.py:1359
  154.6 0.9 pad_maximum_fusion.4
  157.9 55.7 %attention_forward.1 = (bf16[2,1024,1280]{2,1,0:T(8,128)(2,1)}, f32[2,2,8,1024]{3,2,1,0:T(8,128)}) custom-call(bf16[2,1024,3840]{2,1,0:T(8,128)(2,1)} %add_convert_fusion.q_ref.k_ref.v_ref, bf16[2,1024,3840]{2,1,0:T(8,128)(2,1)} %add_convert_fusion.q_ref.k_ref.v_ref, bf16[2,1024,3840]{2,1,0:T(8,128)(2,1)} %add_convert_fusion.q_ref.k_ref.v_ref), custom_call_target="tpu_custom_call" | custom-call | flops 10737418240 | bytes 20971520 | tf_op jit(solution)/shard_map/attention_forward/pallas_call | solution.py:402
  213.6 4.7 fusion.11
  218.4 12.8 %fusion.35 = (f32[2,1024]{1,0:T(2,128)S(1)}, f32[2,1024,1152]{2,1,0:T(8,128)S(1)}, f32[2,1024,1152]{2,1,0:T(8,128)}) fusion(f32[1152]{0:T(1024)S(1)} %get-tuple-element.131, f32[2,1152]{1,0:T(2,128)S(1)} %get-tuple-element.172, bf16[2,512,1152]{2,1,0:T(8,128)(2,1)S(1)} %get-tuple-element.48, bf16[2,512,1152]{2,1,0:T(8,128)(2,1)} %copy-done.11, ...), kind=kOutput, calls=%fused_computation.135 | convolution fusion | flops 6058670080 | bytes 31806976 | tf_op jit(solution)/shard_map/bsc,dc->bsd/dot_general | solution.py:1332
  231.2 1.1 multiply_reduce_fusion.3
  232.3 3.7 add_convert_fusion.2
  236.3 43.5 %up_forward.1 = (bf16[2048,4608]{1,0:T(8,128)(2,1)}, bf16[2048,4608]{1,0:T(8,128)(2,1)}) custom-call(bf16[2048,1152]{1,0:T(8,128)(2,1)} %bitcast.138, bf16[1152,5888]{1,0:T(8,128)(2,1)} %all-gather.3.cloned.1.call-done.w_ref, f32[1,4608]{1,0:T(1,128)} %reshape.204.b_ref), custom_call_target="tpu_custom_call" | custom-call | flops 21743271936 | bytes 37748736 | tf_op jit(solution)/shard_map/up_forward/pallas_call | solution.py:551
  279.8 27.8 %fusion = bf16[1152,4608]{1,0:T(8,128)(2,1)} fusion(bf16[2,1024,1152]{2,1,0:T(8,128)(2,1)S(1)} %bitcast.137, bf16[2,1024,4608]{2,1,0:T(8,128)(2,1)} %bitcast.161), kind=kOutput, calls=%fused_computation.3 | convolution fusion | flops 21748580352 | bytes 34209792 | tf_op jit(solution)/shard_map/bsd,bsf->df/dot_general | solution.py:1332
  307.8 35.4 %down_backward.1 = (bf16[2048,4608]{1,0:T(8,128)(2,1)}, f32[1,4608]{1,0:T(1,128)}) custom-call(bf16[2048,1152]{1,0:T(8,128)(2,1)} %bitcast.135, bf16[1152,4608]{1,0:T(8,128)(2,1)} %all-gather.5.cloned.1.call-done.w_ref, bf16[2048,4608]{1,0:T(8,128)(2,1)} %get-tuple-element.60.slope_ref), custom_call_target="tpu_custom_call" | custom-call | flops 21743271936 | bytes 37748736 | tf_op jit(solution)/shard_map/down_backward/pallas_call | solution.py:594
  343.2 27.3 %fusion.1 = bf16[1152,4608]{1,0:T(8,128)(2,1)} fusion(bf16[2,1024,1152]{2,1,0:T(8,128)(2,1)S(1)} %bitcast.140, bf16[2,1024,4608]{2,1,0:T(8,128)(2,1)} %bitcast.163), kind=kOutput, calls=%fused_computation.4 | convolution fusion | flops 21748580352 | bytes 34209792 | tf_op jit(solution)/shard_map/bsd,bsf->df/dot_general | solution.py:1332
  370.5 34.8 %multiply_reduce_fusion = (bf16[2,1152]{1,0:T(2,128)(2,1)S(1)}, f32[2,1024]{1,0:T(2,128)S(1)}, f32[2,1024]{1,0:T(2,128)S(1)}, bf16[2,1152]{1,0:T(2,128)(2,1)S(1)}, f32[2,1024,1152]{2,1,0:T(8,128)}) fusion(f32[2,1024,1152]{2,1,0:T(8,128)} %copy-done.10, f32[2,1024]{1,0:T(2,128)S(1)} %add_rsqrt_fusion, f32[2,1024]{1,0:T(2,128)S(1)} %broadcast_multiply_fusion.2, ...), kind=kOutput, calls=%fused_computation.26 | convolution fusion | flops 21764497408 | bytes 48416768 | tf_op jit(solution)/shard_map/bsf,df->bsd/dot_general | solution.py:1332
  405.3 39.6 %convert_reduce_fusion = (f32[2,1152]{1,0:T(2,128)S(1)}, bf16[2,1152]{1,0:T(2,128)(2,1)S(1)}, bf16[2,1024,1152]{2,1,0:T(8,128)(2,1)}, bf16[2,1152]{1,0:T(2,128)(...) fusion(bf16[2,512,1152]{2,1,0:T(8,128)(2,1)} %collective-permute-done, ...), kind=kOutput, calls=%fused_computation.6 | convolution fusion | flops 21797527552 | bytes 76765184 | tf_op jit(solution)/shard_map/bsf,df->bsd/dot_general | solution.py:1332
  445.0 6.6 multiply_convert_fusion
  451.6 10.3 %fusion.13 = bf16[1152,1280]{1,0:T(8,128)(2,1)S(1)} fusion(bf16[2,1024,1152]{2,1,0:T(8,128)(2,1)} %multiply_convert_fusion, bf16[2,1024,1280]{2,1,0:T(8,128)(2,1)} %get-tuple-element.53.o_ref), kind=kOutput, calls=%fused_computation.36 | convolution fusion | flops 6041272320 | bytes 12910592 | tf_op jit(solution)/shard_map/bsd,bsc->dc/dot_general | solution.py:1332
  461.9 11.8 %pad_maximum_fusion = bf16[1152,5888]{1,0:T(8,128)(2,1)} fusion(bf16[1152,1280]{1,0:T(8,128)(2,1)S(1)} %fusion.13, bf16[1152,4608]{1,0:T(8,128)(2,1)} %fusion.1), kind=kLoop, calls=%fused_computation.13 | loop fusion | flops 27131904 | bytes 27131904 | tf_op jit(solution)/shard_map/concatenate | solution.py:1462
  473.7 11.2 %convolution_convert_fusion.do_ref = bf16[2,1024,1280]{2,1,0:T(8,128)(2,1)} fusion(bf16[2,1024,1152]{2,1,0:T(8,128)(2,1)} %multiply_convert_fusion, bf16[1152,5888]{1,0:T(8,128)(2,1)} %all-gather.3.cloned.1.call-done.w_ref), kind=kOutput, calls=%fused_computation.37 | convolution fusion | flops 6042419200 | bytes 12910592 | tf_op jit(solution)/shard_map/bsd,dc->bsc/dot_general | solution.py:1332
  485.1 1.5 copy-done.1
  486.5 4.9 pad_maximum_fusion.1
  491.4 5.7 fusion.36
  497.6 1.8 split.32
  499.4 2.0 collective-permute-start.6
  501.4 103.9 %attention_backward.1 = (bf16[2,1024,3840]{2,1,0:T(8,128)(2,1)}, f32[2,2,1,1920]{3,2,1,0:T(1,128)}) custom-call(bf16[2,1024,3840]{2,1,0:T(8,128)(2,1)} %add_convert_fusion.q_ref.k_ref.v_ref, bf16[2,1024,3840]{2,1,0:T(8,128)(2,1)} %add_convert_fusion.q_ref.k_ref.v_ref, bf16[2,1024,3840]{2,1,0:T(8,128)(2,1)} %add_convert_fusion.q_ref.k_ref.v_ref, ...), custom_call_target="tpu_custom_call" | custom-call | tf_op jit(solution)/shard_map/attention_backward/pallas_call | solution.py:491
  605.3 0.8 reduce_sum.161
  606.3 25.8 %bitcast_convert_fusion = bf16[1152,3840]{1,0:T(8,128)(2,1)} fusion(bf16[2,1024,3840]{2,1,0:T(8,128)(2,1)} %get-tuple-element.68, f32[2,1152]{1,0:T(2,128)S(1)} %copy-done.34, f32[2,1152]{1,0:T(2,128)S(1)} %copy-done.36, f32[2,1024]{1,0:T(2,128)S(1)} %copy-done.39, f32[2,1024]{1,0:T(2,128)S(1)} %copy-done.30, bf16[2,512,1152]{2,1,0:T(8,128)(2,1)S(1)} %copy-done.1, ...), kind=kOutput, calls=%fused_computation.5 | convolution fusion | flops 18145050624 | bytes 29329408 | tf_op jit(solution)/shard_map/bsd,bsc->dc/dot_general | solution.py:1332
  632.3 1.9 add_bitcast_fusion
  634.1 1.0 split.30
  635.1 1.0 fusion.37
  636.2 2.0 collective-permute-start.4
  638.2 87.6 %latents_backward.1 = (bf16[4,512,1152]{2,1,0:T(8,128)(2,1)}, f32[2,2,1152]{2,1,0:T(2,128)}, f32[72,3840]{1,0:T(8,128)}, bf16[6,8,72,640]{3,2,1,0:T(8,128)(2,1)}...) custom-call(bf16[2048,3840]{1,0:T(8,128)(2,1)} %bitcast.133, bf16[1152,3840]{1,0:T(8,128)(2,1)} %bitcast.125, ...), custom_call_target="tpu_custom_call" | custom-call | tf_op jit(solution)/shard_map/latents_backward/pallas_call | solution.py:1283
  725.8 1.1 split.38
  726.9 1.2 collective-permute-start.3
  728.1 0.7 convert.28
  729.4 29.8 %closing.1 = (f32[36,128]{1,0:T(8,128)S(1)}, f32[2,16,8,128]{3,2,1,0:T(8,128)S(1)}, f32[6,72,576]{2,1,0:T(8,128)S(1)}, f32[6,1,576]{2,1,0:T(1,128)S(1)}) custom-call(f32[2,8,1728]{2,1,0:T(8,128)S(1)} %pad_maximum_fusion.6.mod_ref, f32[2,36,128]{2,1,0:T(8,128)S(1)} %pad_maximum_fusion.7.bias_ref, bf16[2,128,1728]{2,1,0:T(8,128)(2,1)S(1)} %pad_bitcast_fusion.mod_w_ref, ...), custom_call_target="tpu_custom_call" | custom-call | tf_op jit(solution)/shard_map/closing/pallas_call | solution.py:988
  760.6 0.7 reshape.219
  762.5 5.1 bitcast_select_fusion
  767.7 0.7 add_bitcast_fusion.1
  768.4 1.0 convert_add_fusion.3
  769.6 0.8 copy.94
  770.5 1.9 convert_add_fusion.2
  772.3 4.9 copy.141
  777.2 1.0 copy.142
  (207 shorter events, 11.6 us)
Async XLA Ops:
  7.2 211.2 %all-gather.3.cloned.1.call-start = ((), (), s32[]{:S(2)}) async-start(), calls=%async_computation.2 | async-start | bytes 14413824 | tf_op jit(solution)/shard_map/all_gather | solution.py:1413
  9.9 7.1 copy-start.18
  13.5 3.6 copy-start.14
  17.1 2.3 copy-start.2
  19.4 0.8 copy-start.4
  98.1 3.4 copy-start.3
  101.5 0.6 copy-start.5
  102.2 0.6 copy-start.6
  102.8 0.6 copy-start.8
  103.4 115.0 %copy-start = (bf16[2,512,1152]{2,1,0:T(8,128)(2,1)}, bf16[2,512,1152]{2,1,0:T(8,128)(2,1)S(1)}, u32[]{:S(2)}) copy-start(bf16[2,512,1152]{2,1,0:T(8,128)(2,1)S(1)} %get-tuple-element.48) | copy-start | bytes 7077892
  105.8 201.9 %all-gather.5.cloned.1.call-start = ((), (), s32[]{:S(2)}) async-start(), calls=%async_computation.3 | async-start | bytes 11280384 | tf_op jit(solution)/shard_map/all_gather | solution.py:1428
  108.7 9.9 %slice-start = ((s8[8847360]{0:T(1024)(128)(4,1)}), s8[4194304]{0:T(1024)(128)(4,1)S(1)}, s32[]{:S(2)}) async-start(s8[8847360]{0:T(1024)(128)(4,1)} %bitcast.126), calls=%async_computation.6 | async-start | bytes 8388608
  108.7 9.9 %slice-start.1 = ((s8[8847360]{0:T(1024)(128)(4,1)}), s8[4194304]{0:T(1024)(128)(4,1)S(1)}, s32[]{:S(2)}) async-start(s8[8847360]{0:T(1024)(128)(4,1)} %bitcast.126), calls=%async_computation.7 | async-start | bytes 8388608
  115.5 3.1 copy-start.11
  115.5 3.1 slice-start.2
  116.2 29.0 %copy-start.29 = (f32[2,1024]{1,0:T(2,128)}, f32[2,1024]{1,0:T(2,128)S(1)}, u32[]{:S(2)}) copy-start(f32[2,1024]{1,0:T(2,128)S(1)} %broadcast_multiply_fusion.3) | copy-start | bytes 24580
  117.8 27.4 %copy-start.38 = (f32[2,1024]{1,0:T(2,128)}, f32[2,1024]{1,0:T(2,128)S(1)}, u32[]{:S(2)}) copy-start(f32[2,1024]{1,0:T(2,128)S(1)} %add_rsqrt_fusion.1) | copy-start | bytes 24580
  118.6 38.6 %copy-start.20 = (f32[2,1,1152]{2,1,0:T(1,128)}, f32[2,1,1152]{2,1,0:T(1,128)S(1)}, u32[]{:S(2)}) copy-start(f32[2,1,1152]{2,1,0:T(1,128)S(1)} %get-tuple-element.157) | copy-start | bytes 27652
  118.6 39.3 %copy-start.22 = (f32[2,1,1152]{2,1,0:T(1,128)}, f32[2,1,1152]{2,1,0:T(1,128)S(1)}, u32[]{:S(2)}) copy-start(f32[2,1,1152]{2,1,0:T(1,128)S(1)} %get-tuple-element.159) | copy-start | bytes 27652
  118.6 26.6 %copy-start.33 = (f32[2,1152]{1,0:T(2,128)}, f32[2,1152]{1,0:T(2,128)S(1)}, u32[]{:S(2)}) copy-start(f32[2,1152]{1,0:T(2,128)S(1)} %get-tuple-element.173) | copy-start | bytes 27652
  118.6 26.6 %copy-start.35 = (f32[2,1152]{1,0:T(2,128)}, f32[2,1152]{1,0:T(2,128)S(1)}, u32[]{:S(2)}) copy-start(f32[2,1152]{1,0:T(2,128)S(1)} %get-tuple-element.174) | copy-start | bytes 27652
  118.6 26.6 %copy-start.17 = (bf16[2304,72]{0,1:T(8,128)(2,1)S(1)}, bf16[2304,72]{0,1:T(8,128)(2,1)}, u32[]{:S(2)}) copy-start(bf16[2304,72]{0,1:T(8,128)(2,1)} %param.23) | copy-start | bytes 995332
  118.7 37.7 %copy-start.32 = (bf16[2,576]{1,0:T(2,128)(2,1)S(1)}, bf16[2,576]{1,0:T(2,128)(2,1)}, u32[]{:S(2)}) copy-start(bf16[2,576]{1,0:T(2,128)(2,1)} %param.20) | copy-start | bytes 6916
  118.7 37.8 %copy-start.9 = (f32[36,128]{1,0:T(8,128)S(1)}, f32[36,128]{1,0:T(8,128)}, u32[]{:S(2)}) copy-start(f32[36,128]{1,0:T(8,128)} %copy-done.8) | copy-start | bytes 55300
  118.7 37.8 %copy-start.19 = (f32[2304]{0:T(1024)S(1)}, f32[2304]{0:T(1024)}, u32[]{:S(2)}) copy-start(f32[2304]{0:T(1024)} %copy-done.18) | copy-start | bytes 27652
  145.2 9.4 %collective-permute-start.1 = (bf16[72,2304]{1,0:T(8,128)(2,1)S(1)}, bf16[72,2304]{1,0:T(8,128)(2,1)S(1)}, u32[]{:S(2)}, u32[]{:S(2)}) collective-permute-start(bf16[72,2304]{1,0:T(8,128)(2,1)S(1)} %bitcast.143), channel_id=1, source_target_pairs={{0,1},{1,0},{2,3},{3,2},{4,5},{5,4},{6,7},{7,6},{8,9},{9,8},{10,11... | collective-permute-start | bytes 995336 | tf_op jit(solution)/shard_map/ppermute | solution.py:1359
  155.5 296.1 %reduce-scatter.3.cloned.1.call-start = ((), (), s32[]{:S(2)}) async-start(), calls=%async_computation.4 | async-start | bytes 11280384 | tf_op jit(solution)/shard_map/reduce_scatter | solution.py:1442
  156.0 57.6 %collective-permute-start = (bf16[2,512,1152]{2,1,0:T(8,128)(2,1)}, bf16[2,512,1152]{2,1,0:T(8,128)(2,1)}, u32[]{:S(2)}, u32[]{:S(2)}) collective-permute-start(bf16[2,512,1152]{2,1,0:T(8,128)(2,1)} %get-tuple-element.55), channel_id=1, source_target_pairs={{0,1},{1,0},{2,3},{3,2},{4,5},{5,4},{6,7},{7,6},{8,9},{9,8},{10,11... | collective-permute-start | bytes 7077896 | tf_op jit(solution)/shard_map/ppermute | solution.py:1359
  157.2 56.5 %copy-start.24 = (f32[2,1,1152]{2,0,1:T(2,128)}, f32[2,1,1152]{2,0,1:T(2,128)S(1)}, u32[]{:S(2)}) copy-start(f32[2,1,1152]{2,0,1:T(2,128)S(1)} %copy.128) | copy-start | bytes 27652
  157.9 60.5 %copy-start.26 = (f32[2,1152]{1,0:T(2,128)}, f32[2,1152]{1,0:T(2,128)S(1)}, u32[]{:S(2)}) copy-start(f32[2,1152]{1,0:T(2,128)S(1)} %get-tuple-element.172) | copy-start | bytes 27652
  157.9 55.7 %copy-start.12 = (bf16[2,512,1152]{2,1,0:T(8,128)(2,1)S(1)}, bf16[2,512,1152]{2,1,0:T(8,128)(2,1)}, u32[]{:S(2)}) copy-start(bf16[2,512,1152]{2,1,0:T(8,128)(2,1)} %get-tuple-element.145) | copy-start | bytes 7077892
  231.2 5.1 copy-start.10
  232.3 47.5 %slice-start.3 = ((s8[4718592]{0:T(1024)(128)(4,1)}), s8[524288]{0:T(1024)(128)(4,1)S(1)}, s32[]{:S(2)}) async-start(s8[4718592]{0:T(1024)(128)(4,1)} %bitcast.136), calls=%async_computation.9 | async-start | bytes 1048576
  236.3 43.5 %slice-start.4 = ((s8[4718592]{0:T(1024)(128)(4,1)}), s8[4194304]{0:T(1024)(128)(4,1)S(1)}, s32[]{:S(2)}) async-start(s8[4718592]{0:T(1024)(128)(4,1)} %bitcast.136), calls=%async_computation.10 | async-start | bytes 8388608
  307.6 35.5 %slice-start.5 = ((s8[4718592]{0:T(1024)(128)(4,1)}), s8[524288]{0:T(1024)(128)(4,1)S(1)}, s32[]{:S(2)}) async-start(s8[4718592]{0:T(1024)(128)(4,1)} %bitcast.139), calls=%async_computation.11 | async-start | bytes 1048576
  307.7 326.5 %reduce-scatter.5.cloned.1.call-start = ((), (), s32[]{:S(2)}) async-start(), calls=%async_computation.5 | async-start | bytes 14413824 | tf_op jit(solution)/shard_map/reduce_scatter | solution.py:1464
  307.7 35.4 %slice-start.6 = ((s8[4718592]{0:T(1024)(128)(4,1)}), s8[4194304]{0:T(1024)(128)(4,1)S(1)}, s32[]{:S(2)}) async-start(s8[4718592]{0:T(1024)(128)(4,1)} %bitcast.139), calls=%async_computation.12 | async-start | bytes 8388608
  370.5 34.8 %copy-start.13 = (bf16[2,512,1152]{2,1,0:T(8,128)(2,1)S(1)}, bf16[2,512,1152]{2,1,0:T(8,128)(2,1)}, u32[]{:S(2)}) copy-start(bf16[2,512,1152]{2,1,0:T(8,128)(2,1)} %get-tuple-element.145) | copy-start | bytes 7077892
  370.5 34.8 %copy-start.25 = (f32[2,1,1152]{2,0,1:T(2,128)S(1)}, f32[2,1,1152]{2,0,1:T(2,128)}, u32[]{:S(2)}) copy-start(f32[2,1,1152]{2,0,1:T(2,128)} %copy-done.24) | copy-start | bytes 27652
  370.5 34.9 %copy-start.37 = (f32[1152]{0:T(1024)S(1)}, f32[1152]{0:T(1024)}, u32[]{:S(2)}) copy-start(f32[1152]{0:T(1024)} %get-tuple-element.130) | copy-start | bytes 13828
  405.3 39.6 %copy-start.27 = (f32[2,1152]{1,0:T(2,128)S(1)}, f32[2,1152]{1,0:T(2,128)}, u32[]{:S(2)}) copy-start(f32[2,1152]{1,0:T(2,128)} %copy-done.26) | copy-start | bytes 27652
  484.9 1.7 copy-start.1
  486.5 10.6 %copy-start.23 = (f32[2,1,1152]{2,1,0:T(1,128)S(1)}, f32[2,1,1152]{2,1,0:T(1,128)}, u32[]{:S(2)}) copy-start(f32[2,1,1152]{2,1,0:T(1,128)} %copy-done.22) | copy-start | bytes 27652
  486.5 10.7 %copy-start.21 = (f32[2,1,1152]{2,1,0:T(1,128)S(1)}, f32[2,1,1152]{2,1,0:T(1,128)}, u32[]{:S(2)}) copy-start(f32[2,1,1152]{2,1,0:T(1,128)} %copy-done.20) | copy-start | bytes 27652
  486.5 11.0 %copy-start.31 = (f32[1,4608]{1,0:T(1,128)S(1)}, f32[1,4608]{1,0:T(1,128)}, u32[]{:S(2)}) copy-start(f32[1,4608]{1,0:T(1,128)} %get-tuple-element.75) | copy-start | bytes 55300
  497.1 137.0 %collective-permute-start.2 = (bf16[2,512,1152]{2,1,0:T(8,128)(2,1)}, bf16[2,512,1152]{2,1,0:T(8,128)(2,1)}, u32[]{:S(2)}, u32[]{:S(2)}) collective-permute-start(bf16[2,512,1152]{2,1,0:T(8,128)(2,1)} %get-tuple-element.144), channel_id=1, source_target_pairs={{0,1},{1,0},{2,3},{3,2},{4,5},{5,4},{6,7},{7,6},{8,9},{9,8},{10,11... | collective-permute-start | bytes 7077896 | tf_op jit(solution)/shard_map/ppermute | solution.py:1359
  499.4 132.9 %collective-permute-start.6 = (bf16[72,2304]{1,0:T(8,128)(2,1)}, bf16[72,2304]{1,0:T(8,128)(2,1)}, u32[]{:S(2)}, u32[]{:S(2)}) collective-permute-start(bf16[72,2304]{1,0:T(8,128)(2,1)} %split.32), channel_id=1, source_target_pairs={{0,1},{1,0},{2,3},{3,2},{4,5},{5,4},{6,7},{7,6},{8,9},{9,8},{10,11... | collective-permute-start | bytes 995336 | tf_op jit(solution)/shard_map/ppermute | solution.py:1359
  501.4 104.9 %copy-start.30 = (f32[2,1024]{1,0:T(2,128)S(1)}, f32[2,1024]{1,0:T(2,128)}, u32[]{:S(2)}) copy-start(f32[2,1024]{1,0:T(2,128)} %copy-done.29) | copy-start | bytes 24580
  501.4 104.9 %copy-start.34 = (f32[2,1152]{1,0:T(2,128)S(1)}, f32[2,1152]{1,0:T(2,128)}, u32[]{:S(2)}) copy-start(f32[2,1152]{1,0:T(2,128)} %copy-done.33) | copy-start | bytes 27652
  501.4 104.9 %copy-start.36 = (f32[2,1152]{1,0:T(2,128)S(1)}, f32[2,1152]{1,0:T(2,128)}, u32[]{:S(2)}) copy-start(f32[2,1152]{1,0:T(2,128)} %copy-done.35) | copy-start | bytes 27652
  501.4 104.9 %copy-start.39 = (f32[2,1024]{1,0:T(2,128)S(1)}, f32[2,1024]{1,0:T(2,128)}, u32[]{:S(2)}) copy-start(f32[2,1024]{1,0:T(2,128)} %copy-done.38) | copy-start | bytes 24580
  606.3 25.9 %copy-start.15 = (bf16[72,4608]{1,0:T(8,128)(2,1)S(1)}, bf16[72,4608]{1,0:T(8,128)(2,1)}, u32[]{:S(2)}) copy-start(bf16[72,4608]{1,0:T(8,128)(2,1)} %reduce-scatter.3.cloned.1.call-done) | copy-start | bytes 1990660
  636.1 134.4 %collective-permute-start.5 = (bf16[72,2304]{1,0:T(8,128)(2,1)S(1)}, bf16[72,2304]{1,0:T(8,128)(2,1)S(1)}, u32[]{:S(2)}, u32[]{:S(2)}) collective-permute-start(bf16[72,2304]{1,0:T(8,128)(2,1)S(1)} %split.30), channel_id=1, source_target_pairs={{0,1},{1,0},{2,3},{3,2},{4,5},{5,4},{6,7},{7,6},{8,9},{9,8},{10,11... | collective-permute-start | bytes 995336 | tf_op jit(solution)/shard_map/ppermute | solution.py:1359
  636.2 131.5 %collective-permute-start.4 = (bf16[72,640]{1,0:T(8,128)(2,1)S(1)}, bf16[72,640]{1,0:T(8,128)(2,1)S(1)}, u32[]{:S(2)}, u32[]{:S(2)}) collective-permute-start(bf16[72,640]{1,0:T(8,128)(2,1)S(1)} %get-tuple-element.148), channel_id=1, source_target_pairs={{0,1},{1,0},{2,3},{3,2},{4,5},{5,4},{6,7},{7,6},{8,9},{9,8},{10,11... | collective-permute-start | bytes 276488 | tf_op jit(solution)/shard_map/ppermute | solution.py:1359
  638.2 91.2 %copy-start.7 = (f32[16,8,128]{2,1,0:T(8,128)S(1)}, f32[16,8,128]{2,1,0:T(8,128)}, u32[]{:S(2)}) copy-start(f32[16,8,128]{2,1,0:T(8,128)} %copy-done.6) | copy-start | bytes 196612
  638.2 121.1 %copy-start.28 = (bf16[4,1152]{1,0:T(4,128)(2,1)S(1)}, bf16[4,1152]{1,0:T(4,128)(2,1)}, u32[]{:S(2)}) copy-start(bf16[4,1152]{1,0:T(4,128)(2,1)} %param.13) | copy-start | bytes 27652
  726.9 41.4 %collective-permute-start.3 = (bf16[72,1920]{1,0:T(8,128)(2,1)S(1)}, bf16[72,1920]{1,0:T(8,128)(2,1)}, u32[]{:S(2)}, u32[]{:S(2)}) collective-permute-start(bf16[72,1920]{1,0:T(8,128)(2,1)S(1)} %split.38), channel_id=1, source_target_pairs={{0,1},{1,0},{2,3},{3,2},{4,5},{5,4},{6,7},{7,6},{8,9},{9,8},{10,11... | collective-permute-start | bytes 829448 | tf_op jit(solution)/shard_map/ppermute | solution.py:1359
  761.9 6.5 copy-start.16
Sparse Core Ops, SparseCore 0:
  105.9 103.6 all-gather.2
  212.5 86.8 all-gather.4
  307.8 117.8 reduce-scatter.2
  485.0 140.1 reduce-scatter.4

commit v6 on v5

--- a/solution.py
+++ b/solution.py
@@ -1456,9 +1456,9 @@
     gate_a_grad = jnp.sum(first_grad * attn_out, axis=1)
     attn_bias_grad = jnp.sum(gate_a[:, 0] * jnp.sum(first_grad, axis=1), axis=0)
     attn_grad = (gate_a * first_grad).astype(bf16)
-    attn_grad, down_sum = lax.optimization_barrier((attn_grad, down_sum))
     mixed_grad = mm("bsd,dc->bsc", attn_grad, mix_t).astype(bf16)
     mix_grad = mm("bsd,bsc->dc", attn_grad, mixed).astype(bf16)
+    mix_grad, down_sum = lax.optimization_barrier((mix_grad, down_sum))
     up_grad = jnp.concatenate([up_grad, mix_grad], axis=1)
     up_grad, mixed_grad = lax.optimization_barrier((up_grad, mixed_grad))
     up_sum = lax.psum_scatter(up_grad, "dp", scatter_dimension=0, tiled=True)

time: 792 us -> 793 us (level)
    pallas_call x1, Pallas kernels: 55.7 us -> 46.5 us  [attn_fwd(): pl.pallas_call(partial(attn_fwd_kernel, blk=blk, heads=heads), grid=(n, 2...]
    unnamed x111 -> x113, local copies, waits for them, and re-layouts: 20 us -> 20.1 us
  transfers between devices with their start and end apart: 11 -> 11, of which waited for: 1 -> 2; matrix products, arithmetic and copies ran while one was open for 32% -> 35% of each run, Pallas kernels for 45% -> 45%
where the time goes in v6:
time: 793 us; the launch traced here: 780 us
  Pallas kernels  431 us (54%)
  matrix products  217 us (27%)
  local copies, waits for them, and re-layouts  49.1 us (6%)
  other arithmetic  48.6 us (6%)
  between operations  15 us (2%)
  waiting for transfers between devices  13.1 us (2%)
    dot_general x9, matrix products, mm(): return jnp.einsum(spec, a, b, preferred_element_type=f32)  217 us
    pallas_call x1, Pallas kernels, attn_bwd(): pl.pallas_call(partial(attn_bwd_kernel, blk=blk, heads=heads), grid=(n, 2...  104 us
    pallas_call x1, Pallas kernels, latents_backward(): pl.pallas_call(latents_backward_kernel, grid=(max(pieces + 5, 2 * sent),)...  92.7 us
    pallas_call x1, Pallas kernels, opening(): pl.pallas_call(opening_kernel, in_specs=[vmem, vmem, vmem, vmem, anywhere...  77.9 us
    pallas_call x1, Pallas kernels, attn_fwd(): pl.pallas_call(partial(attn_fwd_kernel, blk=blk, heads=heads), grid=(n, 2...  46.5 us
    pallas_call x1, Pallas kernels, up_forward(): pl.pallas_call(up_forward_kernel, grid=(hidden // cols, count * seq // ro...  43.9 us
    pallas_call x1, Pallas kernels, down_backward(): pl.pallas_call(down_backward_kernel, grid=(hidden // cols, count * seq //...  36.5 us
    pallas_call x1, Pallas kernels, closing(): pl.pallas_call(closing_kernel, in_specs=[vmem] * 4, out_specs=[vmem] * 4,...  29.9 us
  transfers between devices with their start and end apart: 11, of which 2 were waited for; matrix products, arithmetic and copies ran while one was open for 35% of the time, Pallas kernels for 45%

profile of v6, /device:TPU:0, one launch (start us, length us, event | category | flops | bytes accessed | tf_op | source)
XLA Modules:
  0.0 779.6 jit_solution(3002409768809271426)
XLA Ops:
  7.2 1.1 copy.74
  8.4 0.7 reshape.191
  9.2 0.7 convert_element_type.100
  9.9 0.8 reshape.195
  10.7 0.8 reshape.196
  11.5 1.1 copy.107
  12.6 0.9 pad.30
  13.7 0.8 reshape.222
  15.1 0.7 fusion.24
  16.0 1.0 pad_maximum_fusion.5.rest_ref
  17.1 2.3 copy-done.2
  19.4 0.8 copy-done.4
  20.2 77.9 %opening.1 = (bf16[16,72,3840]{2,1,0:T(8,128)(2,1)S(1)}, bf16[72,2944]{1,0:T(8,128)(2,1)S(1)}, bf16[2,512,1152]{2,1,0:T(8,128)(2,1)S(1)}, f32[2,8,1728]{2,1,0:T(...) custom-call(f32[16,8,128]{2,1,0:T(8,128)S(1)} %fusion.20.cond_ref, ...), custom_call_target="tpu_custom_call" | custom-call | tf_op jit(solution)/shard_map/opening/pallas_call | solution.py:896
  98.1 3.5 copy-done.3
  103.6 2.3 pad_maximum_fusion.3
  106.0 0.7 convert_element_type.98
  106.7 1.0 reshape.199
  107.8 0.8 fusion.41
  108.8 6.8 constant_dynamic-slice_fusion.2
  115.6 0.7 convert_reduce_fusion.1
  116.4 1.6 fusion.7
  118.8 26.5 %add_convert_fusion.q_ref.k_ref.v_ref = bf16[2,1024,3840]{2,1,0:T(8,128)(2,1)} fusion(f32[3840]{0:T(1024)S(1)} %constant_dynamic-update-slice_fusion, bf16[1152,3840,1]{1,0,2:T(8,128)(2,1)S(1)} %bitcast.126, f32[2,1152]{1,0:T(2,128)S(1)} %get-tuple-element.173, f32[2,1152]{1,0:T(2,128)S(1)} %get-tuple-element.174, f32[2,1024]{1,0:T(2,128)S(1)} %add_rsqrt_fusion.1, ...), kind=kOutput, calls=%fused_computation | convolution fusion | flops 18156355584 | bytes 29344768 | tf_op jit(solution)/shard_map/bsd,dc->bsc/dot_general | solution.py:1332
  145.7 9.0 %collective-permute-done.1 = bf16[72,2304]{1,0:T(8,128)(2,1)S(1)} collective-permute-done((bf16[72,2304]{1,0:T(8,128)(2,1)S(1)}, bf16[72,2304]{1,0:T(8,128)(2,1)S(1)}, u32[]{:S(2)}, u32[]{:S(2)}) %collective-permute-start.1) | collective-permute-done | bytes 331808 | tf_op jit(solution)/shard_map/ppermute | solution.py:1359
  154.7 0.9 pad_maximum_fusion.4
  157.8 46.5 %attention_forward.1 = (bf16[2,1024,1280]{2,1,0:T(8,128)(2,1)}, f32[2,2,8,1024]{3,2,1,0:T(8,128)}) custom-call(bf16[2,1024,3840]{2,1,0:T(8,128)(2,1)} %add_convert_fusion.q_ref.k_ref.v_ref, bf16[2,1024,3840]{2,1,0:T(8,128)(2,1)} %add_convert_fusion.q_ref.k_ref.v_ref, bf16[2,1024,3840]{2,1,0:T(8,128)(2,1)} %add_convert_fusion.q_ref.k_ref.v_ref), custom_call_target="tpu_custom_call" | custom-call | flops 10737418240 | bytes 20971520 | tf_op jit(solution)/shard_map/attention_forward/pallas_call | solution.py:402
  204.2 4.0 collective-permute-done
  208.2 4.7 fusion.11
  213.0 12.6 %fusion.35 = (f32[2,1024]{1,0:T(2,128)S(1)}, f32[2,1024,1152]{2,1,0:T(8,128)S(1)}, f32[2,1024,1152]{2,1,0:T(8,128)}) fusion(f32[1152]{0:T(1024)S(1)} %get-tuple-element.131, f32[2,1152]{1,0:T(2,128)S(1)} %get-tuple-element.172, bf16[2,512,1152]{2,1,0:T(8,128)(2,1)S(1)} %get-tuple-element.48, bf16[2,512,1152]{2,1,0:T(8,128)(2,1)} %copy-done.11, ...), kind=kOutput, calls=%fused_computation.135 | convolution fusion | flops 6058670080 | bytes 31806976 | tf_op jit(solution)/shard_map/bsc,dc->bsd/dot_general | solution.py:1332
  225.6 1.1 multiply_reduce_fusion.3
  226.8 3.7 add_convert_fusion.2
  230.7 43.9 %up_forward.1 = (bf16[2048,4608]{1,0:T(8,128)(2,1)}, bf16[2048,4608]{1,0:T(8,128)(2,1)}) custom-call(bf16[2048,1152]{1,0:T(8,128)(2,1)} %bitcast.136, bf16[1152,5888]{1,0:T(8,128)(2,1)} %all-gather.3.cloned.1.call-done.w_ref, f32[1,4608]{1,0:T(1,128)} %reshape.204.b_ref), custom_call_target="tpu_custom_call" | custom-call | flops 21743271936 | bytes 37748736 | tf_op jit(solution)/shard_map/up_forward/pallas_call | solution.py:551
  274.6 27.3 %fusion = bf16[1152,4608]{1,0:T(8,128)(2,1)} fusion(bf16[2,1024,1152]{2,1,0:T(8,128)(2,1)S(1)} %bitcast.135, bf16[2,1024,4608]{2,1,0:T(8,128)(2,1)} %bitcast.159), kind=kOutput, calls=%fused_computation.3 | convolution fusion | flops 21748580352 | bytes 34209792 | tf_op jit(solution)/shard_map/bsd,bsf->df/dot_general | solution.py:1332
  302.0 36.5 %down_backward.1 = (bf16[2048,4608]{1,0:T(8,128)(2,1)}, f32[1,4608]{1,0:T(1,128)}) custom-call(bf16[2048,1152]{1,0:T(8,128)(2,1)} %bitcast.133, bf16[1152,4608]{1,0:T(8,128)(2,1)} %all-gather.5.cloned.1.call-done.w_ref, bf16[2048,4608]{1,0:T(8,128)(2,1)} %get-tuple-element.60.slope_ref), custom_call_target="tpu_custom_call" | custom-call | flops 21743271936 | bytes 37748736 | tf_op jit(solution)/shard_map/down_backward/pallas_call | solution.py:594
  338.5 27.6 %fusion.1 = bf16[1152,4608]{1,0:T(8,128)(2,1)} fusion(bf16[2,1024,1152]{2,1,0:T(8,128)(2,1)S(1)} %bitcast.138, bf16[2,1024,4608]{2,1,0:T(8,128)(2,1)} %bitcast.161), kind=kOutput, calls=%fused_computation.4 | convolution fusion | flops 21748580352 | bytes 34209792 | tf_op jit(solution)/shard_map/bsd,bsf->df/dot_general | solution.py:1332
  366.1 34.4 %multiply_reduce_fusion = (bf16[2,1152]{1,0:T(2,128)(2,1)S(1)}, f32[2,1024]{1,0:T(2,128)S(1)}, f32[2,1024]{1,0:T(2,128)S(1)}, bf16[2,1152]{1,0:T(2,128)(2,1)S(1)}, f32[2,1024,1152]{2,1,0:T(8,128)}) fusion(f32[2,1024,1152]{2,1,0:T(8,128)} %copy-done.10, f32[2,1024]{1,0:T(2,128)S(1)} %add_rsqrt_fusion, f32[2,1024]{1,0:T(2,128)S(1)} %broadcast_multiply_fusion.2, ...), kind=kOutput, calls=%fused_computation.26 | convolution fusion | flops 21764497408 | bytes 48416768 | tf_op jit(solution)/shard_map/bsf,df->bsd/dot_general | solution.py:1332
  400.6 39.4 %convert_reduce_fusion = (f32[2,1152]{1,0:T(2,128)S(1)}, bf16[2,1152]{1,0:T(2,128)(2,1)S(1)}, bf16[2,1024,1152]{2,1,0:T(8,128)(2,1)}, bf16[2,1152]{1,0:T(2,128)(...) fusion(bf16[2,512,1152]{2,1,0:T(8,128)(2,1)} %collective-permute-done, ...), kind=kOutput, calls=%fused_computation.6 | convolution fusion | flops 21797527552 | bytes 76765184 | tf_op jit(solution)/shard_map/bsf,df->bsd/dot_general | solution.py:1332
  440.1 12.1 %convolution_convert_fusion.do_ref = bf16[2,1024,1280]{2,1,0:T(8,128)(2,1)} fusion(bf16[1152,5888]{1,0:T(8,128)(2,1)} %all-gather.3.cloned.1.call-done.w_ref, f32[2,1024,1152]{2,1,0:T(8,128)} %get-tuple-element.142, f32[2,1152]{1,0:T(2,128)S(1)} %copy-done.37), kind=kOutput, calls=%fused_computation.37 | convolution fusion | flops 6047137792 | bytes 17638400 | tf_op jit(solution)/shard_map/bsd,dc->bsc/dot_general | solution.py:1332
  452.1 10.7 %fusion.13 = bf16[1152,1280]{1,0:T(8,128)(2,1)} fusion(bf16[2,1024,1280]{2,1,0:T(8,128)(2,1)} %get-tuple-element.53.o_ref, f32[2,1024,1152]{2,1,0:T(8,128)S(1)} %copy-done.14, f32[2,1152]{1,0:T(2,128)S(1)} %copy-done.37), kind=kOutput, calls=%fused_computation.36 | convolution fusion | flops 6045990912 | bytes 17638400 | tf_op jit(solution)/shard_map/bsd,bsc->dc/dot_general | solution.py:1332
  462.8 12.3 %pad_maximum_fusion = bf16[1152,5888]{1,0:T(8,128)(2,1)} fusion(bf16[1152,1280]{1,0:T(8,128)(2,1)} %fusion.13, bf16[1152,4608]{1,0:T(8,128)(2,1)} %fusion.1), kind=kLoop, calls=%fused_computation.13 | loop fusion | flops 27131904 | bytes 27131904 | tf_op jit(solution)/shard_map/concatenate | solution.py:1462
  475.3 1.5 copy-done.1
  476.8 4.2 pad_maximum_fusion.1
  481.1 5.6 fusion.36
  486.7 1.5 collective-permute-start.2
  488.7 1.8 split.32
  491.0 103.9 %attention_backward.1 = (bf16[2,1024,3840]{2,1,0:T(8,128)(2,1)}, f32[2,2,1,1920]{3,2,1,0:T(1,128)}) custom-call(bf16[2,1024,3840]{2,1,0:T(8,128)(2,1)} %add_convert_fusion.q_ref.k_ref.v_ref, bf16[2,1024,3840]{2,1,0:T(8,128)(2,1)} %add_convert_fusion.q_ref.k_ref.v_ref, bf16[2,1024,3840]{2,1,0:T(8,128)(2,1)} %add_convert_fusion.q_ref.k_ref.v_ref, ...), custom_call_target="tpu_custom_call" | custom-call | tf_op jit(solution)/shard_map/attention_backward/pallas_call | solution.py:491
  594.8 0.8 reduce_sum.161
  595.9 25.9 %bitcast_convert_fusion = bf16[1152,3840]{1,0:T(8,128)(2,1)} fusion(bf16[2,1024,3840]{2,1,0:T(8,128)(2,1)} %get-tuple-element.68, f32[2,1152]{1,0:T(2,128)S(1)} %copy-done.33, f32[2,1152]{1,0:T(2,128)S(1)} %copy-done.35, f32[2,1024]{1,0:T(2,128)S(1)} %copy-done.40, f32[2,1024]{1,0:T(2,128)S(1)} %copy-done.29, bf16[2,512,1152]{2,1,0:T(8,128)(2,1)S(1)} %copy-done.1, ...), kind=kOutput, calls=%fused_computation.5 | convolution fusion | flops 18145050624 | bytes 29329408 | tf_op jit(solution)/shard_map/bsd,bsc->dc/dot_general | solution.py:1332
  621.8 1.9 add_bitcast_fusion
  623.7 1.0 split.30
  624.7 1.0 fusion.37
  625.7 1.5 collective-permute-start.5
  627.8 92.7 %latents_backward.1 = (bf16[4,512,1152]{2,1,0:T(8,128)(2,1)}, f32[2,2,1152]{2,1,0:T(2,128)}, f32[72,3840]{1,0:T(8,128)}, bf16[6,8,72,640]{3,2,1,0:T(8,128)(2,1)}...) custom-call(bf16[2048,3840]{1,0:T(8,128)(2,1)} %bitcast.130, bf16[1152,3840]{1,0:T(8,128)(2,1)} %bitcast.123, ...), custom_call_target="tpu_custom_call" | custom-call | tf_op jit(solution)/shard_map/latents_backward/pallas_call | solution.py:1283
  720.5 1.1 split.38
  721.6 0.9 collective-permute-start.3
  722.5 0.7 convert.28
  723.8 29.9 %closing.1 = (f32[36,128]{1,0:T(8,128)S(1)}, f32[2,16,8,128]{3,2,1,0:T(8,128)S(1)}, f32[6,72,576]{2,1,0:T(8,128)S(1)}, f32[6,1,576]{2,1,0:T(1,128)S(1)}) custom-call(f32[2,8,1728]{2,1,0:T(8,128)S(1)} %pad_maximum_fusion.6.mod_ref, f32[2,36,128]{2,1,0:T(8,128)S(1)} %pad_maximum_fusion.7.bias_ref, bf16[2,128,1728]{2,1,0:T(8,128)(2,1)S(1)} %pad_bitcast_fusion.mod_w_ref, ...), custom_call_target="tpu_custom_call" | custom-call | tf_op jit(solution)/shard_map/closing/pallas_call | solution.py:988
  755.2 0.7 reshape.219
  757.1 5.1 bitcast_select_fusion
  762.3 0.7 add_bitcast_fusion.1
  763.0 1.0 convert_add_fusion.3
  764.2 0.8 copy.94
  765.1 1.9 convert_add_fusion.2
  766.9 4.9 copy.141
  771.8 1.0 copy.142
  (208 shorter events, 12.3 us)
Async XLA Ops:
  7.2 205.8 %all-gather.3.cloned.1.call-start = ((), (), s32[]{:S(2)}) async-start(), calls=%async_computation.2 | async-start | bytes 14413824 | tf_op jit(solution)/shard_map/all_gather | solution.py:1413
  9.9 7.1 copy-start.19
  13.5 3.6 copy-start.15
  17.1 2.3 copy-start.2
  19.4 0.8 copy-start.4
  98.1 3.5 copy-start.3
  101.6 0.6 copy-start.5
  102.3 0.6 copy-start.6
  102.9 0.6 copy-start.8
  103.5 109.5 %copy-start = (bf16[2,512,1152]{2,1,0:T(8,128)(2,1)}, bf16[2,512,1152]{2,1,0:T(8,128)(2,1)S(1)}, u32[]{:S(2)}) copy-start(bf16[2,512,1152]{2,1,0:T(8,128)(2,1)S(1)} %get-tuple-element.48) | copy-start | bytes 7077892
  105.9 196.0 %all-gather.5.cloned.1.call-start = ((), (), s32[]{:S(2)}) async-start(), calls=%async_computation.3 | async-start | bytes 11280384 | tf_op jit(solution)/shard_map/all_gather | solution.py:1428
  108.8 9.9 %slice-start = ((s8[8847360]{0:T(1024)(128)(4,1)}), s8[4194304]{0:T(1024)(128)(4,1)S(1)}, s32[]{:S(2)}) async-start(s8[8847360]{0:T(1024)(128)(4,1)} %bitcast.124), calls=%async_computation.6 | async-start | bytes 8388608
  108.8 9.9 %slice-start.1 = ((s8[8847360]{0:T(1024)(128)(4,1)}), s8[4194304]{0:T(1024)(128)(4,1)S(1)}, s32[]{:S(2)}) async-start(s8[8847360]{0:T(1024)(128)(4,1)} %bitcast.124), calls=%async_computation.7 | async-start | bytes 8388608
  115.6 3.1 copy-start.11
  115.6 3.1 slice-start.2
  116.3 29.0 %copy-start.28 = (f32[2,1024]{1,0:T(2,128)}, f32[2,1024]{1,0:T(2,128)S(1)}, u32[]{:S(2)}) copy-start(f32[2,1024]{1,0:T(2,128)S(1)} %broadcast_multiply_fusion.3) | copy-start | bytes 24580
  117.9 27.4 %copy-start.39 = (f32[2,1024]{1,0:T(2,128)}, f32[2,1024]{1,0:T(2,128)S(1)}, u32[]{:S(2)}) copy-start(f32[2,1024]{1,0:T(2,128)S(1)} %add_rsqrt_fusion.1) | copy-start | bytes 24580
  118.7 38.3 %copy-start.21 = (f32[2,1,1152]{2,1,0:T(1,128)}, f32[2,1,1152]{2,1,0:T(1,128)S(1)}, u32[]{:S(2)}) copy-start(f32[2,1,1152]{2,1,0:T(1,128)S(1)} %get-tuple-element.157) | copy-start | bytes 27652
  118.7 39.1 %copy-start.23 = (f32[2,1,1152]{2,1,0:T(1,128)}, f32[2,1,1152]{2,1,0:T(1,128)S(1)}, u32[]{:S(2)}) copy-start(f32[2,1,1152]{2,1,0:T(1,128)S(1)} %get-tuple-element.159) | copy-start | bytes 27652
  118.7 26.7 %copy-start.32 = (f32[2,1152]{1,0:T(2,128)}, f32[2,1152]{1,0:T(2,128)S(1)}, u32[]{:S(2)}) copy-start(f32[2,1152]{1,0:T(2,128)S(1)} %get-tuple-element.173) | copy-start | bytes 27652
  118.7 26.6 %copy-start.34 = (f32[2,1152]{1,0:T(2,128)}, f32[2,1152]{1,0:T(2,128)S(1)}, u32[]{:S(2)}) copy-start(f32[2,1152]{1,0:T(2,128)S(1)} %get-tuple-element.174) | copy-start | bytes 27652
  118.8 26.6 %copy-start.18 = (bf16[2304,72]{0,1:T(8,128)(2,1)S(1)}, bf16[2304,72]{0,1:T(8,128)(2,1)}, u32[]{:S(2)}) copy-start(bf16[2304,72]{0,1:T(8,128)(2,1)} %param.23) | copy-start | bytes 995332
  118.8 37.5 %copy-start.31 = (bf16[2,576]{1,0:T(2,128)(2,1)S(1)}, bf16[2,576]{1,0:T(2,128)(2,1)}, u32[]{:S(2)}) copy-start(bf16[2,576]{1,0:T(2,128)(2,1)} %param.20) | copy-start | bytes 6916
  118.8 37.6 %copy-start.9 = (f32[36,128]{1,0:T(8,128)S(1)}, f32[36,128]{1,0:T(8,128)}, u32[]{:S(2)}) copy-start(f32[36,128]{1,0:T(8,128)} %copy-done.8) | copy-start | bytes 55300
  118.8 37.6 %copy-start.20 = (f32[2304]{0:T(1024)S(1)}, f32[2304]{0:T(1024)}, u32[]{:S(2)}) copy-start(f32[2304]{0:T(1024)} %copy-done.19) | copy-start | bytes 27652
  145.4 9.4 %collective-permute-start.1 = (bf16[72,2304]{1,0:T(8,128)(2,1)S(1)}, bf16[72,2304]{1,0:T(8,128)(2,1)S(1)}, u32[]{:S(2)}, u32[]{:S(2)}) collective-permute-start(bf16[72,2304]{1,0:T(8,128)(2,1)S(1)} %bitcast.141), channel_id=1, source_target_pairs={{0,1},{1,0},{2,3},{3,2},{4,5},{5,4},{6,7},{7,6},{8,9},{9,8},{10,11... | collective-permute-start | bytes 995336 | tf_op jit(solution)/shard_map/ppermute | solution.py:1359
  155.6 307.2 %reduce-scatter.3.cloned.1.call-start = ((), (), s32[]{:S(2)}) async-start(), calls=%async_computation.4 | async-start | bytes 11280384 | tf_op jit(solution)/shard_map/reduce_scatter | solution.py:1442
  155.9 52.3 %collective-permute-start = (bf16[2,512,1152]{2,1,0:T(8,128)(2,1)}, bf16[2,512,1152]{2,1,0:T(8,128)(2,1)}, u32[]{:S(2)}, u32[]{:S(2)}) collective-permute-start(bf16[2,512,1152]{2,1,0:T(8,128)(2,1)} %get-tuple-element.55), channel_id=1, source_target_pairs={{0,1},{1,0},{2,3},{3,2},{4,5},{5,4},{6,7},{7,6},{8,9},{9,8},{10,11... | collective-permute-start | bytes 7077896 | tf_op jit(solution)/shard_map/ppermute | solution.py:1359
  157.0 51.2 %copy-start.25 = (f32[2,1,1152]{2,0,1:T(2,128)}, f32[2,1,1152]{2,0,1:T(2,128)S(1)}, u32[]{:S(2)}) copy-start(f32[2,1,1152]{2,0,1:T(2,128)S(1)} %copy.128) | copy-start | bytes 27652
  157.8 55.2 %copy-start.36 = (f32[2,1152]{1,0:T(2,128)}, f32[2,1152]{1,0:T(2,128)S(1)}, u32[]{:S(2)}) copy-start(f32[2,1152]{1,0:T(2,128)S(1)} %get-tuple-element.172) | copy-start | bytes 27652
  157.8 50.5 %copy-start.12 = (bf16[2,512,1152]{2,1,0:T(8,128)(2,1)S(1)}, bf16[2,512,1152]{2,1,0:T(8,128)(2,1)}, u32[]{:S(2)}) copy-start(bf16[2,512,1152]{2,1,0:T(8,128)(2,1)} %get-tuple-element.145) | copy-start | bytes 7077892
  225.6 5.1 copy-start.10
  226.7 47.9 %slice-start.3 = ((s8[4718592]{0:T(1024)(128)(4,1)}), s8[524288]{0:T(1024)(128)(4,1)S(1)}, s32[]{:S(2)}) async-start(s8[4718592]{0:T(1024)(128)(4,1)} %bitcast.134), calls=%async_computation.9 | async-start | bytes 1048576
  230.7 43.9 %slice-start.4 = ((s8[4718592]{0:T(1024)(128)(4,1)}), s8[4194304]{0:T(1024)(128)(4,1)S(1)}, s32[]{:S(2)}) async-start(s8[4718592]{0:T(1024)(128)(4,1)} %bitcast.134), calls=%async_computation.10 | async-start | bytes 8388608
  301.9 36.6 %slice-start.5 = ((s8[4718592]{0:T(1024)(128)(4,1)}), s8[524288]{0:T(1024)(128)(4,1)S(1)}, s32[]{:S(2)}) async-start(s8[4718592]{0:T(1024)(128)(4,1)} %bitcast.137), calls=%async_computation.11 | async-start | bytes 1048576
  301.9 321.8 %reduce-scatter.5.cloned.1.call-start = ((), (), s32[]{:S(2)}) async-start(), calls=%async_computation.5 | async-start | bytes 14413824 | tf_op jit(solution)/shard_map/reduce_scatter | solution.py:1464
  302.0 36.5 %slice-start.6 = ((s8[4718592]{0:T(1024)(128)(4,1)}), s8[4194304]{0:T(1024)(128)(4,1)S(1)}, s32[]{:S(2)}) async-start(s8[4718592]{0:T(1024)(128)(4,1)} %bitcast.137), calls=%async_computation.12 | async-start | bytes 8388608
  366.1 34.5 %copy-start.13 = (bf16[2,512,1152]{2,1,0:T(8,128)(2,1)S(1)}, bf16[2,512,1152]{2,1,0:T(8,128)(2,1)}, u32[]{:S(2)}) copy-start(bf16[2,512,1152]{2,1,0:T(8,128)(2,1)} %get-tuple-element.145) | copy-start | bytes 7077892
  366.1 34.5 %copy-start.26 = (f32[2,1,1152]{2,0,1:T(2,128)S(1)}, f32[2,1,1152]{2,0,1:T(2,128)}, u32[]{:S(2)}) copy-start(f32[2,1,1152]{2,0,1:T(2,128)} %copy-done.25) | copy-start | bytes 27652
  366.1 34.5 %copy-start.38 = (f32[1152]{0:T(1024)S(1)}, f32[1152]{0:T(1024)}, u32[]{:S(2)}) copy-start(f32[1152]{0:T(1024)} %get-tuple-element.130) | copy-start | bytes 13828
  400.6 39.4 %copy-start.37 = (f32[2,1152]{1,0:T(2,128)S(1)}, f32[2,1152]{1,0:T(2,128)}, u32[]{:S(2)}) copy-start(f32[2,1152]{1,0:T(2,128)} %copy-done.36) | copy-start | bytes 27652
  440.1 12.1 %copy-start.14 = (f32[2,1024,1152]{2,1,0:T(8,128)S(1)}, f32[2,1024,1152]{2,1,0:T(8,128)}, u32[]{:S(2)}) copy-start(f32[2,1024,1152]{2,1,0:T(8,128)} %get-tuple-element.142) | copy-start | bytes 28311556
  475.1 1.7 copy-start.1
  476.8 11.4 %copy-start.24 = (f32[2,1,1152]{2,1,0:T(1,128)S(1)}, f32[2,1,1152]{2,1,0:T(1,128)}, u32[]{:S(2)}) copy-start(f32[2,1,1152]{2,1,0:T(1,128)} %copy-done.23) | copy-start | bytes 27652
  476.8 11.4 %copy-start.22 = (f32[2,1,1152]{2,1,0:T(1,128)S(1)}, f32[2,1,1152]{2,1,0:T(1,128)}, u32[]{:S(2)}) copy-start(f32[2,1,1152]{2,1,0:T(1,128)} %copy-done.21) | copy-start | bytes 27652
  476.8 11.8 %copy-start.30 = (f32[1,4608]{1,0:T(1,128)S(1)}, f32[1,4608]{1,0:T(1,128)}, u32[]{:S(2)}) copy-start(f32[1,4608]{1,0:T(1,128)} %get-tuple-element.75) | copy-start | bytes 55300
  486.7 137.0 %collective-permute-start.2 = (bf16[2,512,1152]{2,1,0:T(8,128)(2,1)}, bf16[2,512,1152]{2,1,0:T(8,128)(2,1)}, u32[]{:S(2)}, u32[]{:S(2)}) collective-permute-start(bf16[2,512,1152]{2,1,0:T(8,128)(2,1)} %get-tuple-element.144), channel_id=1, source_target_pairs={{0,1},{1,0},{2,3},{3,2},{4,5},{5,4},{6,7},{7,6},{8,9},{9,8},{10,11... | collective-permute-start | bytes 7077896 | tf_op jit(solution)/shard_map/ppermute | solution.py:1359
  490.5 131.3 %collective-permute-start.6 = (bf16[72,2304]{1,0:T(8,128)(2,1)}, bf16[72,2304]{1,0:T(8,128)(2,1)}, u32[]{:S(2)}, u32[]{:S(2)}) collective-permute-start(bf16[72,2304]{1,0:T(8,128)(2,1)} %split.32), channel_id=1, source_target_pairs={{0,1},{1,0},{2,3},{3,2},{4,5},{5,4},{6,7},{7,6},{8,9},{9,8},{10,11... | collective-permute-start | bytes 995336 | tf_op jit(solution)/shard_map/ppermute | solution.py:1359
  491.0 104.9 %copy-start.29 = (f32[2,1024]{1,0:T(2,128)S(1)}, f32[2,1024]{1,0:T(2,128)}, u32[]{:S(2)}) copy-start(f32[2,1024]{1,0:T(2,128)} %copy-done.28) | copy-start | bytes 24580
  491.0 104.9 %copy-start.33 = (f32[2,1152]{1,0:T(2,128)S(1)}, f32[2,1152]{1,0:T(2,128)}, u32[]{:S(2)}) copy-start(f32[2,1152]{1,0:T(2,128)} %copy-done.32) | copy-start | bytes 27652
  491.0 104.9 %copy-start.35 = (f32[2,1152]{1,0:T(2,128)S(1)}, f32[2,1152]{1,0:T(2,128)}, u32[]{:S(2)}) copy-start(f32[2,1152]{1,0:T(2,128)} %copy-done.34) | copy-start | bytes 27652
  491.0 104.9 %copy-start.40 = (f32[2,1024]{1,0:T(2,128)S(1)}, f32[2,1024]{1,0:T(2,128)}, u32[]{:S(2)}) copy-start(f32[2,1024]{1,0:T(2,128)} %copy-done.39) | copy-start | bytes 24580
  595.9 25.9 %copy-start.16 = (bf16[72,4608]{1,0:T(8,128)(2,1)S(1)}, bf16[72,4608]{1,0:T(8,128)(2,1)}, u32[]{:S(2)}) copy-start(bf16[72,4608]{1,0:T(8,128)(2,1)} %reduce-scatter.3.cloned.1.call-done) | copy-start | bytes 1990660
  625.7 139.4 %collective-permute-start.5 = (bf16[72,2304]{1,0:T(8,128)(2,1)S(1)}, bf16[72,2304]{1,0:T(8,128)(2,1)S(1)}, u32[]{:S(2)}, u32[]{:S(2)}) collective-permute-start(bf16[72,2304]{1,0:T(8,128)(2,1)S(1)} %split.30), channel_id=1, source_target_pairs={{0,1},{1,0},{2,3},{3,2},{4,5},{5,4},{6,7},{7,6},{8,9},{9,8},{10,11... | collective-permute-start | bytes 995336 | tf_op jit(solution)/shard_map/ppermute | solution.py:1359
  627.2 135.1 %collective-permute-start.4 = (bf16[72,640]{1,0:T(8,128)(2,1)S(1)}, bf16[72,640]{1,0:T(8,128)(2,1)S(1)}, u32[]{:S(2)}, u32[]{:S(2)}) collective-permute-start(bf16[72,640]{1,0:T(8,128)(2,1)S(1)} %get-tuple-element.148), channel_id=1, source_target_pairs={{0,1},{1,0},{2,3},{3,2},{4,5},{5,4},{6,7},{7,6},{8,9},{9,8},{10,11... | collective-permute-start | bytes 276488 | tf_op jit(solution)/shard_map/ppermute | solution.py:1359
  627.7 96.1 %copy-start.7 = (f32[16,8,128]{2,1,0:T(8,128)S(1)}, f32[16,8,128]{2,1,0:T(8,128)}, u32[]{:S(2)}) copy-start(f32[16,8,128]{2,1,0:T(8,128)} %copy-done.6) | copy-start | bytes 196612
  627.7 126.2 %copy-start.27 = (bf16[4,1152]{1,0:T(4,128)(2,1)S(1)}, bf16[4,1152]{1,0:T(4,128)(2,1)}, u32[]{:S(2)}) copy-start(bf16[4,1152]{1,0:T(4,128)(2,1)} %param.13) | copy-start | bytes 27652
  721.6 41.4 %collective-permute-start.3 = (bf16[72,1920]{1,0:T(8,128)(2,1)S(1)}, bf16[72,1920]{1,0:T(8,128)(2,1)}, u32[]{:S(2)}, u32[]{:S(2)}) collective-permute-start(bf16[72,1920]{1,0:T(8,128)(2,1)S(1)} %split.38), channel_id=1, source_target_pairs={{0,1},{1,0},{2,3},{3,2},{4,5},{5,4},{6,7},{7,6},{8,9},{9,8},{10,11... | collective-permute-start | bytes 829448 | tf_op jit(solution)/shard_map/ppermute | solution.py:1359
  756.5 6.5 copy-start.17
Sparse Core Ops, SparseCore 0:
  106.1 103.6 all-gather.2
  212.6 86.8 all-gather.4
  303.5 121.9 reduce-scatter.2
  475.3 145.0 reduce-scatter.4
